TPU v7x, 256 devices: a whole 4x4x8 slice. The times are simulated.
256 devices in a mesh: row: 8 (over z), col: 16 (over y, x), layer: 2 (over core).
Axes of the slice: x: 4, y: 4, z: 8, core: 2. Of those that a mesh axis runs over, the one named last changes fastest.
Arguments:
- amplitudes: bfloat16 [4096, 12288], P('row', ('col', 'layer')), may hold values from -6 to 6
- integrals: bfloat16 [12288, 12288], P(('col', 'layer')), may hold values from -0.109375 to 0.109375
- hole_integrals: bfloat16 [4096, 4096], P('row'), may hold values from -0.09375 to 0.09375
- tile_mask: int32 [96, 96], replicated, may hold values 0 or 1
- occupied_energy: float32 [4096], P('row'), may hold values from -3 to -0.5
- virtual_energy: float32 [12288], P(('col', 'layer')), may hold values from 0.5 to 4
Outputs:
- update: float32 [4096, 12288], P('row', ('col', 'layer'))
All inputs are finite; a program needn't handle non-finite values.
Results may differ from a plain program's by a relative error of at most 0.0003.
Values may be sent and summed in bfloat16 or wider, within the bound.
No kernel may reach another device: no remote copies, remote signals or barrier semaphores. Data moves between devices by JAX's collectives and lax.ppermute only.
A program may use at most 128 MiB of HBM per device.

v0:
```python
import jax
import jax.numpy as jnp
from jax import lax
from jax.sharding import PartitionSpec as P

TB = 128


def shards(amplitudes, integrals, hole_integrals, tile_mask, occupied_energy, virtual_energy):
    local_width = amplitudes.shape[1]
    position = lax.axis_index(("col", "layer"))
    my_tiles = local_width // TB
    mask_rows = lax.dynamic_slice_in_dim(tile_mask, position * my_tiles, my_tiles, 0)
    expanded = jnp.repeat(jnp.repeat(mask_rows, TB, axis=0), TB, axis=1).astype(jnp.bfloat16)
    masked = integrals * expanded
    ladder = lax.psum_scatter(
        lax.dot_general(
            masked, amplitudes, (((0,), (1,)), ((), ())), preferred_element_type=jnp.float32
        ),
        ("col", "layer"),
        scatter_dimension=0,
        tiled=True,
    ).T
    holes = jnp.dot(
        hole_integrals,
        lax.all_gather(amplitudes, "row", axis=0, tiled=True),
        preferred_element_type=jnp.float32,
    )
    denominator = virtual_energy[None, :] - occupied_energy[:, None]
    return (ladder + holes) / denominator


def solution(mesh):
    return jax.shard_map(
        shards,
        mesh=mesh,
        in_specs=(
            P("row", ("col", "layer")),
            P(("col", "layer"), None),
            P("row", None),
            P(),
            P("row"),
            P(("col", "layer")),
        ),
        out_specs=P("row", ("col", "layer")),
        check_vma=False,
    )
```

profile of v0, /device:TPU:8, one launch (start us, length us, event | category | flops | bytes accessed | tf_op | source)
XLA Modules:
  0.0 208.4 jit_solution(14107899326573754954)
XLA Ops:
  7.4 0.0 copy-start
  7.4 0.0 all-gather.2.cloned.1.call-start
  7.4 0.7 all-gather.2.cloned.1.call-update
  8.1 0.0 reduce-scatter.2.cloned.1.call-start
  8.1 0.7 dynamic-slice_convert_fusion
  8.9 12.0 %broadcast_in_dim.9 = bf16[384,96,128]{2,1,0:T(8,128)(2,1)} broadcast(bf16[384,96]{1,0:T(8,128)(2,1)S(1)} %bitcast.11), dimensions={0,1} | broadcast | bytes 9510912 | tf_op jit(solution)/shard_map/broadcast_in_dim | solution.py:14
  20.9 0.0 copy-done
  20.9 23.2 %fusion = f32[12288,512]{1,0:T(8,128)} fusion(bf16[512,384]{1,0:T(8,128)(2,1)S(1)} %copy-done, bf16[384,12288]{1,0:T(8,128)(2,1)} %param.7, bf16[48,8,96,128]{3,2,1,0:T(8,128)(2,1)} %bitcast.10), kind=kOutput, calls=%fused_computation.1 | convolution fusion | flops 4836556800 | bytes 44433408 | tf_op jit(solution)/shard_map/dot_general | solution.py:17
  44.0 0.0 copy-start.1
  44.1 0.0 copy-start.2
  44.1 0.0 reduce-scatter.2.cloned.1.call-update
  44.1 13.8 %all-gather.2.cloned.1.call-done = bf16[4096,384]{1,0:T(8,128)(2,1)} async-done(((bf16[512,384]{1,0:T(8,128)(2,1)}), bf16[4096,384]{1,0:T(8,128)(2,1)}) %all-gather.2.cloned.1.call-update) | async-done | bytes 3145744 | tf_op jit(solution)/shard_map/all_gather | solution.py:26
  57.9 136.8 %reduce-scatter.2.cloned.1.call-done = f32[384,512]{1,0:T(8,128)} async-done(((f32[12288,512]{1,0:T(8,128)}), f32[384,512]{1,0:T(8,128)}) %reduce-scatter.2.cloned.1.call-update) | async-done | bytes 786448 | tf_op jit(solution)/shard_map/reduce_scatter | solution.py:16
  194.7 0.0 copy-done.1
  194.7 0.0 copy-done.2
  194.7 5.1 %fusion.2 = f32[512,384]{0,1:T(8,128)S(1)} fusion(bf16[512,4096]{1,0:T(8,128)(2,1)} %param.8, bf16[4096,384]{1,0:T(8,128)(2,1)} %all-gather.2.cloned.1.call-done, f32[384,512]{1,0:T(8,128)} %reduce-scatter.2.cloned.1.call-done, f32[512]{0:T(512)S(1)} %copy-done.1, f32[384]{0:T(512)S(1)} %copy-done.2), kind=kOutput, calls=%fused_computation.4 | convolution fusion | flops 1611202560 | bytes 8916480 | tf_op jit(solution)/shard_map/dot_general | solution.py:24
  199.8 1.1 copy.8
  (1 shorter events, 0.0 us)
Async XLA Ops:
  7.4 13.5 %copy-start = (bf16[512,384]{1,0:T(8,128)(2,1)S(1)}, bf16[512,384]{1,0:T(8,128)(2,1)}, u32[]{:S(2)}) copy-start(bf16[512,384]{1,0:T(8,128)(2,1)} %param.6) | copy-start | bytes 1179652
  7.4 50.5 %all-gather.2.cloned.1.call-start = ((), (), s32[]{:S(2)}) async-start(), calls=%async_computation.2 | async-start | bytes 3538944 | tf_op jit(solution)/shard_map/all_gather | solution.py:26
  8.1 186.6 %reduce-scatter.2.cloned.1.call-start = ((), (), s32[]{:S(2)}) async-start(), calls=%async_computation.1 | async-start | bytes 25952256 | tf_op jit(solution)/shard_map/reduce_scatter | solution.py:16
  44.0 150.7 %copy-start.1 = (f32[512]{0:T(512)S(1)}, f32[512]{0:T(512)}, u32[]{:S(2)}) copy-start(f32[512]{0:T(512)} %param.10) | copy-start | bytes 6148
  44.1 150.7 %copy-start.2 = (f32[384]{0:T(512)S(1)}, f32[384]{0:T(512)}, u32[]{:S(2)}) copy-start(f32[384]{0:T(512)} %param.11) | copy-start | bytes 4612
Sparse Core Ops, SparseCore 0:
  10.0 47.8 all-gather.1
Sparse Core Ops, SparseCore 1:
  44.2 150.5 reduce-scatter.1
where the time goes:
time: 210 us; the launch traced here: 208 us
  waiting for transfers between devices  151 us (72%)
  matrix products  28.3 us (13%)
  between operations  14.9 us (7%)
  local copies, waits for them, and re-layouts  13.2 us (6%)
    reduce_scatter x1, waiting for transfers between devices, shards(): lax.psum_scatter(lax.dot_general(masked, amplitudes, (((0,), (1,)), ((),...  137 us
    dot_general x1, matrix products, shards(): lax.dot_general(masked, amplitudes, (((0,), (1,)), ((), ())), preferred_e...  23.2 us
    all_gather x1, waiting for transfers between devices, shards(): lax.all_gather(amplitudes, 'row', axis=0, tiled=True)  13.8 us
    broadcast_in_dim x1, local copies, waits for them, and re-layouts, shards(): jnp.repeat(jnp.repeat(mask_rows, TB, axis=0), TB, axis=1)  12 us
    dot_general x1, matrix products, shards(): jnp.dot(hole_integrals, lax.all_gather(amplitudes, 'row', axis=0, tiled=T...  5.12 us
  transfers between devices with their start and end apart: 2, of which 2 were waited for; matrix products, arithmetic and copies ran while one was open for 17% of the time, Pallas kernels for 0%

commit v1 on v0

v1 whole, which is shorter than its diff:
```python
import functools

import jax
import jax.numpy as jnp
from jax import lax
from jax.experimental import pallas as pl
from jax.experimental.pallas import tpu as pltpu
from jax.sharding import PartitionSpec as P

TB = 128
X = 4
Y = 4
F32 = jnp.float32
I16 = jnp.int16
I32 = jnp.int32
BF16 = jnp.bfloat16
TOP = 32700.0
STEPS = 64.0
VMEM = 48 * 1024 * 1024


def shift_x(d):
    return [(y * X + x, y * X + (x + d) % X) for y in range(Y) for x in range(X)]


def shift_y(d):
    return [(y * X + x, ((y + d) % Y) * X + x) for y in range(Y) for x in range(X)]


def encode(block):
    peak = jnp.maximum(jnp.max(jnp.abs(block), axis=0, keepdims=True), 1e-30)
    code = jnp.floor(jnp.log2(TOP / peak) * STEPS)
    scale = jnp.exp2(code * (1.0 / STEPS))
    return jnp.round(block * scale).astype(I32).astype(I16), code


def decode(block, code):
    scale = jnp.exp2(code.astype(F32) * (1.0 / STEPS))
    return block.astype(I32).astype(F32) * (1.0 / scale)


def put_code(ref, start, row, code):
    rows = ref[pl.ds(start, 16), :].astype(I32)
    at = lax.broadcasted_iota(I32, rows.shape, 0) == row
    ref[pl.ds(start, 16), :] = jnp.where(at, code.astype(I32), rows).astype(I16)


def get_code(ref, start, row):
    rows = ref[pl.ds(start, 16), :].astype(I32)
    at = lax.broadcasted_iota(I32, rows.shape, 0) == row
    return jnp.sum(jnp.where(at, rows, 0).astype(F32), axis=0, keepdims=True)


def pick(i, table):
    out = jnp.int32(table[-1])
    for k in range(len(table) - 2, -1, -1):
        out = jnp.where(i == k, jnp.int32(table[k]), out)
    return out


def column_block(meta, dx, dy, other_layer):
    x = lax.rem(meta[0] + dx, X)
    y = lax.rem(meta[1] + dy, Y)
    layer = 1 - meta[2] if other_layer else meta[2]
    return (y * X + x) * 2 + layer


def masked(meta, tiles, block_at, v_ref):
    rows = []
    for kt in range(tiles):
        row = []
        for qt in range(tiles):
            m = meta[3 + kt * 96 + block_at * tiles + qt].astype(F32)
            keep = jnp.broadcast_to(m, (TB, TB)).astype(BF16)
            row.append(v_ref[kt * TB:(kt + 1) * TB, qt * TB:(qt + 1) * TB] * keep)
        rows.append(jnp.concatenate(row, axis=1))
    return jnp.concatenate(rows, axis=0)


def params():
    return pltpu.CompilerParams(vmem_limit_bytes=VMEM)


def cost(flops, moved):
    return pl.CostEstimate(flops=flops, bytes_accessed=moved, transcendentals=0)


FIRST = [(2, 0), (2, 1), (2, 2), (2, 3), (0, 2), (1, 2), (3, 2)]
SECOND = [(dx, dy) for dx in (0, 1, 3) for dy in (0, 1, 3)]


def pack(meta, integrals, width, dests):
    n = len(dests)

    def body(meta_ref, v_ref, out_ref):
        i = pl.program_id(0)
        at = column_block(meta_ref, pick(i, [d[0] for d in dests]), pick(i, [d[1] for d in dests]), True)
        out_ref[0] = masked(meta_ref, width // TB, at, v_ref)

    def v_map(i, meta_ref):
        return 0, column_block(meta_ref, pick(i, [d[0] for d in dests]), pick(i, [d[1] for d in dests]), True)

    return pl.pallas_call(
        body,
        out_shape=jax.ShapeDtypeStruct((n, width, width), BF16),
        grid_spec=pltpu.PrefetchScalarGridSpec(
            num_scalar_prefetch=1,
            grid=(n,),
            in_specs=[pl.BlockSpec((width, width), v_map)],
            out_specs=pl.BlockSpec((1, width, width), lambda i, m: (i, 0, 0)),
        ),
        compiler_params=params(),
        cost_estimate=cost(0, 4 * n * width * width),
        name="pack",
    )(meta, integrals)


def dest(axis, d, o):
    return (d, o) if axis == 0 else (o, d)


def product(meta_ref, at, width, v_ref, vp, a_s, v_s):
    v_s[:width, :] = masked(meta_ref, width // TB, at, v_ref)
    v_s[width:, :] = vp
    return jnp.dot(a_s[...], v_s[...], preferred_element_type=F32)


def load_a(a_ref, ap_ref, a_s, width):
    @pl.when(pl.program_id(0) == 0)
    def _():
        a_s[:, :width] = a_ref[...]
        a_s[:, width:] = ap_ref[...]


def far(axis, meta, a, ap, integrals, v1):
    rows, width = a.shape
    half, q = rows // 2, rows // 4
    table = [FIRST.index(dest(axis, 2, o)) for o in range(4)]
    msg = 4 * q + 16

    def place(i):
        return (2, i) if axis == 0 else (i, 2)

    def body(meta_ref, a_ref, ap_ref, v_ref, vp_ref, up_ref, down_ref, a_s, v_s):
        i = pl.program_id(0)
        load_a(a_ref, ap_ref, a_s, width)
        at = column_block(meta_ref, *place(i), False)
        part = product(meta_ref, at, width, v_ref, vp_ref[0], a_s, v_s)
        for ref, lo in ((up_ref, 0), (down_ref, q)):
            coded, code = encode(part[lo:lo + q])
            ref[pl.ds(pl.multiple_of(i * q, q), q), :] = coded
            put_code(ref, 4 * q, i, code)

    return pl.pallas_call(
        body,
        out_shape=[jax.ShapeDtypeStruct((msg, width), I16)] * 2,
        grid_spec=pltpu.PrefetchScalarGridSpec(
            num_scalar_prefetch=1,
            grid=(4,),
            in_specs=[
                pl.BlockSpec((half, width), lambda i, m: (axis, 0)),
                pl.BlockSpec((half, width), lambda i, m: (axis, 0)),
                pl.BlockSpec((width, width), lambda i, m: (0, column_block(m, *place(i), False))),
                pl.BlockSpec((1, width, width), lambda i, m: (pick(i, table), 0, 0)),
            ],
            out_specs=[pl.BlockSpec((msg, width), lambda i, m: (0, 0))] * 2,
            scratch_shapes=[pltpu.VMEM((half, 2 * width), BF16), pltpu.VMEM((2 * width, width), BF16)],
        ),
        compiler_params=params(),
        cost_estimate=cost(2 * 4 * half * 2 * width * width, 4 * 4 * width * width),
        name="far_y" if axis else "far_x",
    )(meta, a, ap, integrals, v1)


NEAR = [(1, 2), (3, 2), (1, 0), (1, 1), (1, 3), (3, 0), (3, 1), (3, 3)]
HOME = [(0, 2), (0, 0), (0, 1), (0, 3)]


def v_tables(axis, steps):
    one, two = [], []
    for d, o in steps:
        at = dest(axis, d, o)
        one.append(FIRST.index(at) if at in FIRST else None)
        two.append(SECOND.index(at) if at in SECOND else None)
    for t in (one, two):
        known = [v for v in t if v is not None]
        last = known[0]
        for k, v in enumerate(t):
            last = v if v is not None else last
            t[k] = last
    return one, two


def near(axis, meta, a, ap, integrals, v1, v2):
    rows, width = a.shape
    half, q = rows // 2, rows // 4
    msg = 4 * q + 16
    one, two = v_tables(axis, NEAR)

    def spot(i):
        return pick(i, [s[0] for s in NEAR]), pick(i, [s[1] for s in NEAR])

    def body(meta_ref, a_ref, ap_ref, v_ref, v1_ref, v2_ref, up_ref, down_ref, up_st, down_st, a_s, v_s):
        i = pl.program_id(0)
        load_a(a_ref, ap_ref, a_s, width)
        d, o = spot(i)
        at = column_block(meta_ref, *dest(axis, d, o), False)
        vp = jnp.where(i < 2, v1_ref[0], v2_ref[0])
        part = product(meta_ref, at, width, v_ref, vp, a_s, v_s)
        here = pl.ds(pl.multiple_of(o * q, q), q)

        @pl.when(d == 1)
        def _():
            up_st[here, :] = part[:q]
            coded, code = encode(part[q:])
            up_ref[here, :] = coded
            put_code(up_ref, 4 * q, o, code)

        @pl.when(d == 3)
        def _():
            down_st[here, :] = part[q:]
            coded, code = encode(part[:q])
            down_ref[here, :] = coded
            put_code(down_ref, 4 * q, o, code)

    whole = lambda n: pl.BlockSpec((n, width), lambda i, m: (0, 0))
    return pl.pallas_call(
        body,
        out_shape=[jax.ShapeDtypeStruct((msg, width), I16)] * 2 + [jax.ShapeDtypeStruct((4 * q, width), F32)] * 2,
        grid_spec=pltpu.PrefetchScalarGridSpec(
            num_scalar_prefetch=1,
            grid=(len(NEAR),),
            in_specs=[
                pl.BlockSpec((half, width), lambda i, m: (axis, 0)),
                pl.BlockSpec((half, width), lambda i, m: (axis, 0)),
                pl.BlockSpec((width, width), lambda i, m: (0, column_block(m, *dest(axis, *spot(i)), False))),
                pl.BlockSpec((1, width, width), lambda i, m: (pick(i, one), 0, 0)),
                pl.BlockSpec((1, width, width), lambda i, m: (pick(i, two), 0, 0)),
            ],
            out_specs=[whole(msg), whole(msg), whole(4 * q), whole(4 * q)],
            scratch_shapes=[pltpu.VMEM((half, 2 * width), BF16), pltpu.VMEM((2 * width, width), BF16)],
        ),
        compiler_params=params(),
        cost_estimate=cost(2 * 8 * half * 2 * width * width, 8 * 4 * width * width),
        name="near_y" if axis else "near_x",
    )(meta, a, ap, integrals, v1, v2)


def home(axis, meta, a, ap, integrals, v1, v2):
    rows, width = a.shape
    half = rows // 2
    one, two = v_tables(axis, HOME)

    def spot(i):
        return 0, pick(i, [s[1] for s in HOME])

    def body(meta_ref, a_ref, ap_ref, v_ref, v1_ref, v2_ref, out_ref, a_s, v_s):
        i = pl.program_id(0)
        load_a(a_ref, ap_ref, a_s, width)
        at = column_block(meta_ref, *dest(axis, *spot(i)), False)
        vp = jnp.where(i < 1, v1_ref[0], v2_ref[0])
        out_ref[0] = product(meta_ref, at, width, v_ref, vp, a_s, v_s)

    return pl.pallas_call(
        body,
        out_shape=jax.ShapeDtypeStruct((4, half, width), F32),
        grid_spec=pltpu.PrefetchScalarGridSpec(
            num_scalar_prefetch=1,
            grid=(len(HOME),),
            in_specs=[
                pl.BlockSpec((half, width), lambda i, m: (axis, 0)),
                pl.BlockSpec((half, width), lambda i, m: (axis, 0)),
                pl.BlockSpec((width, width), lambda i, m: (0, column_block(m, *dest(axis, *spot(i)), False))),
                pl.BlockSpec((1, width, width), lambda i, m: (pick(i, one), 0, 0)),
                pl.BlockSpec((1, width, width), lambda i, m: (pick(i, two), 0, 0)),
            ],
            out_specs=pl.BlockSpec((1, half, width), lambda i, m: (spot(i)[1], 0, 0)),
            scratch_shapes=[pltpu.VMEM((half, 2 * width), BF16), pltpu.VMEM((2 * width, width), BF16)],
        ),
        compiler_params=params(),
        cost_estimate=cost(2 * 4 * half * 2 * width * width, 4 * 4 * width * width),
        name="home_y" if axis else "home_x",
    )(meta, a, ap, integrals, v1, v2)


def relay(name, up_in, down_in, up_st, down_st):
    msg, width = up_in.shape
    q = (msg - 16) // 4

    def body(ui_ref, uc_ref, di_ref, dc_ref, us_ref, ds_ref, up_ref, down_ref):
        i = pl.program_id(0)
        here = pl.ds(pl.multiple_of(i * q, q), q)
        for got, codes, own, out in ((ui_ref, uc_ref, us_ref, up_ref), (di_ref, dc_ref, ds_ref, down_ref)):
            total = own[...] + decode(got[...], get_code(codes, 0, i))
            coded, code = encode(total)
            out[here, :] = coded
            put_code(out, 4 * q, i, code)

    data = pl.BlockSpec((q, width), lambda i: (i, 0))
    codes = pl.BlockSpec((16, width), lambda i: (4 * q // 16, 0))
    return pl.pallas_call(
        body,
        out_shape=[jax.ShapeDtypeStruct((msg, width), I16)] * 2,
        grid=(4,),
        in_specs=[data, codes, data, codes, data, data],
        out_specs=[pl.BlockSpec((msg, width), lambda i: (0, 0))] * 2,
        compiler_params=params(),
        cost_estimate=cost(0, 16 * q * width * 4),
        name=name,
    )(up_in, up_in, down_in, down_in, up_st, down_st)


def turn(name, st, first_near, first_far, second_near, second_far):
    _, half, width = st.shape
    q = half // 2

    def body(st_ref, fn, fnc, ff, ffc, sn, snc, sf, sfc, own_ref, m1_ref, m2_ref, m3_ref):
        i = pl.program_id(0)
        top = st_ref[0, :q] + decode(fn[...], get_code(fnc, 0, i)) + decode(ff[...], get_code(ffc, 0, i))
        low = st_ref[0, q:] + decode(sn[...], get_code(snc, 0, i)) + decode(sf[...], get_code(sfc, 0, i))

        @pl.when(i == 0)
        def _():
            own_ref[:q] = top
            own_ref[q:] = low

        for k, ref in ((1, m1_ref), (2, m2_ref), (3, m3_ref)):
            @pl.when(i == k)
            def _():
                for n, part in ((0, top), (1, low)):
                    coded, code = encode(part)
                    ref[n * q:(n + 1) * q, :] = coded
                    put_code(ref, 2 * q, n, code)

    data = pl.BlockSpec((q, width), lambda i: (i, 0))
    codes = pl.BlockSpec((16, width), lambda i: (4 * q // 16, 0))
    whole = lambda n: pl.BlockSpec((n, width), lambda i: (0, 0))
    return pl.pallas_call(
        body,
        out_shape=[jax.ShapeDtypeStruct((half, width), F32)] + [jax.ShapeDtypeStruct((half + 16, width), I16)] * 3,
        grid=(4,),
        in_specs=[pl.BlockSpec((1, half, width), lambda i: (i, 0, 0))] + [data, codes] * 4,
        out_specs=[whole(half)] + [whole(half + 16)] * 3,
        compiler_params=params(),
        cost_estimate=cost(0, 4 * half * width * 10),
        name=name,
    )(st, *[r for m in (first_near, first_far, second_near, second_far) for r in (m, m)])


def finish(own_x, own_y, got_x, got_y, holes, occupied, virtual):
    half, width = own_x.shape
    q = half // 2

    def body(ox, oy, x1, x2, x3, y1, y2, y3, holes_ref, occ_ref, virt_ref, out_ref):
        for own, got, lo in ((ox, (x1, x2, x3), 0), (oy, (y1, y2, y3), half)):
            for n in range(2):
                total = own[n * q:(n + 1) * q]
                for ref in got:
                    total = total + decode(ref[n * q:(n + 1) * q, :], get_code(ref, 2 * q, n))
                here = slice(lo + n * q, lo + (n + 1) * q)
                total = total + holes_ref[here, :]
                out_ref[here, :] = total / (virt_ref[...] - occ_ref[here, :])

    return pl.pallas_call(
        body,
        out_shape=jax.ShapeDtypeStruct((2 * half, width), F32),
        compiler_params=params(),
        cost_estimate=cost(0, 2 * half * width * 12),
        name="finish",
    )(own_x, own_y, *got_x, *got_y, holes, occupied[:, None], virtual[None, :])


def shards(amplitudes, integrals, hole_integrals, tile_mask, occupied_energy, virtual_energy):
    width = amplitudes.shape[1]
    tiles = width // TB
    col, layer = lax.axis_index("col"), lax.axis_index("layer")
    mask_rows = lax.dynamic_slice_in_dim(tile_mask, (col * 2 + layer) * tiles, tiles, 0)
    meta = jnp.concatenate([jnp.stack([lax.rem(col, X), lax.div(col, X), layer]).astype(I32), mask_rows.reshape(-1)])
    swap = [(0, 1), (1, 0)]

    gathered = lax.all_gather(amplitudes, "row", axis=0, tiled=True)
    a, ap = amplitudes, lax.ppermute(amplitudes, "layer", swap)
    v1 = lax.ppermute(pack(meta, integrals, width, FIRST), "layer", swap)
    v2 = lax.ppermute(pack(meta, integrals, width, SECOND), "layer", swap)

    shift = (shift_x, shift_y)
    send = lambda value, axis, d: lax.ppermute(value, "col", shift[axis](d))
    got, own = [None, None], [None, None]
    far_in, near_in, stash = [None, None], [None, None], [None, None]
    for axis in (0, 1):
        up, down = far(axis, meta, a, ap, integrals, v1)
        far_in[axis] = send(up, axis, 1), send(down, axis, -1)
    for axis in (0, 1):
        up, down, up_st, down_st = near(axis, meta, a, ap, integrals, v1, v2)
        near_in[axis] = send(down, axis, -1), send(up, axis, 1)
        stash[axis] = up_st, down_st
    homes = [home(axis, meta, a, ap, integrals, v1, v2) for axis in (0, 1)]
    last = [None, None]
    for axis in (0, 1):
        up, down = relay("relay_y" if axis else "relay_x", *far_in[axis], *stash[axis])
        last[axis] = send(up, axis, 1), send(down, axis, -1)
    for axis in (0, 1):
        own[axis], m1, m2, m3 = turn(
            "turn_y" if axis else "turn_x", homes[axis], near_in[axis][0], last[axis][0], near_in[axis][1], last[axis][1]
        )
        got[axis] = send(m2, 1 - axis, 2), send(m1, 1 - axis, 1), send(m3, 1 - axis, -1)
    holes = jnp.dot(hole_integrals, gathered, preferred_element_type=F32)
    return finish(own[0], own[1], got[0], got[1], holes, occupied_energy, virtual_energy)


def solution(mesh):
    return jax.shard_map(
        shards,
        mesh=mesh,
        in_specs=(
            P("row", ("col", "layer")),
            P(("col", "layer"), None),
            P("row", None),
            P(),
            P("row"),
            P(("col", "layer")),
        ),
        out_specs=P("row", ("col", "layer")),
        check_vma=False,
    )
```

time: 210 us -> 113 us (0.54)
  the two profiles are of different devices: /device:TPU:8 before, /device:TPU:6 now
where the time goes in v1:
time: 113 us; the launch traced here: 112 us
  Pallas kernels  50.7 us (45%)
  starting transfers between devices  25.4 us (22%)
  waiting for transfers between devices  13.8 us (12%)
  between operations  13.6 us (12%)
  matrix products  5.49 us (5%)
  local copies, waits for them, and re-layouts  3.37 us (3%)
    ppermute x18, starting transfers between devices, shards(): send = lambda value, axis, d: lax.ppermute(value, 'col', shift[axis](d))  24.6 us
    pallas_call x2, Pallas kernels, near(): pl.pallas_call(body, out_shape=[jax.ShapeDtypeStruct((msg, width), I16)]...  15.7 us
    pallas_call x2, Pallas kernels, pack(): pl.pallas_call(body, out_shape=jax.ShapeDtypeStruct((n, width, width), BF...  10.6 us
    ppermute x18, waiting for transfers between devices, shards(): send = lambda value, axis, d: lax.ppermute(value, 'col', shift[axis](d))  8.88 us
    pallas_call x2, Pallas kernels, home(): pl.pallas_call(body, out_shape=jax.ShapeDtypeStruct((4, half, width), F32...  8.05 us
    pallas_call x2, Pallas kernels, far(): pl.pallas_call(body, out_shape=[jax.ShapeDtypeStruct((msg, width), I16)]...  7.99 us
    dot_general x1, matrix products, shards(): holes = jnp.dot(hole_integrals, gathered, preferred_element_type=F32)  5.49 us
    pallas_call x2, Pallas kernels, turn(): pl.pallas_call(body, out_shape=[jax.ShapeDtypeStruct((half, width), F32)]...  4.66 us
  transfers between devices with their start and end apart: 22, of which 4 were waited for; matrix products, arithmetic and copies ran while one was open for 6% of the time, Pallas kernels for 44%

profile of v1, /device:TPU:6, one launch (start us, length us, event | category | flops | bytes accessed | tf_op | source)
XLA Modules:
  0.0 112.4 jit_solution(17926688762115247283)
XLA Ops:
  6.5 0.7 all-gather.2.cloned.1.call-update
  7.3 0.1 copy-done
  7.3 0.1 reshape.3
  7.4 0.1 pad_add_fusion.meta_ref
  7.5 5.8 %pack.3 = bf16[9,384,384]{2,1,0:T(8,128)(2,1)S(1)} custom-call(s32[291]{0:T(512)S(1)} %pad_add_fusion.meta_ref, bf16[384,12288]{1,0:T(8,128)(2,1)} %v_ref.15), custom_call_target="tpu_custom_call" | custom-call | bytes 5308416 | tf_op jit(solution)/shard_map/pack/pallas_call | solution.py:103
  13.3 0.0 copy-start.1
  13.4 0.1 collective-permute-start.2
  13.5 4.8 %pack.2 = bf16[7,384,384]{2,1,0:T(8,128)(2,1)S(1)} custom-call(s32[291]{0:T(512)S(1)} %pad_add_fusion.meta_ref, bf16[384,12288]{1,0:T(8,128)(2,1)} %v_ref.15), custom_call_target="tpu_custom_call" | custom-call | bytes 4128768 | tf_op jit(solution)/shard_map/pack/pallas_call | solution.py:103
  18.2 0.6 collective-permute-start.1
  18.8 0.1 collective-permute-start
  18.9 4.2 %collective-permute-done.ap_ref = bf16[512,384]{1,0:T(8,128)(2,1)S(1)} collective-permute-done((bf16[512,384]{1,0:T(8,128)(2,1)S(1)}, bf16[512,384]{1,0:T(8,128)(2,1)S(1)}, u32[]{:S(2)}, u32[]{:S(2)}) %collective-permute-start) | collective-permute-done | bytes 393248 | tf_op jit(solution)/shard_map/ppermute | solution.py:382
  23.1 0.0 collective-permute-done.1.v1_ref.vp_ref
  23.1 4.0 %far_y.1 = (s16[528,384]{1,0:T(8,128)(2,1)S(1)}, s16[528,384]{1,0:T(8,128)(2,1)S(1)}) custom-call(s32[291]{0:T(512)S(1)} %pad_add_fusion.meta_ref, bf16[512,384]{1,0:T(8,128)(2,1)S(1)} %copy-done.1, bf16[512,384]{1,0:T(8,128)(2,1)S(1)} %collective-permute-done.ap_ref, bf16[384,12288]{1,0:T(8,128)(2,1)} %v_ref.15, ...), custom_call_target="tpu_custom_call" | custom-call | flops 603979776 | bytes 2359296 | tf_op jit(solution)/shard_map/far_y/pallas_call | solution.py:154
  27.1 1.7 %collective-permute-start.10 = (s16[528,384]{1,0:T(8,128)(2,1)S(1)}, s16[528,384]{1,0:T(8,128)(2,1)S(1)}, u32[]{:S(2)}, u32[]{:S(2)}) collective-permute-start(s16[528,384]{1,0:T(8,128)(2,1)S(1)} %get-tuple-element.39), channel_id=1, source_target_pairs={{0,8},{2,10},{4,12},{6,14},{8,16},{10,18},{12,20},{14,22},{16,24},... | collective-permute-start | bytes 1216520 | tf_op jit(solution)/shard_map/ppermute | solution.py:387
  28.8 1.7 %collective-permute-start.11 = (s16[528,384]{1,0:T(8,128)(2,1)S(1)}, s16[528,384]{1,0:T(8,128)(2,1)S(1)}, u32[]{:S(2)}, u32[]{:S(2)}) collective-permute-start(s16[528,384]{1,0:T(8,128)(2,1)S(1)} %get-tuple-element.40), channel_id=1, source_target_pairs={{0,24},{2,26},{4,28},{6,30},{8,0},{10,2},{12,4},{14,6},{16,8},{18,... | collective-permute-start | bytes 1216520 | tf_op jit(solution)/shard_map/ppermute | solution.py:387
  30.4 4.0 %far_x.1 = (s16[528,384]{1,0:T(8,128)(2,1)S(1)}, s16[528,384]{1,0:T(8,128)(2,1)S(1)}) custom-call(s32[291]{0:T(512)S(1)} %pad_add_fusion.meta_ref, bf16[512,384]{1,0:T(8,128)(2,1)S(1)} %copy-done.1, bf16[512,384]{1,0:T(8,128)(2,1)S(1)} %collective-permute-done.ap_ref, bf16[384,12288]{1,0:T(8,128)(2,1)} %v_ref.15, ...), custom_call_target="tpu_custom_call" | custom-call | flops 603979776 | bytes 2359296 | tf_op jit(solution)/shard_map/far_x/pallas_call | solution.py:154
  34.5 2.3 %collective-permute-start.4 = (s16[528,384]{1,0:T(8,128)(2,1)S(1)}, s16[528,384]{1,0:T(8,128)(2,1)S(1)}, u32[]{:S(2)}, u32[]{:S(2)}) collective-permute-start(s16[528,384]{1,0:T(8,128)(2,1)S(1)} %get-tuple-element.30), channel_id=1, source_target_pairs={{0,2},{2,4},{4,6},{6,0},{8,10},{10,12},{12,14},{14,8},{16,18},{18,... | collective-permute-start | bytes 1216520 | tf_op jit(solution)/shard_map/ppermute | solution.py:387
  36.7 0.0 collective-permute-start.5
  36.7 0.0 collective-permute-done.2.v2_ref
  36.7 1.5 %copy-done.5 = bf16[9,384,384]{2,1,0:T(8,128)(2,1)} copy-done((bf16[9,384,384]{2,1,0:T(8,128)(2,1)}, bf16[9,384,384]{2,1,0:T(8,128)(2,1)S(1)}, u32[]{:S(2)}) %copy-start.5) | copy-done | bytes 2654232
  38.2 7.4 %near_y.1 = (s16[528,384]{1,0:T(8,128)(2,1)S(1)}, s16[528,384]{1,0:T(8,128)(2,1)S(1)}, f32[512,384]{1,0:T(8,128)S(1)}, f32[512,384]{1,0:T(8,128)S(1)}) custom-call(s32[291]{0:T(512)S(1)} %pad_add_fusion.meta_ref, bf16[512,384]{1,0:T(8,128)(2,1)S(1)} %copy-done.1, bf16[512,384]{1,0:T(8,128)(2,1)S(1)} %collective-permute-done.ap_ref, ...), custom_call_target="tpu_custom_call" | custom-call | flops 1207959552 | bytes 4718592 | tf_op jit(solution)/shard_map/near_y/pallas_call | solution.py:227
  45.7 0.0 collective-permute-done.10.ui_ref.uc_ref
  45.7 0.0 collective-permute-done.11.di_ref.dc_ref
  45.7 0.7 relay_y.1
  46.4 0.3 collective-permute-start.12
  46.7 3.0 %collective-permute-start.14 = (s16[528,384]{1,0:T(8,128)(2,1)S(1)}, s16[528,384]{1,0:T(8,128)(2,1)S(1)}, u32[]{:S(2)}, u32[]{:S(2)}) collective-permute-start(s16[528,384]{1,0:T(8,128)(2,1)S(1)} %get-tuple-element.45), channel_id=1, source_target_pairs={{0,24},{2,26},{4,28},{6,30},{8,0},{10,2},{12,4},{14,6},{16,8},{18,... | collective-permute-start | bytes 1216520 | tf_op jit(solution)/shard_map/ppermute | solution.py:387
  49.7 0.0 collective-permute-start.13
  49.7 0.0 collective-permute-done.4.ui_ref.uc_ref
  49.7 3.2 %collective-permute-start.9 = (s16[528,384]{1,0:T(8,128)(2,1)S(1)}, s16[528,384]{1,0:T(8,128)(2,1)S(1)}, u32[]{:S(2)}, u32[]{:S(2)}) collective-permute-start(s16[528,384]{1,0:T(8,128)(2,1)S(1)} %get-tuple-element.38), channel_id=1, source_target_pairs={{0,24},{2,26},{4,28},{6,30},{8,0},{10,2},{12,4},{14,6},{16,8},{18,... | collective-permute-start | bytes 1216520 | tf_op jit(solution)/shard_map/ppermute | solution.py:387
  53.0 8.3 %near_x.1 = (s16[528,384]{1,0:T(8,128)(2,1)}, s16[528,384]{1,0:T(8,128)(2,1)}, f32[512,384]{1,0:T(8,128)S(1)}, f32[512,384]{1,0:T(8,128)S(1)}) custom-call(s32[291]{0:T(512)S(1)} %pad_add_fusion.meta_ref, bf16[512,384]{1,0:T(8,128)(2,1)S(1)} %copy-done.1, bf16[512,384]{1,0:T(8,128)(2,1)S(1)} %collective-permute-done.ap_ref, bf16[384,12288]{1,0:T(8,128)(2,1)} %v_ref.15, ...), custom_call_target="tpu_custom_call" | custom-call | flops 1207959552 | bytes 4718592 | tf_op jit(solution)/shard_map/near_x/pallas_call | solution.py:227
  61.3 0.0 collective-permute-done.5.di_ref.dc_ref
  61.3 1.6 %relay_x.1 = (s16[528,384]{1,0:T(8,128)(2,1)}, s16[528,384]{1,0:T(8,128)(2,1)}) custom-call(s16[528,384]{1,0:T(8,128)(2,1)S(1)} %collective-permute-done.4.ui_ref.uc_ref, s16[528,384]{1,0:T(8,128)(2,1)S(1)} %collective-permute-done.4.ui_ref.uc_ref, s16[528,384]{1,0:T(8,128)(2,1)S(1)} %collective-permute-done.5.di_ref.dc_ref, ...), custom_call_target="tpu_custom_call" | custom-call | bytes 3145728 | tf_op jit(solution)/shard_map/relay_x/pallas_call | solution.py:301
  62.8 3.2 %collective-permute-start.6 = (s16[528,384]{1,0:T(8,128)(2,1)}, s16[528,384]{1,0:T(8,128)(2,1)S(1)}, u32[]{:S(2)}, u32[]{:S(2)}) collective-permute-start(s16[528,384]{1,0:T(8,128)(2,1)} %get-tuple-element.34), channel_id=1, source_target_pairs={{0,2},{2,4},{4,6},{6,0},{8,10},{10,12},{12,14},{14,8},{16,18},{18,... | collective-permute-start | bytes 1216520 | tf_op jit(solution)/shard_map/ppermute | solution.py:387
  66.1 0.0 collective-permute-done.12.ff.ffc
  66.1 0.0 collective-permute-start.8
  66.1 0.0 collective-permute-done.14.sf.sfc
  66.1 0.1 collective-permute-start.3
  66.2 1.0 collective-permute-done.13.sn.snc
  67.2 3.0 %collective-permute-start.7 = (s16[528,384]{1,0:T(8,128)(2,1)}, s16[528,384]{1,0:T(8,128)(2,1)}, u32[]{:S(2)}, u32[]{:S(2)}) collective-permute-start(s16[528,384]{1,0:T(8,128)(2,1)} %get-tuple-element.35), channel_id=1, source_target_pairs={{0,2},{2,4},{4,6},{6,0},{8,10},{10,12},{12,14},{14,8},{16,18},{18,... | collective-permute-start | bytes 1216520 | tf_op jit(solution)/shard_map/ppermute | solution.py:387
  70.2 4.0 %home_y.1.st_ref = f32[4,256,384]{2,1,0:T(8,128)S(1)} custom-call(s32[291]{0:T(512)S(1)} %pad_add_fusion.meta_ref, bf16[512,384]{1,0:T(8,128)(2,1)S(1)} %copy-done.1, bf16[512,384]{1,0:T(8,128)(2,1)S(1)} %collective-permute-done.ap_ref, bf16[384,12288]{1,0:T(8,128)(2,1)} %v_ref.15, bf16[7,384,384]{2,1,0:T(8,128)(2,1)S(1)} %collective-permute-done.1.v1_ref.vp_ref, ...), custom_call_target="tpu_custom_call" | custom-call | flops 603979776 | bytes 2359296 | tf_op jit(solution)/shard_map/home_y/pallas_call | solution.py:264
  74.2 0.0 copy-start.6
  74.2 0.0 copy-start.7
  74.2 0.0 collective-permute-done.9.fn.fnc
  74.2 1.8 %turn_y.1 = (f32[256,384]{1,0:T(8,128)S(1)}, s16[272,384]{1,0:T(8,128)(2,1)}, s16[272,384]{1,0:T(8,128)(2,1)}, s16[272,384]{1,0:T(8,128)(2,1)}) custom-call(f32[4,256,384]{2,1,0:T(8,128)S(1)} %home_y.1.st_ref, s16[528,384]{1,0:T(8,128)(2,1)S(1)} %collective-permute-done.9.fn.fnc, s16[528,384]{1,0:T(8,128)(2,1)S(1)} %collective-permute-done.9.fn.fnc, ...), custom_call_target="tpu_custom_call" | custom-call | bytes 3932160 | tf_op jit(solution)/shard_map/turn_y/pallas_call | solution.py:338
  76.1 0.8 copy-done.3
  76.9 0.7 collective-permute-start.18
  77.5 0.9 copy.7.occ_ref
  78.4 4.0 %home_x.1.st_ref = f32[4,256,384]{2,1,0:T(8,128)S(1)} custom-call(s32[291]{0:T(512)S(1)} %pad_add_fusion.meta_ref, bf16[512,384]{1,0:T(8,128)(2,1)S(1)} %copy-done.1, bf16[512,384]{1,0:T(8,128)(2,1)S(1)} %collective-permute-done.ap_ref, bf16[384,12288]{1,0:T(8,128)(2,1)} %v_ref.15, bf16[7,384,384]{2,1,0:T(8,128)(2,1)S(1)} %collective-permute-done.1.v1_ref.vp_ref, ...), custom_call_target="tpu_custom_call" | custom-call | flops 603979776 | bytes 2359296 | tf_op jit(solution)/shard_map/home_x/pallas_call | solution.py:264
  82.4 0.0 collective-permute-done.6.ff.ffc
  82.5 1.2 %collective-permute-start.19 = (s16[272,384]{1,0:T(8,128)(2,1)}, s16[272,384]{1,0:T(8,128)(2,1)S(1)}, u32[]{:S(2)}, u32[]{:S(2)}) collective-permute-start(s16[272,384]{1,0:T(8,128)(2,1)} %get-tuple-element.51), channel_id=1, source_target_pairs={{0,2},{2,4},{4,6},{6,0},{8,10},{10,12},{12,14},{14,8},{16,18},{18,... | collective-permute-start | bytes 626696 | tf_op jit(solution)/shard_map/ppermute | solution.py:387
  83.6 0.0 collective-permute-done.8.sf.sfc
  83.6 0.9 collective-permute-start.20
  84.6 7.4 %collective-permute-done.3.fn.fnc = s16[528,384]{1,0:T(8,128)(2,1)} collective-permute-done((s16[528,384]{1,0:T(8,128)(2,1)}, s16[528,384]{1,0:T(8,128)(2,1)}, u32[]{:S(2)}, u32[]{:S(2)}) %collective-permute-start.3) | collective-permute-done | bytes 405536 | tf_op jit(solution)/shard_map/ppermute | solution.py:387
  91.9 2.8 %turn_x.1 = (f32[256,384]{1,0:T(8,128)S(1)}, s16[272,384]{1,0:T(8,128)(2,1)S(1)}, s16[272,384]{1,0:T(8,128)(2,1)S(1)}, s16[272,384]{1,0:T(8,128)(2,1)S(1)}) custom-call(f32[4,256,384]{2,1,0:T(8,128)S(1)} %home_x.1.st_ref, s16[528,384]{1,0:T(8,128)(2,1)} %collective-permute-done.3.fn.fnc, s16[528,384]{1,0:T(8,128)(2,1)} %collective-permute-done.3.fn.fnc, ...), custom_call_target="tpu_custom_call" | custom-call | bytes 3932160 | tf_op jit(solution)/shard_map/turn_x/pallas_call | solution.py:338
  94.8 0.1 collective-permute-start.15
  94.9 1.2 %collective-permute-start.16 = (s16[272,384]{1,0:T(8,128)(2,1)S(1)}, s16[272,384]{1,0:T(8,128)(2,1)S(1)}, u32[]{:S(2)}, u32[]{:S(2)}) collective-permute-start(s16[272,384]{1,0:T(8,128)(2,1)S(1)} %get-tuple-element.48), channel_id=1, source_target_pairs={{0,8},{2,10},{4,12},{6,14},{8,16},{10,18},{12,20},{14,22},{16,24},... | collective-permute-start | bytes 626696 | tf_op jit(solution)/shard_map/ppermute | solution.py:387
  96.1 0.0 collective-permute-done.18.y1
  96.1 2.1 %collective-permute-start.17 = (s16[272,384]{1,0:T(8,128)(2,1)S(1)}, s16[272,384]{1,0:T(8,128)(2,1)S(1)}, u32[]{:S(2)}, u32[]{:S(2)}) collective-permute-start(s16[272,384]{1,0:T(8,128)(2,1)S(1)} %get-tuple-element.49), channel_id=1, source_target_pairs={{0,24},{2,26},{4,28},{6,30},{8,0},{10,2},{12,4},{14,6},{16,8},{18,... | collective-permute-start | bytes 626696 | tf_op jit(solution)/shard_map/ppermute | solution.py:387
  98.2 5.5 %fusion.holes_ref = f32[512,384]{1,0:T(8,128)S(1)} fusion(bf16[512,4096]{1,0:T(8,128)(2,1)} %param.8, bf16[4096,384]{1,0:T(8,128)(2,1)} %all-gather.2.cloned.1.call-done), kind=kOutput, calls=%fused_computation.2 | convolution fusion | flops 1610612736 | bytes 8126464 | tf_op jit(solution)/shard_map/dot_general | solution.py:407
  103.7 0.0 collective-permute-done.19.y2
  103.7 0.0 collective-permute-done.15.x1
  103.7 0.5 collective-permute-done.16.x2
  104.2 0.0 collective-permute-done.17.x3
  104.2 1.4 %finish.1 = f32[512,384]{1,0:T(8,128)} custom-call(f32[256,384]{1,0:T(8,128)S(1)} %get-tuple-element.37.ox, f32[256,384]{1,0:T(8,128)S(1)} %copy-done.4, s16[272,384]{1,0:T(8,128)(2,1)S(1)} %collective-permute-done.15.x1, s16[272,384]{1,0:T(8,128)(2,1)S(1)} %collective-permute-done.16.x2, s16[272,384]{1,0:T(8,128)(2,1)S(1)} %collective-permute-done.17.x3, ...), custom_call_target="tpu_custom_call" | custom-call | bytes 2359296 | tf_op jit(solution)/shard_map/finish/pallas_call | solution.py:364
  (16 shorter events, 0.0 us)
Async XLA Ops:
  6.5 0.8 copy-start
  6.5 91.6 %all-gather.2.cloned.1.call-start = ((), (), s32[]{:S(2)}) async-start(), calls=%async_computation | async-start | bytes 3538944 | tf_op jit(solution)/shard_map/all_gather | solution.py:381
  13.3 5.5 %copy-start.1 = (bf16[512,384]{1,0:T(8,128)(2,1)S(1)}, bf16[512,384]{1,0:T(8,128)(2,1)}, u32[]{:S(2)}) copy-start(bf16[512,384]{1,0:T(8,128)(2,1)} %a_ref.11) | copy-start | bytes 1179652
  13.4 23.4 %collective-permute-start.2 = (bf16[9,384,384]{2,1,0:T(8,128)(2,1)S(1)}, bf16[9,384,384]{2,1,0:T(8,128)(2,1)S(1)}, u32[]{:S(2)}, u32[]{:S(2)}) collective-permute-start(bf16[9,384,384]{2,1,0:T(8,128)(2,1)S(1)} %pack.3), channel_id=1, source_target_pairs={{0,1},{1,0},{2,3},{3,2},{4,5},{5,4},{6,7},{7,6},{8,9},{9,8},{10,11... | collective-permute-start | bytes 7962632 | tf_op jit(solution)/shard_map/ppermute | solution.py:384
  18.2 4.9 %collective-permute-start.1 = (bf16[7,384,384]{2,1,0:T(8,128)(2,1)S(1)}, bf16[7,384,384]{2,1,0:T(8,128)(2,1)S(1)}, u32[]{:S(2)}, u32[]{:S(2)}) collective-permute-start(bf16[7,384,384]{2,1,0:T(8,128)(2,1)S(1)} %pack.2), channel_id=1, source_target_pairs={{0,1},{1,0},{2,3},{3,2},{4,5},{5,4},{6,7},{7,6},{8,9},{9,8},{10,11... | collective-permute-start | bytes 6193160 | tf_op jit(solution)/shard_map/ppermute | solution.py:383
  18.8 4.3 %collective-permute-start = (bf16[512,384]{1,0:T(8,128)(2,1)S(1)}, bf16[512,384]{1,0:T(8,128)(2,1)S(1)}, u32[]{:S(2)}, u32[]{:S(2)}) collective-permute-start(bf16[512,384]{1,0:T(8,128)(2,1)S(1)} %copy-done.1), channel_id=1, source_target_pairs={{0,1},{1,0},{2,3},{3,2},{4,5},{5,4},{6,7},{7,6},{8,9},{9,8},{10,11... | collective-permute-start | bytes 1179656 | tf_op jit(solution)/shard_map/ppermute | solution.py:382
  27.1 18.6 %collective-permute-start.10 = (s16[528,384]{1,0:T(8,128)(2,1)S(1)}, s16[528,384]{1,0:T(8,128)(2,1)S(1)}, u32[]{:S(2)}, u32[]{:S(2)}) collective-permute-start(s16[528,384]{1,0:T(8,128)(2,1)S(1)} %get-tuple-element.39), channel_id=1, source_target_pairs={{0,8},{2,10},{4,12},{6,14},{8,16},{10,18},{12,20},{14,22},{16,24},... | collective-permute-start | bytes 1216520 | tf_op jit(solution)/shard_map/ppermute | solution.py:387
  28.8 16.9 %collective-permute-start.11 = (s16[528,384]{1,0:T(8,128)(2,1)S(1)}, s16[528,384]{1,0:T(8,128)(2,1)S(1)}, u32[]{:S(2)}, u32[]{:S(2)}) collective-permute-start(s16[528,384]{1,0:T(8,128)(2,1)S(1)} %get-tuple-element.40), channel_id=1, source_target_pairs={{0,24},{2,26},{4,28},{6,30},{8,0},{10,2},{12,4},{14,6},{16,8},{18,... | collective-permute-start | bytes 1216520 | tf_op jit(solution)/shard_map/ppermute | solution.py:387
  34.5 15.3 %collective-permute-start.4 = (s16[528,384]{1,0:T(8,128)(2,1)S(1)}, s16[528,384]{1,0:T(8,128)(2,1)S(1)}, u32[]{:S(2)}, u32[]{:S(2)}) collective-permute-start(s16[528,384]{1,0:T(8,128)(2,1)S(1)} %get-tuple-element.30), channel_id=1, source_target_pairs={{0,2},{2,4},{4,6},{6,0},{8,10},{10,12},{12,14},{14,8},{16,18},{18,... | collective-permute-start | bytes 1216520 | tf_op jit(solution)/shard_map/ppermute | solution.py:387
  36.7 24.5 %collective-permute-start.5 = (s16[528,384]{1,0:T(8,128)(2,1)S(1)}, s16[528,384]{1,0:T(8,128)(2,1)S(1)}, u32[]{:S(2)}, u32[]{:S(2)}) collective-permute-start(s16[528,384]{1,0:T(8,128)(2,1)S(1)} %get-tuple-element.31), channel_id=1, source_target_pairs={{0,6},{2,0},{4,2},{6,4},{8,14},{10,8},{12,10},{14,12},{16,22},{18,... | collective-permute-start | bytes 1216520 | tf_op jit(solution)/shard_map/ppermute | solution.py:387
  36.7 1.5 %copy-start.5 = (bf16[9,384,384]{2,1,0:T(8,128)(2,1)}, bf16[9,384,384]{2,1,0:T(8,128)(2,1)S(1)}, u32[]{:S(2)}) copy-start(bf16[9,384,384]{2,1,0:T(8,128)(2,1)S(1)} %collective-permute-done.2.v2_ref) | copy-start | bytes 7962628
  46.4 19.7 %collective-permute-start.12 = (s16[528,384]{1,0:T(8,128)(2,1)S(1)}, s16[528,384]{1,0:T(8,128)(2,1)S(1)}, u32[]{:S(2)}, u32[]{:S(2)}) collective-permute-start(s16[528,384]{1,0:T(8,128)(2,1)S(1)} %get-tuple-element.43), channel_id=1, source_target_pairs={{0,8},{2,10},{4,12},{6,14},{8,16},{10,18},{12,20},{14,22},{16,24},... | collective-permute-start | bytes 1216520 | tf_op jit(solution)/shard_map/ppermute | solution.py:387
  46.7 19.4 %collective-permute-start.14 = (s16[528,384]{1,0:T(8,128)(2,1)S(1)}, s16[528,384]{1,0:T(8,128)(2,1)S(1)}, u32[]{:S(2)}, u32[]{:S(2)}) collective-permute-start(s16[528,384]{1,0:T(8,128)(2,1)S(1)} %get-tuple-element.45), channel_id=1, source_target_pairs={{0,24},{2,26},{4,28},{6,30},{8,0},{10,2},{12,4},{14,6},{16,8},{18,... | collective-permute-start | bytes 1216520 | tf_op jit(solution)/shard_map/ppermute | solution.py:387
  49.7 17.5 %collective-permute-start.13 = (s16[528,384]{1,0:T(8,128)(2,1)S(1)}, s16[528,384]{1,0:T(8,128)(2,1)S(1)}, u32[]{:S(2)}, u32[]{:S(2)}) collective-permute-start(s16[528,384]{1,0:T(8,128)(2,1)S(1)} %get-tuple-element.44), channel_id=1, source_target_pairs={{0,8},{2,10},{4,12},{6,14},{8,16},{10,18},{12,20},{14,22},{16,24},... | collective-permute-start | bytes 1216520 | tf_op jit(solution)/shard_map/ppermute | solution.py:387
  49.7 24.5 %collective-permute-start.9 = (s16[528,384]{1,0:T(8,128)(2,1)S(1)}, s16[528,384]{1,0:T(8,128)(2,1)S(1)}, u32[]{:S(2)}, u32[]{:S(2)}) collective-permute-start(s16[528,384]{1,0:T(8,128)(2,1)S(1)} %get-tuple-element.38), channel_id=1, source_target_pairs={{0,24},{2,26},{4,28},{6,30},{8,0},{10,2},{12,4},{14,6},{16,8},{18,... | collective-permute-start | bytes 1216520 | tf_op jit(solution)/shard_map/ppermute | solution.py:387
  62.8 19.6 %collective-permute-start.6 = (s16[528,384]{1,0:T(8,128)(2,1)}, s16[528,384]{1,0:T(8,128)(2,1)S(1)}, u32[]{:S(2)}, u32[]{:S(2)}) collective-permute-start(s16[528,384]{1,0:T(8,128)(2,1)} %get-tuple-element.34), channel_id=1, source_target_pairs={{0,2},{2,4},{4,6},{6,0},{8,10},{10,12},{12,14},{14,8},{16,18},{18,... | collective-permute-start | bytes 1216520 | tf_op jit(solution)/shard_map/ppermute | solution.py:387
  66.1 17.5 %collective-permute-start.8 = (s16[528,384]{1,0:T(8,128)(2,1)}, s16[528,384]{1,0:T(8,128)(2,1)}, u32[]{:S(2)}, u32[]{:S(2)}) collective-permute-start(s16[528,384]{1,0:T(8,128)(2,1)} %get-tuple-element.36), channel_id=1, source_target_pairs={{0,6},{2,0},{4,2},{6,4},{8,14},{10,8},{12,10},{14,12},{16,22},{18,... | collective-permute-start | bytes 1216520 | tf_op jit(solution)/shard_map/ppermute | solution.py:387
  66.1 25.8 %collective-permute-start.3 = (s16[528,384]{1,0:T(8,128)(2,1)}, s16[528,384]{1,0:T(8,128)(2,1)}, u32[]{:S(2)}, u32[]{:S(2)}) collective-permute-start(s16[528,384]{1,0:T(8,128)(2,1)} %get-tuple-element.29), channel_id=1, source_target_pairs={{0,6},{2,0},{4,2},{6,4},{8,14},{10,8},{12,10},{14,12},{16,22},{18,... | collective-permute-start | bytes 1216520 | tf_op jit(solution)/shard_map/ppermute | solution.py:387
  67.2 24.8 %collective-permute-start.7 = (s16[528,384]{1,0:T(8,128)(2,1)}, s16[528,384]{1,0:T(8,128)(2,1)}, u32[]{:S(2)}, u32[]{:S(2)}) collective-permute-start(s16[528,384]{1,0:T(8,128)(2,1)} %get-tuple-element.35), channel_id=1, source_target_pairs={{0,2},{2,4},{4,6},{6,0},{8,10},{10,12},{12,14},{14,8},{16,18},{18,... | collective-permute-start | bytes 1216520 | tf_op jit(solution)/shard_map/ppermute | solution.py:387
  74.2 3.3 %copy-start.6 = (f32[512]{0:T(512)S(1)}, f32[512]{0:T(512)}, u32[]{:S(2)}) copy-start(f32[512]{0:T(512)} %param.10) | copy-start | bytes 6148
  74.2 4.2 %copy-start.7 = (f32[384]{0:T(512)S(1)}, f32[384]{0:T(512)}, u32[]{:S(2)}) copy-start(f32[384]{0:T(512)} %param.11) | copy-start | bytes 4612
  76.1 0.8 copy-start.3
  76.9 19.2 %collective-permute-start.18 = (s16[272,384]{1,0:T(8,128)(2,1)}, s16[272,384]{1,0:T(8,128)(2,1)S(1)}, u32[]{:S(2)}, u32[]{:S(2)}) collective-permute-start(s16[272,384]{1,0:T(8,128)(2,1)} %get-tuple-element.50), channel_id=1, source_target_pairs={{0,4},{2,6},{4,0},{6,2},{8,12},{10,14},{12,8},{14,10},{16,20},{18,... | collective-permute-start | bytes 626696 | tf_op jit(solution)/shard_map/ppermute | solution.py:387
  82.5 21.2 %collective-permute-start.19 = (s16[272,384]{1,0:T(8,128)(2,1)}, s16[272,384]{1,0:T(8,128)(2,1)S(1)}, u32[]{:S(2)}, u32[]{:S(2)}) collective-permute-start(s16[272,384]{1,0:T(8,128)(2,1)} %get-tuple-element.51), channel_id=1, source_target_pairs={{0,2},{2,4},{4,6},{6,0},{8,10},{10,12},{12,14},{14,8},{16,18},{18,... | collective-permute-start | bytes 626696 | tf_op jit(solution)/shard_map/ppermute | solution.py:387
  83.6 20.1 %collective-permute-start.20 = (s16[272,384]{1,0:T(8,128)(2,1)}, s16[272,384]{1,0:T(8,128)(2,1)S(1)}, u32[]{:S(2)}, u32[]{:S(2)}) collective-permute-start(s16[272,384]{1,0:T(8,128)(2,1)} %get-tuple-element.52), channel_id=1, source_target_pairs={{0,6},{2,0},{4,2},{6,4},{8,14},{10,8},{12,10},{14,12},{16,22},{18,... | collective-permute-start | bytes 626696 | tf_op jit(solution)/shard_map/ppermute | solution.py:387
  94.8 8.9 %collective-permute-start.15 = (s16[272,384]{1,0:T(8,128)(2,1)S(1)}, s16[272,384]{1,0:T(8,128)(2,1)S(1)}, u32[]{:S(2)}, u32[]{:S(2)}) collective-permute-start(s16[272,384]{1,0:T(8,128)(2,1)S(1)} %get-tuple-element.47), channel_id=1, source_target_pairs={{0,16},{2,18},{4,20},{6,22},{8,24},{10,26},{12,28},{14,30},{16,0},... | collective-permute-start | bytes 626696 | tf_op jit(solution)/shard_map/ppermute | solution.py:387
  94.9 9.3 %collective-permute-start.16 = (s16[272,384]{1,0:T(8,128)(2,1)S(1)}, s16[272,384]{1,0:T(8,128)(2,1)S(1)}, u32[]{:S(2)}, u32[]{:S(2)}) collective-permute-start(s16[272,384]{1,0:T(8,128)(2,1)S(1)} %get-tuple-element.48), channel_id=1, source_target_pairs={{0,8},{2,10},{4,12},{6,14},{8,16},{10,18},{12,20},{14,22},{16,24},... | collective-permute-start | bytes 626696 | tf_op jit(solution)/shard_map/ppermute | solution.py:387
  96.1 8.1 %copy-start.2 = (f32[512,1]{1,0:T(8,128)S(1)}, f32[512,1]{1,0:T(8,128)}, u32[]{:S(2)}) copy-start(f32[512,1]{1,0:T(8,128)} %copy.7.occ_ref) | copy-start | bytes 6148
  96.1 8.1 %copy-start.4 = (f32[256,384]{1,0:T(8,128)S(1)}, f32[256,384]{1,0:T(8,128)}, u32[]{:S(2)}) copy-start(f32[256,384]{1,0:T(8,128)} %copy-done.3) | copy-start | bytes 1179652
  96.1 8.1 %collective-permute-start.17 = (s16[272,384]{1,0:T(8,128)(2,1)S(1)}, s16[272,384]{1,0:T(8,128)(2,1)S(1)}, u32[]{:S(2)}, u32[]{:S(2)}) collective-permute-start(s16[272,384]{1,0:T(8,128)(2,1)S(1)} %get-tuple-element.49), channel_id=1, source_target_pairs={{0,24},{2,26},{4,28},{6,30},{8,0},{10,2},{12,4},{14,6},{16,8},{18,... | collective-permute-start | bytes 626696 | tf_op jit(solution)/shard_map/ppermute | solution.py:387
Sparse Core Ops, SparseCore 0:
  9.1 47.8 all-gather.1

commit v2 on v0

v2 whole, which is shorter than its diff:
```python
import jax
import jax.numpy as jnp
from jax import lax
from jax.experimental import pallas as pl
from jax.experimental.pallas import tpu as pltpu
from jax.sharding import PartitionSpec as P

TB = 128
X = 4
Y = 4
F32 = jnp.float32
I16 = jnp.int16
I32 = jnp.int32
BF16 = jnp.bfloat16
TOP = 32700.0
STEPS = 64.0
SCALE = 1000
VMEM = 10 * 1024 * 1024
SM = pl.BlockSpec(memory_space=pltpu.SMEM)
VM = pl.BlockSpec(memory_space=pltpu.VMEM)
ANY = pl.BlockSpec(memory_space=pl.ANY)

FAR, NEAR, HOME, ALL = (0, 4), (4, 8), (12, 4), (0, 16)


def hop(first, d):
    pairs = []
    for y in range(Y):
        for x in range(X):
            for layer in range(2):
                along_x = (layer == 0) == first
                to = (y * X + (x + d) % X) if along_x else ((y + d) % Y * X + x)
                pairs.append(((y * X + x) * 2 + layer, to * 2 + layer))
    return pairs


def send(value, first, d):
    return lax.ppermute(value, ("col", "layer"), hop(first, d))


def inside(value):
    return pltpu.with_memory_space_constraint(value, pltpu.VMEM)


def params():
    return pltpu.CompilerParams(vmem_limit_bytes=VMEM)


def cost(flops, moved):
    return pl.CostEstimate(flops=int(flops) // SCALE, bytes_accessed=int(moved) // SCALE, transcendentals=0)


def loop(n, unroll=1):
    def run(step):
        lax.fori_loop(0, n, lambda i, c: (step(i), c)[1], 0, unroll=unroll)
    return run


def rows_at(i, n):
    return pl.ds(pl.multiple_of(i * n, n), n)


def encode(block):
    peak = jnp.maximum(jnp.max(jnp.abs(block), axis=0, keepdims=True), 1e-30)
    code = jnp.floor(jnp.log2(TOP / peak) * STEPS)
    scale = jnp.exp2(code * (1.0 / STEPS))
    return jnp.round(block * scale).astype(I32).astype(I16), code


def put(ref, k, block):
    coded, code = encode(block)
    ref[rows_at(k, TB), :] = coded
    last = slice(ref.shape[0] - 16, ref.shape[0])
    rows = ref[last, :].astype(I32)
    at = lax.broadcasted_iota(I32, rows.shape, 0) == k
    ref[last, :] = jnp.where(at, code.astype(I32), rows).astype(I16)


def get(ref, k):
    rows = ref[ref.shape[0] - 16:, :].astype(I32)
    at = lax.broadcasted_iota(I32, rows.shape, 0) == k
    code = jnp.sum(jnp.where(at, rows, 0).astype(F32), axis=0, keepdims=True)
    scale = jnp.exp2(code * (1.0 / STEPS))
    return ref[rows_at(k, TB), :].astype(I32).astype(F32) * (1.0 / scale)


def pack(name, mask, integrals, parts, after=()):
    width = integrals.shape[0]
    tiles = width // TB
    total = sum(n for _, n, _ in parts)

    def body(mask_ref, v_ref, *refs):
        outs, (mask_s, sem, mask_sem) = refs[len(after):-3], refs[-3:]
        mask_copy = pltpu.make_async_copy(mask_ref, mask_s, mask_sem)
        mask_copy.start()
        col, layer = lax.axis_index("col"), lax.axis_index("layer")
        x, y = lax.rem(col, X), lax.div(col, X)
        row = (col * 2 + layer) * tiles

        def source(place, mine):
            who = layer if mine else 1 - layer
            d, o = jnp.right_shift(place, 2), jnp.bitwise_and(place, 3)
            d = jnp.where(d == 0, 2, jnp.where(d == 1, 1, jnp.where(d == 2, 3, 0)))
            dx, dy = jnp.where(who == 0, d, o), jnp.where(who == 0, o, d)
            return (lax.rem(y + dy, Y) * X + lax.rem(x + dx, X)) * 2 + who

        def copy(out, k, at, slot):
            return pltpu.make_async_copy(
                v_ref.at[:, pl.ds(pl.multiple_of(at * width, width), width)], out.at[k], sem.at[slot]
            )

        slots = [sum(n for _, n, _ in parts[:p]) for p in range(len(parts))]
        for (start, n, mine), out, slot in zip(parts, outs, slots):
            @loop(n)
            def _(k):
                copy(out, k, source(start + k, mine), slot + k).start()
        mask_copy.wait()
        for (start, n, mine), out, slot in zip(parts, outs, slots):
            @loop(n)
            def _(k):
                at = source(start + k, mine)
                copy(out, k, at, slot + k).wait()
                for kt in range(tiles):
                    for qt in range(tiles):
                        here = (k, slice(kt * TB, (kt + 1) * TB), slice(qt * TB, (qt + 1) * TB))

                        @pl.when(mask_s[row + kt, at * tiles + qt] == 0)
                        def _():
                            out[here] = jnp.zeros((TB, TB), BF16)

    return pl.pallas_call(
        body,
        out_shape=[pltpu.VMEM((n, width, width), BF16) for _, n, _ in parts],
        in_specs=[ANY, ANY] + [ANY] * len(after),
        out_specs=[VM] * len(parts),
        scratch_shapes=[pltpu.SMEM(mask.shape, I32), pltpu.SemaphoreType.DMA((total,)), pltpu.SemaphoreType.DMA(())],
        compiler_params=params(),
        cost_estimate=cost(0, 4 * total * width * width),
        name=name,
    )(*(pltpu.with_memory_space_constraint(v, pltpu.HBM) for v in (mask, integrals)), *after)


def product(lhs, own_ref, k, their_ref, their_k):
    return jnp.dot(lhs, jnp.concatenate([own_ref[k], their_ref[their_k]], axis=0), preferred_element_type=F32)


def left(a_ref, ap_ref):
    return jnp.concatenate([a_ref[...], ap_ref[...]], axis=1)


def far(a, ap, own_v, v1):
    rows, width = a.shape
    half = rows // 2
    n = half // TB
    msg = 4 * half + 16

    def body(a_ref, ap_ref, own_ref, v1_ref, up_ref, down_ref):
        lhs = left(a_ref, ap_ref)

        @loop(4)
        def _(o):
            part = product(lhs, own_ref, o, v1_ref, o)
            for b in range(n):
                put(up_ref, o * n + b, part[b * TB:(b + 1) * TB])
                put(down_ref, o * n + b, part[half + b * TB:half + (b + 1) * TB])

    return pl.pallas_call(
        body,
        out_shape=[pltpu.VMEM((msg, width), I16)] * 2,
        in_specs=[VM] * 4,
        out_specs=[VM] * 2,
        compiler_params=params(),
        cost_estimate=cost(2 * 4 * rows * 2 * width * width, 4 * 4 * width * width),
        name="far",
    )(*map(inside, (a, ap, own_v, v1)))


def near(a, ap, own_v, v2):
    rows, width = a.shape
    half = rows // 2
    n = half // TB
    msg = 4 * half + 16

    def body(a_ref, ap_ref, own_ref, v2_ref, up_ref, down_ref, up_st, down_st):
        lhs = left(a_ref, ap_ref)

        @loop(4)
        def _(o):
            part = product(lhs, own_ref, 4 + o, v2_ref, o)
            up_st[rows_at(o, half), :] = part[:half]
            for b in range(n):
                put(up_ref, o * n + b, part[half + b * TB:half + (b + 1) * TB])
            part = product(lhs, own_ref, 8 + o, v2_ref, 4 + o)
            down_st[rows_at(o, half), :] = part[half:]
            for b in range(n):
                put(down_ref, o * n + b, part[b * TB:(b + 1) * TB])

    return pl.pallas_call(
        body,
        out_shape=[pltpu.VMEM((msg, width), I16)] * 2 + [pltpu.VMEM((4 * half, width), F32)] * 2,
        in_specs=[VM] * 4,
        out_specs=[VM] * 4,
        compiler_params=params(),
        cost_estimate=cost(2 * 8 * rows * 2 * width * width, 8 * 4 * width * width),
        name="near",
    )(*map(inside, (a, ap, own_v, v2)))


def home(a, ap, own_v, v2, near_up, near_down):
    rows, width = a.shape
    n = rows // TB
    h = n // 2

    def body(a_ref, ap_ref, own_ref, v2_ref, up_ref, down_ref, out_ref):
        lhs = left(a_ref, ap_ref)

        @loop(4)
        def _(o):
            part = product(lhs, own_ref, 12 + o, v2_ref, o)
            for b in range(n):
                here = slice(b * TB, (b + 1) * TB)
                out_ref[o, here, :] = part[here] + get(up_ref if b < h else down_ref, o * h + b % h)

    return pl.pallas_call(
        body,
        out_shape=pltpu.VMEM((4, rows, width), F32),
        in_specs=[VM] * 6,
        out_specs=VM,
        compiler_params=params(),
        cost_estimate=cost(2 * 4 * rows * 2 * width * width, 4 * 4 * width * width),
        name="home",
    )(*map(inside, (a, ap, own_v, v2, near_up, near_down)))


def relay(got, own):
    rows, width = own.shape

    def body(got_ref, own_ref, out_ref):
        @loop(rows // TB)
        def _(k):
            put(out_ref, k, own_ref[rows_at(k, TB), :] + get(got_ref, k))

    return pl.pallas_call(
        body,
        out_shape=pltpu.VMEM(got.shape, I16),
        in_specs=[VM] * 2,
        out_specs=VM,
        compiler_params=params(),
        cost_estimate=cost(0, 8 * rows * width),
        name="relay",
    )(*map(inside, (got, own)))


def turn(st, far_up, far_down):
    _, rows, width = st.shape
    n = rows // TB
    h = n // 2

    def body(st_ref, up_ref, down_ref, own_ref, m1_ref, m2_ref, m3_ref):
        for o, ref in ((2, m2_ref), (1, m1_ref), (3, m3_ref), (0, own_ref)):
            for b in range(n):
                part = st_ref[o, b * TB:(b + 1) * TB, :] + get(up_ref if b < h else down_ref, o * h + b % h)
                if o == 0:
                    ref[b * TB:(b + 1) * TB, :] = part
                else:
                    put(ref, b, part)

    return pl.pallas_call(
        body,
        out_shape=[pltpu.VMEM((rows, width), F32)] + [pltpu.VMEM((rows + 16, width), I16)] * 3,
        in_specs=[VM] * 3,
        out_specs=[VM] * 4,
        compiler_params=params(),
        cost_estimate=cost(0, 4 * rows * width * 10),
        name="turn",
    )(*map(inside, (st, far_up, far_down)))


def hole_sum(hole_integrals, gathered):
    rows, depth = hole_integrals.shape
    width = gathered.shape[1]
    parts = 8
    step = depth // parts

    def body(h_hbm, a_hbm, out_ref, h_ref, a_ref, sem):
        copies = []
        for i in range(parts):
            here = slice(i * step, (i + 1) * step)
            pair = (
                pltpu.make_async_copy(h_hbm.at[:, here], h_ref.at[i], sem.at[0, i]),
                pltpu.make_async_copy(a_hbm.at[here, :], a_ref.at[i], sem.at[1, i]),
            )
            for copy in pair:
                copy.start()
            copies.append(pair)
        for i in range(parts):
            for copy in copies[i]:
                copy.wait()
            part = jnp.dot(h_ref[i], a_ref[i], preferred_element_type=F32)
            out_ref[...] = part if i == 0 else out_ref[...] + part

    return pl.pallas_call(
        body,
        out_shape=pltpu.VMEM((rows, width), F32),
        in_specs=[ANY] * 2,
        out_specs=VM,
        scratch_shapes=[
            pltpu.VMEM((parts, rows, step), BF16),
            pltpu.VMEM((parts, step, width), BF16),
            pltpu.SemaphoreType.DMA((2, parts)),
        ],
        compiler_params=params(),
        cost_estimate=cost(2 * rows * depth * width, 2 * depth * (rows + width)),
        name="holes",
    )(*(pltpu.with_memory_space_constraint(v, pltpu.HBM) for v in (hole_integrals, gathered)))


def finish(own, got, holes, occupied, virtual):
    rows, width = own.shape

    def body(own_ref, m1, m2, m3, holes_ref, occ_ref, virt_ref, out_ref):
        virt = virt_ref[...]
        for b in range(rows // TB):
            here = slice(b * TB, (b + 1) * TB)
            total = own_ref[here, :] + get(m1, b) + get(m2, b) + get(m3, b)
            occ = jnp.broadcast_to(occ_ref[:, here], (TB, TB)).T
            occ = jnp.concatenate([occ] * (width // TB), axis=1)
            out_ref[here, :] = (total + holes_ref[here, :]) / (virt - occ)

    return pl.pallas_call(
        body,
        out_shape=jax.ShapeDtypeStruct((rows, width), F32),
        in_specs=[VM] * 7,
        out_specs=VM,
        compiler_params=params(),
        cost_estimate=cost(0, 4 * rows * width * 6),
        name="finish",
    )(own, *got, holes, occupied[None, :], virtual[None, :])


def shards(amplitudes, integrals, hole_integrals, tile_mask, occupied_energy, virtual_energy):
    swap = [(0, 1), (1, 0)]
    gathered = lax.all_gather(amplitudes, "row", axis=0, tiled=True)
    a, ap = amplitudes, lax.ppermute(amplitudes, "layer", swap)
    first, second = pack("pack_far_near", tile_mask, integrals, [(*FAR, False), (*NEAR, False)])
    v1 = lax.ppermute(first, "layer", swap)
    v2 = lax.ppermute(second, "layer", swap)
    own_v, third = pack("pack_own_home", tile_mask, integrals, [(*ALL, True), (*HOME, False)], [first])
    v3 = lax.ppermute(third, "layer", swap)

    up, down = far(a, ap, own_v, v1)
    far_up, far_down = send(up, True, 1), send(down, True, -1)
    up, down, up_st, down_st = near(a, ap, own_v, v2)
    near_down, near_up = send(up, True, 1), send(down, True, -1)
    up = relay(far_up, up_st)
    far_up = send(up, True, 1)
    down = relay(far_down, down_st)
    far_down = send(down, True, -1)
    st = home(a, ap, own_v, v3, near_up, near_down)
    own, m1, m2, m3 = turn(st, far_up, far_down)
    got = send(m2, False, 2), send(m1, False, 1), send(m3, False, -1)
    holes = hole_sum(hole_integrals, gathered)
    return finish(own, got, holes, occupied_energy, virtual_energy)


def solution(mesh):
    return jax.shard_map(
        shards,
        mesh=mesh,
        in_specs=(
            P("row", ("col", "layer")),
            P(("col", "layer"), None),
            P("row", None),
            P(),
            P("row"),
            P(("col", "layer")),
        ),
        out_specs=P("row", ("col", "layer")),
        check_vma=False,
    )
```

time: 210 us -> 76.6 us (0.36)
  waiting for transfers between devices: 151 us -> 23.9 us
  matrix products: 28.3 us -> 0 us
  Pallas kernels: 0 us -> 23.8 us
  starting transfers between devices: 0.05 us -> 15.1 us
  local copies, waits for them, and re-layouts: 13.2 us -> 0.02 us
    reduce_scatter x1 -> x0, waiting for transfers between devices: 137 us -> none  [shards(): lax.psum_scatter(lax.dot_general(masked, amplitudes, (((0,), (1,)), ((),...]
    dot_general x2 -> x0, matrix products: 28.3 us -> none  [the longest x1 23.2 us: shards(): lax.dot_general(masked, amplitudes, (((0,), (1,)), ((), ())), preferred_e...]
    pallas_call x0 -> x10, Pallas kernels: none -> 23.8 us  [the longest x2 6.79 us: pack(): pl.pallas_call(body, out_shape=[pltpu.VMEM((n, width, width), BF16) for _...]
    ppermute x0 -> x13, waiting for transfers between devices: none -> 23.1 us  [the longest x9 20.8 us: send(): return lax.ppermute(value, ('col', 'layer'), hop(first, d))]
    ppermute x0 -> x13, starting transfers between devices: none -> 15.1 us  [the longest x9 14.4 us: send(): return lax.ppermute(value, ('col', 'layer'), hop(first, d))]
    all_gather x1, waiting for transfers between devices: 13.8 us -> 0.01 us  [shards(): gathered = lax.all_gather(amplitudes, 'row', axis=0, tiled=True)]
    broadcast_in_dim x2 -> x1, local copies, waits for them, and re-layouts: 12 us -> 0.01 us  [finish(): virtual[None, :]]
  transfers between devices with their start and end apart: 2 -> 14, of which waited for: 2 -> 8; matrix products, arithmetic and copies ran while one was open for 17% -> 0% of each run, Pallas kernels for 0% -> 29%
where the time goes in v2:
time: 76.6 us; the launch traced here: 76.3 us
  waiting for transfers between devices  23.9 us (31%)
  Pallas kernels  23.8 us (31%)
  starting transfers between devices  15.1 us (20%)
  between operations  13.5 us (18%)
    ppermute x9, waiting for transfers between devices, send(): return lax.ppermute(value, ('col', 'layer'), hop(first, d))  20.8 us
    ppermute x9, starting transfers between devices, send(): return lax.ppermute(value, ('col', 'layer'), hop(first, d))  14.4 us
    pallas_call x2, Pallas kernels, pack(): pl.pallas_call(body, out_shape=[pltpu.VMEM((n, width, width), BF16) for _...  6.79 us
    pallas_call x1, Pallas kernels, near(): pl.pallas_call(body, out_shape=[pltpu.VMEM((msg, width), I16)] * 2 + [plt...  4.07 us
    pallas_call x1, Pallas kernels, hole_sum(): pl.pallas_call(body, out_shape=pltpu.VMEM((rows, width), F32), in_specs=[...  4.01 us
    pallas_call x1, Pallas kernels, far(): pl.pallas_call(body, out_shape=[pltpu.VMEM((msg, width), I16)] * 2, in_sp...  2.73 us
    pallas_call x1, Pallas kernels, home(): pl.pallas_call(body, out_shape=pltpu.VMEM((4, rows, width), F32), in_spec...  2.4 us
    ppermute x1, waiting for transfers between devices, shards(): a, ap = (amplitudes, lax.ppermute(amplitudes, 'layer', swap))  2.37 us
  transfers between devices with their start and end apart: 14, of which 8 were waited for; matrix products, arithmetic and copies ran while one was open for 0% of the time, Pallas kernels for 29%

profile of v2, /device:TPU:8, one launch (start us, length us, event | category | flops | bytes accessed | tf_op | source)
XLA Modules:
  0.0 76.3 jit_solution(3456048760774718257)
XLA Ops:
  6.5 0.0 all-gather.2.cloned.1.call-start
  6.5 0.7 all-gather.2.cloned.1.call-update
  7.3 0.0 copy-start
  7.3 3.0 %pack_far_near.1 = (bf16[4,384,384]{2,1,0:T(8,128)(2,1)S(1)}, bf16[8,384,384]{2,1,0:T(8,128)(2,1)S(1)}) custom-call(s32[96,96]{1,0:T(8,128)} %mask_ref.3, bf16[384,12288]{1,0:T(8,128)(2,1)} %v_ref.3), custom_call_target="tpu_custom_call" | custom-call | bytes 7077 | tf_op jit(solution)/shard_map/pack_far_near/pallas_call | solution.py:131
  10.3 0.1 collective-permute-start.2
  10.4 0.5 collective-permute-start.5
  10.9 0.0 copy-done
  10.9 0.1 collective-permute-start
  11.0 3.8 %pack_own_home.1 = (bf16[16,384,384]{2,1,0:T(8,128)(2,1)S(1)}, bf16[4,384,384]{2,1,0:T(8,128)(2,1)S(1)}) custom-call(s32[96,96]{1,0:T(8,128)} %mask_ref.3, bf16[384,12288]{1,0:T(8,128)(2,1)} %v_ref.3, bf16[4,384,384]{2,1,0:T(8,128)(2,1)S(1)} %get-tuple-element.19.refs_0_), custom_call_target="tpu_custom_call" | custom-call | bytes 11796 | tf_op jit(solution)/shard_map/pack_own_home/pallas_call | solution.py:131
  14.8 2.4 %collective-permute-done.ap_ref = bf16[512,384]{1,0:T(8,128)(2,1)S(1)} collective-permute-done((bf16[512,384]{1,0:T(8,128)(2,1)S(1)}, bf16[512,384]{1,0:T(8,128)(2,1)S(1)}, u32[]{:S(2)}, u32[]{:S(2)}) %collective-permute-start) | collective-permute-done | bytes 393248 | tf_op jit(solution)/shard_map/ppermute | solution.py:344
  17.1 0.0 collective-permute-done.5.v1_ref
  17.1 2.7 %far.1 = (s16[1040,384]{1,0:T(8,128)(2,1)S(1)}, s16[1040,384]{1,0:T(8,128)(2,1)S(1)}) custom-call(bf16[512,384]{1,0:T(8,128)(2,1)S(1)} %copy-done, bf16[512,384]{1,0:T(8,128)(2,1)S(1)} %collective-permute-done.ap_ref, bf16[16,384,384]{2,1,0:T(8,128)(2,1)S(1)} %get-tuple-element.20.own_ref, bf16[4,384,384]{2,1,0:T(8,128)(2,1)S(1)} %collective-permute-done.5.v1_ref), custom_call_target="tpu_custom_call" | custom-call | flops 1207959 | bytes 2359 | tf_op jit(solution)/shard_map/far/pallas_call | solution.py:167
  19.9 2.8 %collective-permute-start.8 = (s16[1040,384]{1,0:T(8,128)(2,1)S(1)}, s16[1040,384]{1,0:T(8,128)(2,1)S(1)}, u32[]{:S(2)}, u32[]{:S(2)}) collective-permute-start(s16[1040,384]{1,0:T(8,128)(2,1)S(1)} %get-tuple-element.27), channel_id=1, source_target_pairs={{0,6},{1,25},{2,0},{3,27},{4,2},{5,29},{6,4},{7,31},{8,14},{9,1},{... | collective-permute-start | bytes 2396168 | tf_op jit(solution)/shard_map/ppermute | solution.py:38
  22.7 0.0 collective-permute-start.6
  22.7 0.0 collective-permute-start.1
  22.7 0.0 collective-permute-done.2.v2_ref
  22.7 4.1 %near.1 = (s16[1040,384]{1,0:T(8,128)(2,1)S(1)}, s16[1040,384]{1,0:T(8,128)(2,1)S(1)}, f32[1024,384]{1,0:T(8,128)S(1)}, f32[1024,384]{1,0:T(8,128)S(1)}) custom-call(bf16[512,384]{1,0:T(8,128)(2,1)S(1)} %copy-done, bf16[512,384]{1,0:T(8,128)(2,1)S(1)} %collective-permute-done.ap_ref, bf16[16,384,384]{2,1,0:T(8,128)(2,1)S(1)} %get-tuple-element.20.own_ref, ...), custom_call_target="tpu_custom_call" | custom-call | flops 2415919 | bytes 4718 | tf_op jit(solution)/shard_map/near/pallas_call | solution.py:198
  26.8 3.3 %collective-permute-start.3 = (s16[1040,384]{1,0:T(8,128)(2,1)S(1)}, s16[1040,384]{1,0:T(8,128)(2,1)S(1)}, u32[]{:S(2)}, u32[]{:S(2)}) collective-permute-start(s16[1040,384]{1,0:T(8,128)(2,1)S(1)} %get-tuple-element.23), channel_id=1, source_target_pairs={{0,6},{1,25},{2,0},{3,27},{4,2},{5,29},{6,4},{7,31},{8,14},{9,1},{... | collective-permute-start | bytes 2396168 | tf_op jit(solution)/shard_map/ppermute | solution.py:38
  30.1 0.0 collective-permute-start.4
  30.1 2.2 %collective-permute-done.8.got_ref = s16[1040,384]{1,0:T(8,128)(2,1)S(1)} collective-permute-done((s16[1040,384]{1,0:T(8,128)(2,1)S(1)}, s16[1040,384]{1,0:T(8,128)(2,1)S(1)}, u32[]{:S(2)}, u32[]{:S(2)}) %collective-permute-start.8) | collective-permute-done | bytes 798752 | tf_op jit(solution)/shard_map/ppermute | solution.py:38
  32.4 0.8 relay.3
  33.1 3.8 %collective-permute-start.9 = (s16[1040,384]{1,0:T(8,128)(2,1)S(1)}, s16[1040,384]{1,0:T(8,128)(2,1)S(1)}, u32[]{:S(2)}, u32[]{:S(2)}) collective-permute-start(s16[1040,384]{1,0:T(8,128)(2,1)S(1)} %relay.3), channel_id=1, source_target_pairs={{0,6},{1,25},{2,0},{3,27},{4,2},{5,29},{6,4},{7,31},{8,14},{9,1},{... | collective-permute-start | bytes 2396168 | tf_op jit(solution)/shard_map/ppermute | solution.py:38
  36.9 0.0 collective-permute-done.6.got_ref
  36.9 0.8 %relay.2 = s16[1040,384]{1,0:T(8,128)(2,1)S(1)} custom-call(s16[1040,384]{1,0:T(8,128)(2,1)S(1)} %collective-permute-done.6.got_ref, f32[1024,384]{1,0:T(8,128)S(1)} %get-tuple-element.26.own_ref), custom_call_target="tpu_custom_call" | custom-call | bytes 3145 | tf_op jit(solution)/shard_map/relay/pallas_call | solution.py:243
  37.7 0.1 collective-permute-start.7
  37.8 0.0 collective-permute-done.1.v2_ref
  37.8 3.1 %collective-permute-done.3.up_ref = s16[1040,384]{1,0:T(8,128)(2,1)S(1)} collective-permute-done((s16[1040,384]{1,0:T(8,128)(2,1)S(1)}, s16[1040,384]{1,0:T(8,128)(2,1)S(1)}, u32[]{:S(2)}, u32[]{:S(2)}) %collective-permute-start.3) | collective-permute-done | bytes 798752 | tf_op jit(solution)/shard_map/ppermute | solution.py:38
  40.9 3.7 %collective-permute-done.4.down_ref = s16[1040,384]{1,0:T(8,128)(2,1)S(1)} collective-permute-done((s16[1040,384]{1,0:T(8,128)(2,1)S(1)}, s16[1040,384]{1,0:T(8,128)(2,1)S(1)}, u32[]{:S(2)}, u32[]{:S(2)}) %collective-permute-start.4) | collective-permute-done | bytes 798752 | tf_op jit(solution)/shard_map/ppermute | solution.py:38
  44.6 2.4 %home.1.st_ref = f32[4,512,384]{2,1,0:T(8,128)S(1)} custom-call(bf16[512,384]{1,0:T(8,128)(2,1)S(1)} %copy-done, bf16[512,384]{1,0:T(8,128)(2,1)S(1)} %collective-permute-done.ap_ref, bf16[16,384,384]{2,1,0:T(8,128)(2,1)S(1)} %get-tuple-element.20.own_ref, bf16[4,384,384]{2,1,0:T(8,128)(2,1)S(1)} %collective-permute-done.1.v2_ref, ...), custom_call_target="tpu_custom_call" | custom-call | flops 1207959 | bytes 2359 | tf_op jit(solution)/shard_map/home/pallas_call | solution.py:224
  47.0 0.0 copy-start.2
  47.0 2.4 %collective-permute-done.9.down_ref = s16[1040,384]{1,0:T(8,128)(2,1)S(1)} collective-permute-done((s16[1040,384]{1,0:T(8,128)(2,1)S(1)}, s16[1040,384]{1,0:T(8,128)(2,1)S(1)}, u32[]{:S(2)}, u32[]{:S(2)}) %collective-permute-start.9) | collective-permute-done | bytes 798752 | tf_op jit(solution)/shard_map/ppermute | solution.py:38
  49.5 3.7 %collective-permute-done.7.up_ref = s16[1040,384]{1,0:T(8,128)(2,1)S(1)} collective-permute-done((s16[1040,384]{1,0:T(8,128)(2,1)S(1)}, s16[1040,384]{1,0:T(8,128)(2,1)S(1)}, u32[]{:S(2)}, u32[]{:S(2)}) %collective-permute-start.7) | collective-permute-done | bytes 798752 | tf_op jit(solution)/shard_map/ppermute | solution.py:38
  53.2 0.9 %turn.1 = (f32[512,384]{1,0:T(8,128)S(1)}, s16[528,384]{1,0:T(8,128)(2,1)S(1)}, s16[528,384]{1,0:T(8,128)(2,1)S(1)}, s16[528,384]{1,0:T(8,128)(2,1)S(1)}) custom-call(f32[4,512,384]{2,1,0:T(8,128)S(1)} %home.1.st_ref, s16[1040,384]{1,0:T(8,128)(2,1)S(1)} %collective-permute-done.7.up_ref, s16[1040,384]{1,0:T(8,128)(2,1)S(1)} %collective-permute-done.9.down_ref), custom_call_target="tpu_custom_call" | custom-call | bytes 7864 | tf_op jit(solution)/shard_map/turn/pallas_call | solution.py:268
  54.1 2.4 %collective-permute-start.10 = (s16[528,384]{1,0:T(8,128)(2,1)S(1)}, s16[528,384]{1,0:T(8,128)(2,1)S(1)}, u32[]{:S(2)}, u32[]{:S(2)}) collective-permute-start(s16[528,384]{1,0:T(8,128)(2,1)S(1)} %get-tuple-element.30), channel_id=1, source_target_pairs={{0,16},{1,5},{2,18},{3,7},{4,20},{5,1},{6,22},{7,3},{8,24},{9,13},... | collective-permute-start | bytes 1216520 | tf_op jit(solution)/shard_map/ppermute | solution.py:38
  56.5 0.0 collective-permute-start.11
  56.5 2.0 %collective-permute-start.12 = (s16[528,384]{1,0:T(8,128)(2,1)S(1)}, s16[528,384]{1,0:T(8,128)(2,1)S(1)}, u32[]{:S(2)}, u32[]{:S(2)}) collective-permute-start(s16[528,384]{1,0:T(8,128)(2,1)S(1)} %get-tuple-element.32), channel_id=1, source_target_pairs={{0,24},{1,7},{2,26},{3,1},{4,28},{5,3},{6,30},{7,5},{8,0},{9,15},{... | collective-permute-start | bytes 1216520 | tf_op jit(solution)/shard_map/ppermute | solution.py:38
  58.5 0.0 copy-done.2
  58.5 0.0 copy-start.1
  58.5 0.0 all-gather.2.cloned.1.call-done.a_hbm
  58.5 4.0 %holes.1.holes_ref = f32[512,384]{1,0:T(8,128)S(1)} custom-call(bf16[512,4096]{1,0:T(8,128)(2,1)} %h_hbm.1, bf16[4096,384]{1,0:T(8,128)(2,1)} %all-gather.2.cloned.1.call-done.a_hbm), custom_call_target="tpu_custom_call" | custom-call | flops 1610612 | bytes 7340 | tf_op jit(solution)/shard_map/holes/pallas_call | solution.py:302
  62.5 1.1 %collective-permute-done.10.m1 = s16[528,384]{1,0:T(8,128)(2,1)S(1)} collective-permute-done((s16[528,384]{1,0:T(8,128)(2,1)S(1)}, s16[528,384]{1,0:T(8,128)(2,1)S(1)}, u32[]{:S(2)}, u32[]{:S(2)}) %collective-permute-start.10) | collective-permute-done | bytes 405536 | tf_op jit(solution)/shard_map/ppermute | solution.py:38
  63.7 4.4 %collective-permute-done.11.m2 = s16[528,384]{1,0:T(8,128)(2,1)S(1)} collective-permute-done((s16[528,384]{1,0:T(8,128)(2,1)S(1)}, s16[528,384]{1,0:T(8,128)(2,1)S(1)}, u32[]{:S(2)}, u32[]{:S(2)}) %collective-permute-start.11) | collective-permute-done | bytes 405536 | tf_op jit(solution)/shard_map/ppermute | solution.py:38
  68.1 0.0 collective-permute-done.12.m3
  68.1 0.0 copy-done.1
  68.1 1.4 %finish.1 = f32[512,384]{1,0:T(8,128)} custom-call(f32[512,384]{1,0:T(8,128)S(1)} %get-tuple-element.29.own_ref, s16[528,384]{1,0:T(8,128)(2,1)S(1)} %collective-permute-done.10.m1, s16[528,384]{1,0:T(8,128)(2,1)S(1)} %collective-permute-done.11.m2, s16[528,384]{1,0:T(8,128)(2,1)S(1)} %collective-permute-done.12.m3, f32[512,384]{1,0:T(8,128)S(1)} %holes.1.holes_ref, ...), custom_call_target="tpu_custom_call" | custom-call | bytes 4718 | tf_op jit(solution)/shard_map/finish/pallas_call | solution.py:330
  (1 shorter events, 0.0 us)
Async XLA Ops:
  6.5 52.0 %all-gather.2.cloned.1.call-start = ((), (), s32[]{:S(2)}) async-start(), calls=%async_computation | async-start | bytes 3538944 | tf_op jit(solution)/shard_map/all_gather | solution.py:343
  7.3 3.6 %copy-start = (bf16[512,384]{1,0:T(8,128)(2,1)S(1)}, bf16[512,384]{1,0:T(8,128)(2,1)}, u32[]{:S(2)}) copy-start(bf16[512,384]{1,0:T(8,128)(2,1)} %a_ref.5) | copy-start | bytes 1179652
  10.3 12.5 %collective-permute-start.2 = (bf16[8,384,384]{2,1,0:T(8,128)(2,1)S(1)}, bf16[8,384,384]{2,1,0:T(8,128)(2,1)S(1)}, u32[]{:S(2)}, u32[]{:S(2)}) collective-permute-start(bf16[8,384,384]{2,1,0:T(8,128)(2,1)S(1)} %get-tuple-element.22), channel_id=1, source_target_pairs={{0,1},{1,0},{2,3},{3,2},{4,5},{5,4},{6,7},{7,6},{8,9},{9,8},{10,11... | collective-permute-start | bytes 7077896 | tf_op jit(solution)/shard_map/ppermute | solution.py:347
  10.4 6.8 %collective-permute-start.5 = (bf16[4,384,384]{2,1,0:T(8,128)(2,1)S(1)}, bf16[4,384,384]{2,1,0:T(8,128)(2,1)S(1)}, u32[]{:S(2)}, u32[]{:S(2)}) collective-permute-start(bf16[4,384,384]{2,1,0:T(8,128)(2,1)S(1)} %get-tuple-element.19.refs_0_), channel_id=1, source_target_pairs={{0,1},{1,0},{2,3},{3,2},{4,5},{5,4},{6,7},{7,6},{8,9},{9,8},{10,11... | collective-permute-start | bytes 3538952 | tf_op jit(solution)/shard_map/ppermute | solution.py:346
  10.9 6.3 %collective-permute-start = (bf16[512,384]{1,0:T(8,128)(2,1)S(1)}, bf16[512,384]{1,0:T(8,128)(2,1)S(1)}, u32[]{:S(2)}, u32[]{:S(2)}) collective-permute-start(bf16[512,384]{1,0:T(8,128)(2,1)S(1)} %copy-done), channel_id=1, source_target_pairs={{0,1},{1,0},{2,3},{3,2},{4,5},{5,4},{6,7},{7,6},{8,9},{9,8},{10,11... | collective-permute-start | bytes 1179656 | tf_op jit(solution)/shard_map/ppermute | solution.py:344
  19.9 12.5 %collective-permute-start.8 = (s16[1040,384]{1,0:T(8,128)(2,1)S(1)}, s16[1040,384]{1,0:T(8,128)(2,1)S(1)}, u32[]{:S(2)}, u32[]{:S(2)}) collective-permute-start(s16[1040,384]{1,0:T(8,128)(2,1)S(1)} %get-tuple-element.27), channel_id=1, source_target_pairs={{0,6},{1,25},{2,0},{3,27},{4,2},{5,29},{6,4},{7,31},{8,14},{9,1},{... | collective-permute-start | bytes 2396168 | tf_op jit(solution)/shard_map/ppermute | solution.py:38
  22.7 14.2 %collective-permute-start.6 = (s16[1040,384]{1,0:T(8,128)(2,1)S(1)}, s16[1040,384]{1,0:T(8,128)(2,1)S(1)}, u32[]{:S(2)}, u32[]{:S(2)}) collective-permute-start(s16[1040,384]{1,0:T(8,128)(2,1)S(1)} %get-tuple-element.25), channel_id=1, source_target_pairs={{0,2},{1,9},{2,4},{3,11},{4,6},{5,13},{6,0},{7,15},{8,10},{9,17},{... | collective-permute-start | bytes 2396168 | tf_op jit(solution)/shard_map/ppermute | solution.py:38
  22.7 15.0 %collective-permute-start.1 = (bf16[4,384,384]{2,1,0:T(8,128)(2,1)S(1)}, bf16[4,384,384]{2,1,0:T(8,128)(2,1)S(1)}, u32[]{:S(2)}, u32[]{:S(2)}) collective-permute-start(bf16[4,384,384]{2,1,0:T(8,128)(2,1)S(1)} %get-tuple-element.21), channel_id=1, source_target_pairs={{0,1},{1,0},{2,3},{3,2},{4,5},{5,4},{6,7},{7,6},{8,9},{9,8},{10,11... | collective-permute-start | bytes 3538952 | tf_op jit(solution)/shard_map/ppermute | solution.py:349
  26.8 14.1 %collective-permute-start.3 = (s16[1040,384]{1,0:T(8,128)(2,1)S(1)}, s16[1040,384]{1,0:T(8,128)(2,1)S(1)}, u32[]{:S(2)}, u32[]{:S(2)}) collective-permute-start(s16[1040,384]{1,0:T(8,128)(2,1)S(1)} %get-tuple-element.23), channel_id=1, source_target_pairs={{0,6},{1,25},{2,0},{3,27},{4,2},{5,29},{6,4},{7,31},{8,14},{9,1},{... | collective-permute-start | bytes 2396168 | tf_op jit(solution)/shard_map/ppermute | solution.py:38
  30.1 14.5 %collective-permute-start.4 = (s16[1040,384]{1,0:T(8,128)(2,1)S(1)}, s16[1040,384]{1,0:T(8,128)(2,1)S(1)}, u32[]{:S(2)}, u32[]{:S(2)}) collective-permute-start(s16[1040,384]{1,0:T(8,128)(2,1)S(1)} %get-tuple-element.24), channel_id=1, source_target_pairs={{0,2},{1,9},{2,4},{3,11},{4,6},{5,13},{6,0},{7,15},{8,10},{9,17},{... | collective-permute-start | bytes 2396168 | tf_op jit(solution)/shard_map/ppermute | solution.py:38
  33.1 16.4 %collective-permute-start.9 = (s16[1040,384]{1,0:T(8,128)(2,1)S(1)}, s16[1040,384]{1,0:T(8,128)(2,1)S(1)}, u32[]{:S(2)}, u32[]{:S(2)}) collective-permute-start(s16[1040,384]{1,0:T(8,128)(2,1)S(1)} %relay.3), channel_id=1, source_target_pairs={{0,6},{1,25},{2,0},{3,27},{4,2},{5,29},{6,4},{7,31},{8,14},{9,1},{... | collective-permute-start | bytes 2396168 | tf_op jit(solution)/shard_map/ppermute | solution.py:38
  37.7 15.5 %collective-permute-start.7 = (s16[1040,384]{1,0:T(8,128)(2,1)S(1)}, s16[1040,384]{1,0:T(8,128)(2,1)S(1)}, u32[]{:S(2)}, u32[]{:S(2)}) collective-permute-start(s16[1040,384]{1,0:T(8,128)(2,1)S(1)} %relay.2), channel_id=1, source_target_pairs={{0,2},{1,9},{2,4},{3,11},{4,6},{5,13},{6,0},{7,15},{8,10},{9,17},{... | collective-permute-start | bytes 2396168 | tf_op jit(solution)/shard_map/ppermute | solution.py:38
  47.0 11.5 %copy-start.2 = (f32[384]{0:T(512)S(1)}, f32[384]{0:T(512)}, u32[]{:S(2)}) copy-start(f32[384]{0:T(512)} %param.11) | copy-start | bytes 4612
  54.1 9.6 %collective-permute-start.10 = (s16[528,384]{1,0:T(8,128)(2,1)S(1)}, s16[528,384]{1,0:T(8,128)(2,1)S(1)}, u32[]{:S(2)}, u32[]{:S(2)}) collective-permute-start(s16[528,384]{1,0:T(8,128)(2,1)S(1)} %get-tuple-element.30), channel_id=1, source_target_pairs={{0,16},{1,5},{2,18},{3,7},{4,20},{5,1},{6,22},{7,3},{8,24},{9,13},... | collective-permute-start | bytes 1216520 | tf_op jit(solution)/shard_map/ppermute | solution.py:38
  56.5 11.6 %collective-permute-start.11 = (s16[528,384]{1,0:T(8,128)(2,1)S(1)}, s16[528,384]{1,0:T(8,128)(2,1)S(1)}, u32[]{:S(2)}, u32[]{:S(2)}) collective-permute-start(s16[528,384]{1,0:T(8,128)(2,1)S(1)} %get-tuple-element.31), channel_id=1, source_target_pairs={{0,8},{1,3},{2,10},{3,5},{4,12},{5,7},{6,14},{7,1},{8,16},{9,11},{... | collective-permute-start | bytes 1216520 | tf_op jit(solution)/shard_map/ppermute | solution.py:38
  56.5 11.6 %collective-permute-start.12 = (s16[528,384]{1,0:T(8,128)(2,1)S(1)}, s16[528,384]{1,0:T(8,128)(2,1)S(1)}, u32[]{:S(2)}, u32[]{:S(2)}) collective-permute-start(s16[528,384]{1,0:T(8,128)(2,1)S(1)} %get-tuple-element.32), channel_id=1, source_target_pairs={{0,24},{1,7},{2,26},{3,1},{4,28},{5,3},{6,30},{7,5},{8,0},{9,15},{... | collective-permute-start | bytes 1216520 | tf_op jit(solution)/shard_map/ppermute | solution.py:38
  58.5 9.6 %copy-start.1 = (f32[512]{0:T(512)S(1)}, f32[512]{0:T(512)}, u32[]{:S(2)}) copy-start(f32[512]{0:T(512)} %param.10) | copy-start | bytes 6148
Sparse Core Ops, SparseCore 0:
  9.1 47.8 all-gather.1

commit v3 on v2

--- a/solution.py
+++ b/solution.py
@@ -20,7 +20,7 @@
 VM = pl.BlockSpec(memory_space=pltpu.VMEM)
 ANY = pl.BlockSpec(memory_space=pl.ANY)
 
-FAR, NEAR, HOME, ALL = (0, 4), (4, 8), (12, 4), (0, 16)
+FAR, REST, ALL = (0, 4), (4, 12), (0, 16)
 
 
 def hop(first, d):
@@ -38,6 +38,29 @@
     return lax.ppermute(value, ("col", "layer"), hop(first, d))
 
 
+def run(body, after, operands, in_specs, out_shape, out_specs, carry=(), **kw):
+    n, m, c = len(operands), len(after), len(carry)
+    single = not isinstance(out_shape, list)
+    shapes, specs = ([out_shape], [out_specs]) if single else (out_shape, out_specs)
+    k = len(shapes)
+
+    def whole(*refs):
+        ins, outs = refs[:n + c + m], refs[n + c + m:]
+        for i in range(c):
+            outs[k + i][...] = ins[n + i][...]
+        body(*ins[:n], *outs[:k], *outs[k + c:])
+
+    out = pl.pallas_call(
+        whole,
+        in_specs=list(in_specs) + [VM] * c + [ANY] * m,
+        out_shape=list(shapes) + [pltpu.VMEM(v.shape, v.dtype) for v in carry],
+        out_specs=list(specs) + [VM] * c,
+        compiler_params=params(),
+        **kw,
+    )(*operands, *map(inside, carry), *after)
+    return out[0] if single and not c else out
+
+
 def inside(value):
     return pltpu.with_memory_space_constraint(value, pltpu.VMEM)
 
@@ -48,6 +71,9 @@
 
 def cost(flops, moved):
     return pl.CostEstimate(flops=int(flops) // SCALE, bytes_accessed=int(moved) // SCALE, transcendentals=0)
+
+
+LONG = cost(10 ** 14, 0)
 
 
 def loop(n, unroll=1):
@@ -148,7 +174,11 @@
     return jnp.concatenate([a_ref[...], ap_ref[...]], axis=1)
 
 
-def far(a, ap, own_v, v1):
+def hand_on(blocks, after, estimate=cost(0, 0)):
+    return run(lambda: None, after, [], [], [], [], blocks, cost_estimate=estimate, name="hand_on")
+
+
+def far(a, ap, own_v, v1, after=(), carry=()):
     rows, width = a.shape
     half = rows // 2
     n = half // TB
@@ -164,18 +194,20 @@
                 put(up_ref, o * n + b, part[b * TB:(b + 1) * TB])
                 put(down_ref, o * n + b, part[half + b * TB:half + (b + 1) * TB])
 
-    return pl.pallas_call(
-        body,
+    return run(
+        body,
+        after,
+        [*map(inside, (a, ap, own_v, v1))],
+        [VM] * 4,
         out_shape=[pltpu.VMEM((msg, width), I16)] * 2,
-        in_specs=[VM] * 4,
         out_specs=[VM] * 2,
-        compiler_params=params(),
         cost_estimate=cost(2 * 4 * rows * 2 * width * width, 4 * 4 * width * width),
+        carry=carry,
         name="far",
-    )(*map(inside, (a, ap, own_v, v1)))
-
-
-def near(a, ap, own_v, v2):
+    )
+
+
+def near(a, ap, own_v, v2, after=(), carry=()):
     rows, width = a.shape
     half = rows // 2
     n = half // TB
@@ -195,18 +227,20 @@
             for b in range(n):
                 put(down_ref, o * n + b, part[b * TB:(b + 1) * TB])
 
-    return pl.pallas_call(
-        body,
+    return run(
+        body,
+        after,
+        [*map(inside, (a, ap, own_v, v2))],
+        [VM] * 4,
         out_shape=[pltpu.VMEM((msg, width), I16)] * 2 + [pltpu.VMEM((4 * half, width), F32)] * 2,
-        in_specs=[VM] * 4,
         out_specs=[VM] * 4,
-        compiler_params=params(),
-        cost_estimate=cost(2 * 8 * rows * 2 * width * width, 8 * 4 * width * width),
+        cost_estimate=LONG,
+        carry=carry,
         name="near",
-    )(*map(inside, (a, ap, own_v, v2)))
-
-
-def home(a, ap, own_v, v2, near_up, near_down):
+    )
+
+
+def home(a, ap, own_v, v2, near_up, near_down, after=(), carry=()):
     rows, width = a.shape
     n = rows // TB
     h = n // 2
@@ -216,23 +250,25 @@
 
         @loop(4)
         def _(o):
-            part = product(lhs, own_ref, 12 + o, v2_ref, o)
+            part = product(lhs, own_ref, 12 + o, v2_ref, 8 + o)
             for b in range(n):
                 here = slice(b * TB, (b + 1) * TB)
                 out_ref[o, here, :] = part[here] + get(up_ref if b < h else down_ref, o * h + b % h)
 
-    return pl.pallas_call(
-        body,
+    return run(
+        body,
+        after,
+        [*map(inside, (a, ap, own_v, v2, near_up, near_down))],
+        [VM] * 6,
         out_shape=pltpu.VMEM((4, rows, width), F32),
-        in_specs=[VM] * 6,
         out_specs=VM,
-        compiler_params=params(),
-        cost_estimate=cost(2 * 4 * rows * 2 * width * width, 4 * 4 * width * width),
+        cost_estimate=LONG,
+        carry=carry,
         name="home",
-    )(*map(inside, (a, ap, own_v, v2, near_up, near_down)))
-
-
-def relay(got, own):
+    )
+
+
+def relay(got, own, after=(), carry=()):
     rows, width = own.shape
 
     def body(got_ref, own_ref, out_ref):
@@ -240,18 +276,20 @@
         def _(k):
             put(out_ref, k, own_ref[rows_at(k, TB), :] + get(got_ref, k))
 
-    return pl.pallas_call(
-        body,
+    return run(
+        body,
+        after,
+        [*map(inside, (got, own))],
+        [VM] * 2,
         out_shape=pltpu.VMEM(got.shape, I16),
-        in_specs=[VM] * 2,
         out_specs=VM,
-        compiler_params=params(),
         cost_estimate=cost(0, 8 * rows * width),
+        carry=carry,
         name="relay",
-    )(*map(inside, (got, own)))
-
-
-def turn(st, far_up, far_down):
+    )
+
+
+def turn(st, far_up, far_down, after=(), carry=()):
     _, rows, width = st.shape
     n = rows // TB
     h = n // 2
@@ -265,54 +303,45 @@
                 else:
                     put(ref, b, part)
 
-    return pl.pallas_call(
-        body,
+    return run(
+        body,
+        after,
+        [*map(inside, (st, far_up, far_down))],
+        [VM] * 3,
         out_shape=[pltpu.VMEM((rows, width), F32)] + [pltpu.VMEM((rows + 16, width), I16)] * 3,
-        in_specs=[VM] * 3,
         out_specs=[VM] * 4,
-        compiler_params=params(),
         cost_estimate=cost(0, 4 * rows * width * 10),
+        carry=carry,
         name="turn",
-    )(*map(inside, (st, far_up, far_down)))
-
-
-def hole_sum(hole_integrals, gathered):
-    rows, depth = hole_integrals.shape
-    width = gathered.shape[1]
-    parts = 8
-    step = depth // parts
-
-    def body(h_hbm, a_hbm, out_ref, h_ref, a_ref, sem):
-        copies = []
-        for i in range(parts):
-            here = slice(i * step, (i + 1) * step)
-            pair = (
-                pltpu.make_async_copy(h_hbm.at[:, here], h_ref.at[i], sem.at[0, i]),
-                pltpu.make_async_copy(a_hbm.at[here, :], a_ref.at[i], sem.at[1, i]),
-            )
-            for copy in pair:
-                copy.start()
-            copies.append(pair)
-        for i in range(parts):
-            for copy in copies[i]:
-                copy.wait()
-            part = jnp.dot(h_ref[i], a_ref[i], preferred_element_type=F32)
-            out_ref[...] = part if i == 0 else out_ref[...] + part
-
-    return pl.pallas_call(
-        body,
+    )
+
+
+def hole_part(name, hole_integrals, blocks, away, before=None, after=()):
+    rows = hole_integrals.shape[0]
+    depth, width = blocks[0].shape
+    count = hole_integrals.shape[1] // depth
+    more = [] if before is None else [before]
+
+    def body(h_ref, *refs):
+        out_ref = refs[-1]
+        here = lax.axis_index("row")
+        total = refs[len(blocks)][...] if more else None
+        for ref, k in zip(refs, away):
+            at = lax.rem(here + (k + count), count)
+            part = jnp.dot(h_ref[:, rows_at(at, depth)], ref[...], preferred_element_type=F32)
+            total = part if total is None else total + part
+        out_ref[...] = total
+
+    return run(
+        body,
+        after,
+        [*map(inside, (hole_integrals, *blocks, *more))],
+        [VM] * (1 + len(blocks) + len(more)),
         out_shape=pltpu.VMEM((rows, width), F32),
-        in_specs=[ANY] * 2,
         out_specs=VM,
-        scratch_shapes=[
-            pltpu.VMEM((parts, rows, step), BF16),
-            pltpu.VMEM((parts, step, width), BF16),
-            pltpu.SemaphoreType.DMA((2, parts)),
-        ],
-        compiler_params=params(),
-        cost_estimate=cost(2 * rows * depth * width, 2 * depth * (rows + width)),
-        name="holes",
-    )(*(pltpu.with_memory_space_constraint(v, pltpu.HBM) for v in (hole_integrals, gathered)))
+        cost_estimate=LONG,
+        name=name,
+    )
 
 
 def finish(own, got, holes, occupied, virtual):
@@ -340,26 +369,40 @@
 
 def shards(amplitudes, integrals, hole_integrals, tile_mask, occupied_energy, virtual_energy):
     swap = [(0, 1), (1, 0)]
-    gathered = lax.all_gather(amplitudes, "row", axis=0, tiled=True)
-    a, ap = amplitudes, lax.ppermute(amplitudes, "layer", swap)
-    first, second = pack("pack_far_near", tile_mask, integrals, [(*FAR, False), (*NEAR, False)])
+    z = lax.axis_size("row")
+    a = amplitudes
+
+    def ring(value, d):
+        return lax.ppermute(value, "row", [(i, (i + d) % z) for i in range(z)])
+
+    first, second = pack("pack_theirs", tile_mask, integrals, [(*FAR, False), (*REST, False)])
     v1 = lax.ppermute(first, "layer", swap)
+    ap = lax.ppermute(a, "layer", swap)
+    high, low = [ring(a, 1)], [ring(a, -1)]
     v2 = lax.ppermute(second, "layer", swap)
-    own_v, third = pack("pack_own_home", tile_mask, integrals, [(*ALL, True), (*HOME, False)], [first])
-    v3 = lax.ppermute(third, "layer", swap)
+    [own_v] = pack("pack_own", tile_mask, integrals, [(*ALL, True)], [first])
 
     up, down = far(a, ap, own_v, v1)
     far_up, far_down = send(up, True, 1), send(down, True, -1)
-    up, down, up_st, down_st = near(a, ap, own_v, v2)
+    here = hand_on([high[0], low[0]], [up])
+    high.append(ring(here[0], 1))
+    low.append(ring(here[1], -1))
+    up, down, up_st, down_st = near(a, ap, own_v, v2, here)
     near_down, near_up = send(up, True, 1), send(down, True, -1)
     up = relay(far_up, up_st)
     far_up = send(up, True, 1)
-    down = relay(far_down, down_st)
+    down = relay(far_down, down_st, [up])
     far_down = send(down, True, -1)
-    st = home(a, ap, own_v, v3, near_up, near_down)
-    own, m1, m2, m3 = turn(st, far_up, far_down)
+    here = hand_on([high[1], low[1]], [down], LONG)
+    high.append(ring(here[0], 1))
+    low.append(ring(here[1], -1))
+    st = home(a, ap, own_v, v2, near_up, near_down, here)
+    here = hand_on([high[2]], [st])
+    high.append(ring(here[0], 1))
+    own, m1, m2, m3 = turn(st, far_up, far_down, here)
     got = send(m2, False, 2), send(m1, False, 1), send(m3, False, -1)
-    holes = hole_sum(hole_integrals, gathered)
+    low[2:] = hand_on(low[2:], [m1, m2, m3])
+    holes = hole_part("holes", hole_integrals, [a, *high, *low], [0, -1, -2, -3, -4, 1, 2, 3], None, [m1, m2, m3])
     return finish(own, got, holes, occupied_energy, virtual_energy)
 
 

time: 76.6 us -> 69.9 us (0.913)
  between operations: 13.5 us -> 0.22 us
  starting transfers between devices: 15.1 us -> 26.6 us
  waiting for transfers between devices: 23.9 us -> 17.4 us
  Pallas kernels: 23.8 us -> 25.6 us
    ppermute x2 -> x8, starting transfers between devices: 0.1 us -> 12.9 us  [the longest x7 12.8 us: ring(): return lax.ppermute(value, 'row', [(i, (i + d) % z) for i in range(z)])]
    ppermute x9, waiting for transfers between devices: 20.8 us -> 15.2 us  [send(): return lax.ppermute(value, ('col', 'layer'), hop(first, d))]
    pallas_call x7 -> x11, Pallas kernels: 15.6 us -> 17.4 us  [run(): pl.pallas_call(whole, in_specs=list(in_specs) + [VM] * c + [ANY] * m, out...]
    ppermute x9, starting transfers between devices: 14.4 us -> 13.1 us  [send(): return lax.ppermute(value, ('col', 'layer'), hop(first, d))]
    ppermute x2 -> x8, waiting for transfers between devices: 2.37 us -> 2.13 us  [the longest x7 2.12 us: ring(): return lax.ppermute(value, 'row', [(i, (i + d) % z) for i in range(z)])]
  transfers between devices with their start and end apart: 14 -> 19, of which waited for: 8 -> 8; matrix products, arithmetic and copies ran while one was open for 0% -> 0% of each run, Pallas kernels for 29% -> 30%
where the time goes in v3:
time: 69.9 us; the launch traced here: 69.7 us
  starting transfers between devices  26.6 us (38%)
  Pallas kernels  25.6 us (37%)
  waiting for transfers between devices  17.4 us (25%)
    pallas_call x11, Pallas kernels, run(): pl.pallas_call(whole, in_specs=list(in_specs) + [VM] * c + [ANY] * m, out...  17.4 us
    ppermute x9, waiting for transfers between devices, send(): return lax.ppermute(value, ('col', 'layer'), hop(first, d))  15.2 us
    ppermute x9, starting transfers between devices, send(): return lax.ppermute(value, ('col', 'layer'), hop(first, d))  13.1 us
    ppermute x7, starting transfers between devices, ring(): return lax.ppermute(value, 'row', [(i, (i + d) % z) for i in range(z)])  12.8 us
    pallas_call x2, Pallas kernels, pack(): pl.pallas_call(body, out_shape=[pltpu.VMEM((n, width, width), BF16) for _...  6.79 us
    ppermute x7, waiting for transfers between devices, ring(): return lax.ppermute(value, 'row', [(i, (i + d) % z) for i in range(z)])  2.12 us
  transfers between devices with their start and end apart: 19, of which 8 were waited for; matrix products, arithmetic and copies ran while one was open for 0% of the time, Pallas kernels for 30%

profile of v3, /device:TPU:8, one launch (start us, length us, event | category | flops | bytes accessed | tf_op | source)
XLA Modules:
  0.0 69.7 jit_solution(14424633560404747011)
XLA Ops:
  0.0 0.0 copy-start
  0.0 3.5 %pack_theirs.1 = (bf16[4,384,384]{2,1,0:T(8,128)(2,1)S(1)}, bf16[12,384,384]{2,1,0:T(8,128)(2,1)S(1)}) custom-call(s32[96,96]{1,0:T(8,128)} %mask_ref.3, bf16[384,12288]{1,0:T(8,128)(2,1)} %v_ref.3), custom_call_target="tpu_custom_call" | custom-call | bytes 9437 | tf_op jit(solution)/shard_map/pack_theirs/pallas_call | solution.py:157
  3.5 0.1 collective-permute-start.1
  3.6 0.5 collective-permute-start.4
  4.1 0.0 copy-done
  4.1 0.1 collective-permute-start
  4.2 1.9 %collective-permute-start.2 = (bf16[512,384]{1,0:T(8,128)(2,1)S(1)}, bf16[512,384]{1,0:T(8,128)(2,1)S(1)}, u32[]{:S(2)}, u32[]{:S(2)}) collective-permute-start(bf16[512,384]{1,0:T(8,128)(2,1)S(1)} %copy-done), channel_id=1, source_target_pairs={{0,32},{32,64},{64,96},{96,128},{128,160},{160,192},{192,224},{224... | collective-permute-start | bytes 1179656 | tf_op jit(solution)/shard_map/ppermute | solution.py:376
  6.1 3.9 %collective-permute-start.3 = (bf16[512,384]{1,0:T(8,128)(2,1)S(1)}, bf16[512,384]{1,0:T(8,128)(2,1)S(1)}, u32[]{:S(2)}, u32[]{:S(2)}) collective-permute-start(bf16[512,384]{1,0:T(8,128)(2,1)S(1)} %copy-done), channel_id=1, source_target_pairs={{0,224},{32,0},{64,32},{96,64},{128,96},{160,128},{192,160},{224,1... | collective-permute-start | bytes 1179656 | tf_op jit(solution)/shard_map/ppermute | solution.py:376
  10.0 3.3 %pack_own.1.refs_2_ = bf16[16,384,384]{2,1,0:T(8,128)(2,1)S(1)} custom-call(s32[96,96]{1,0:T(8,128)} %mask_ref.3, bf16[384,12288]{1,0:T(8,128)(2,1)} %v_ref.3, bf16[4,384,384]{2,1,0:T(8,128)(2,1)S(1)} %get-tuple-element.21.refs_0_), custom_call_target="tpu_custom_call" | custom-call | bytes 9437 | tf_op jit(solution)/shard_map/pack_own/pallas_call | solution.py:157
  13.4 0.0 collective-permute-done.refs_1_
  13.4 0.0 collective-permute-done.4.refs_3_
  13.4 2.7 %far.1 = (s16[1040,384]{1,0:T(8,128)(2,1)S(1)}, s16[1040,384]{1,0:T(8,128)(2,1)S(1)}) custom-call(bf16[512,384]{1,0:T(8,128)(2,1)S(1)} %copy-done, bf16[512,384]{1,0:T(8,128)(2,1)S(1)} %collective-permute-done.refs_1_, bf16[16,384,384]{2,1,0:T(8,128)(2,1)S(1)} %pack_own.1.refs_2_, bf16[4,384,384]{2,1,0:T(8,128)(2,1)S(1)} %collective-permute-done.4.refs_3_), custom_call_target="tpu_custom_call" | custom-call | flops 1207959 | bytes 2359 | tf_op jit(solution)/shard_map/far/pallas_call | solution.py:53
  16.1 1.6 %collective-permute-start.10 = (s16[1040,384]{1,0:T(8,128)(2,1)S(1)}, s16[1040,384]{1,0:T(8,128)(2,1)S(1)}, u32[]{:S(2)}, u32[]{:S(2)}) collective-permute-start(s16[1040,384]{1,0:T(8,128)(2,1)S(1)} %get-tuple-element.23.refs_2_), channel_id=1, source_target_pairs={{0,2},{1,9},{2,4},{3,11},{4,6},{5,13},{6,0},{7,15},{8,10},{9,17},{... | collective-permute-start | bytes 2396168 | tf_op jit(solution)/shard_map/ppermute | solution.py:38
  17.7 1.7 %collective-permute-start.9 = (s16[1040,384]{1,0:T(8,128)(2,1)S(1)}, s16[1040,384]{1,0:T(8,128)(2,1)S(1)}, u32[]{:S(2)}, u32[]{:S(2)}) collective-permute-start(s16[1040,384]{1,0:T(8,128)(2,1)S(1)} %get-tuple-element.28), channel_id=1, source_target_pairs={{0,6},{1,25},{2,0},{3,27},{4,2},{5,29},{6,4},{7,31},{8,14},{9,1},{... | collective-permute-start | bytes 2396168 | tf_op jit(solution)/shard_map/ppermute | solution.py:38
  19.4 0.3 collective-permute-done.2.refs_0_.refs_2_
  19.7 0.0 collective-permute-done.3.refs_1_.refs_6_
  19.7 0.1 hand_on.4
  19.8 0.4 collective-permute-start.7
  20.2 4.0 %collective-permute-start.8 = (bf16[512,384]{1,0:T(8,128)(2,1)S(1)}, bf16[512,384]{1,0:T(8,128)(2,1)S(1)}, u32[]{:S(2)}, u32[]{:S(2)}) collective-permute-start(bf16[512,384]{1,0:T(8,128)(2,1)S(1)} %get-tuple-element.25.refs_5_), channel_id=1, source_target_pairs={{0,224},{32,0},{64,32},{96,64},{128,96},{160,128},{192,160},{224,1... | collective-permute-start | bytes 1179656 | tf_op jit(solution)/shard_map/ppermute | solution.py:376
  24.2 0.0 copy-done.1
  24.2 0.0 copy-done.3
  24.2 0.0 collective-permute-done.1.refs_3_
  24.2 4.1 %near.1 = (s16[1040,384]{1,0:T(8,128)(2,1)S(1)}, s16[1040,384]{1,0:T(8,128)(2,1)S(1)}, f32[1024,384]{1,0:T(8,128)S(1)}, f32[1024,384]{1,0:T(8,128)S(1)}) custom-call(bf16[512,384]{1,0:T(8,128)(2,1)S(1)} %copy-done, bf16[512,384]{1,0:T(8,128)(2,1)S(1)} %collective-permute-done.refs_1_, bf16[16,384,384]{2,1,0:T(8,128)(2,1)S(1)} %pack_own.1.refs_2_, ...), custom_call_target="tpu_custom_call" | custom-call | flops 99999997952 | tf_op jit(solution)/shard_map/near/pallas_call | solution.py:53
  28.3 1.7 %collective-permute-start.5 = (s16[1040,384]{1,0:T(8,128)(2,1)S(1)}, s16[1040,384]{1,0:T(8,128)(2,1)S(1)}, u32[]{:S(2)}, u32[]{:S(2)}) collective-permute-start(s16[1040,384]{1,0:T(8,128)(2,1)S(1)} %get-tuple-element.26), channel_id=1, source_target_pairs={{0,6},{1,25},{2,0},{3,27},{4,2},{5,29},{6,4},{7,31},{8,14},{9,1},{... | collective-permute-start | bytes 2396168 | tf_op jit(solution)/shard_map/ppermute | solution.py:38
  30.0 0.0 collective-permute-done.10.refs_0_
  30.0 0.4 collective-permute-start.6
  30.4 1.7 %relay.2.refs_2_ = s16[1040,384]{1,0:T(8,128)(2,1)} custom-call(s16[1040,384]{1,0:T(8,128)(2,1)S(1)} %collective-permute-done.10.refs_0_, f32[1024,384]{1,0:T(8,128)S(1)} %get-tuple-element.30.refs_1_), custom_call_target="tpu_custom_call" | custom-call | bytes 3145 | tf_op jit(solution)/shard_map/relay/pallas_call | solution.py:53
  32.1 0.0 collective-permute-done.9.refs_0_
  32.1 0.9 %collective-permute-start.11 = (s16[1040,384]{1,0:T(8,128)(2,1)}, s16[1040,384]{1,0:T(8,128)(2,1)}, u32[]{:S(2)}, u32[]{:S(2)}) collective-permute-start(s16[1040,384]{1,0:T(8,128)(2,1)} %relay.2.refs_2_), channel_id=1, source_target_pairs={{0,2},{1,9},{2,4},{3,11},{4,6},{5,13},{6,0},{7,15},{8,10},{9,17},{... | collective-permute-start | bytes 2396168 | tf_op jit(solution)/shard_map/ppermute | solution.py:38
  33.0 1.7 %relay.3.refs_2_ = s16[1040,384]{1,0:T(8,128)(2,1)} custom-call(s16[1040,384]{1,0:T(8,128)(2,1)S(1)} %collective-permute-done.9.refs_0_, f32[1024,384]{1,0:T(8,128)S(1)} %get-tuple-element.29.refs_1_, s16[1040,384]{1,0:T(8,128)(2,1)} %relay.2.refs_2_), custom_call_target="tpu_custom_call" | custom-call | bytes 3145 | tf_op jit(solution)/shard_map/relay/pallas_call | solution.py:53
  34.6 0.0 collective-permute-done.7.refs_0_.refs_3_
  34.6 2.3 %collective-permute-start.12 = (s16[1040,384]{1,0:T(8,128)(2,1)}, s16[1040,384]{1,0:T(8,128)(2,1)}, u32[]{:S(2)}, u32[]{:S(2)}) collective-permute-start(s16[1040,384]{1,0:T(8,128)(2,1)} %relay.3.refs_2_), channel_id=1, source_target_pairs={{0,6},{1,25},{2,0},{3,27},{4,2},{5,29},{6,4},{7,31},{8,14},{9,1},{... | collective-permute-start | bytes 2396168 | tf_op jit(solution)/shard_map/ppermute | solution.py:38
  37.0 0.0 collective-permute-done.8.refs_1_.refs_7_
  37.0 0.1 hand_on.5
  37.0 0.1 collective-permute-start.13
  37.1 3.3 %collective-permute-done.5.refs_4_ = s16[1040,384]{1,0:T(8,128)(2,1)S(1)} collective-permute-done((s16[1040,384]{1,0:T(8,128)(2,1)S(1)}, s16[1040,384]{1,0:T(8,128)(2,1)S(1)}, u32[]{:S(2)}, u32[]{:S(2)}) %collective-permute-start.5) | collective-permute-done | bytes 798752 | tf_op jit(solution)/shard_map/ppermute | solution.py:38
  40.5 2.4 %collective-permute-start.18 = (bf16[512,384]{1,0:T(8,128)(2,1)S(1)}, bf16[512,384]{1,0:T(8,128)(2,1)S(1)}, u32[]{:S(2)}, u32[]{:S(2)}) collective-permute-start(bf16[512,384]{1,0:T(8,128)(2,1)S(1)} %get-tuple-element.32.refs_7_), channel_id=1, source_target_pairs={{0,224},{32,0},{64,32},{96,64},{128,96},{160,128},{192,160},{224,1... | collective-permute-start | bytes 1179656 | tf_op jit(solution)/shard_map/ppermute | solution.py:376
  42.9 0.5 collective-permute-done.6.refs_5_
  43.4 2.4 %home.1.refs_1_.refs_0_ = f32[4,512,384]{2,1,0:T(8,128)S(1)} custom-call(bf16[512,384]{1,0:T(8,128)(2,1)S(1)} %copy-done, bf16[512,384]{1,0:T(8,128)(2,1)S(1)} %collective-permute-done.refs_1_, bf16[16,384,384]{2,1,0:T(8,128)(2,1)S(1)} %pack_own.1.refs_2_, bf16[12,384,384]{2,1,0:T(8,128)(2,1)S(1)} %collective-permute-done.1.refs_3_, ...), custom_call_target="tpu_custom_call" | custom-call | flops 99999997952 | tf_op jit(solution)/shard_map/home/pallas_call | solution.py:53
  45.8 0.0 copy-start.7
  45.8 1.8 %collective-permute-done.13.refs_0_.refs_4_ = bf16[512,384]{1,0:T(8,128)(2,1)S(1)} collective-permute-done((bf16[512,384]{1,0:T(8,128)(2,1)S(1)}, bf16[512,384]{1,0:T(8,128)(2,1)S(1)}, u32[]{:S(2)}, u32[]{:S(2)}) %collective-permute-start.13) | collective-permute-done | bytes 393248 | tf_op jit(solution)/shard_map/ppermute | solution.py:376
  47.7 0.1 collective-permute-start.17
  47.8 0.0 copy-done.7
  47.8 0.0 copy-start.2
  47.8 0.0 copy-start.4
  47.8 0.0 copy-start.6
  47.8 1.3 %collective-permute-done.12.refs_2_ = s16[1040,384]{1,0:T(8,128)(2,1)} collective-permute-done((s16[1040,384]{1,0:T(8,128)(2,1)}, s16[1040,384]{1,0:T(8,128)(2,1)}, u32[]{:S(2)}, u32[]{:S(2)}) %collective-permute-start.12) | collective-permute-done | bytes 798752 | tf_op jit(solution)/shard_map/ppermute | solution.py:38
  49.1 2.9 %collective-permute-done.11.refs_1_ = s16[1040,384]{1,0:T(8,128)(2,1)} collective-permute-done((s16[1040,384]{1,0:T(8,128)(2,1)}, s16[1040,384]{1,0:T(8,128)(2,1)}, u32[]{:S(2)}, u32[]{:S(2)}) %collective-permute-start.11) | collective-permute-done | bytes 798752 | tf_op jit(solution)/shard_map/ppermute | solution.py:38
  52.0 2.3 %turn.1 = (f32[512,384]{1,0:T(8,128)S(1)}, s16[528,384]{1,0:T(8,128)(2,1)S(1)}, s16[528,384]{1,0:T(8,128)(2,1)S(1)}, s16[528,384]{1,0:T(8,128)(2,1)S(1)}) custom-call(f32[4,512,384]{2,1,0:T(8,128)S(1)} %home.1.refs_1_.refs_0_, s16[1040,384]{1,0:T(8,128)(2,1)} %collective-permute-done.11.refs_1_, s16[1040,384]{1,0:T(8,128)(2,1)} %collective-permute-done.12.refs_2_, ...), custom_call_target="tpu_custom_call" | custom-call | bytes 7864 | tf_op jit(solution)/shard_map/turn/pallas_call | solution.py:53
  54.4 2.4 %collective-permute-start.14 = (s16[528,384]{1,0:T(8,128)(2,1)S(1)}, s16[528,384]{1,0:T(8,128)(2,1)S(1)}, u32[]{:S(2)}, u32[]{:S(2)}) collective-permute-start(s16[528,384]{1,0:T(8,128)(2,1)S(1)} %get-tuple-element.34.refs_2_.refs_10_), channel_id=1, source_target_pairs={{0,16},{1,5},{2,18},{3,7},{4,20},{5,1},{6,22},{7,3},{8,24},{9,13},... | collective-permute-start | bytes 1216520 | tf_op jit(solution)/shard_map/ppermute | solution.py:38
  56.7 0.0 collective-permute-start.15
  56.8 2.0 %collective-permute-start.16 = (s16[528,384]{1,0:T(8,128)(2,1)S(1)}, s16[528,384]{1,0:T(8,128)(2,1)S(1)}, u32[]{:S(2)}, u32[]{:S(2)}) collective-permute-start(s16[528,384]{1,0:T(8,128)(2,1)S(1)} %get-tuple-element.36.refs_3_.refs_11_), channel_id=1, source_target_pairs={{0,24},{1,7},{2,26},{3,1},{4,28},{5,3},{6,30},{7,5},{8,0},{9,15},{... | collective-permute-start | bytes 1216520 | tf_op jit(solution)/shard_map/ppermute | solution.py:38
  58.8 0.0 collective-permute-done.18.refs_0_
  58.8 0.0 copy-start.5
  58.8 0.0 collective-permute-done.17.refs_5_
  58.8 0.0 copy-done.2
  58.9 0.0 copy-done.4
  58.9 0.0 copy-done.6
  58.9 2.3 %holes.1.holes_ref = f32[512,384]{1,0:T(8,128)S(1)} custom-call(bf16[512,4096]{1,0:T(8,128)(2,1)S(1)} %copy-done.6, bf16[512,384]{1,0:T(8,128)(2,1)S(1)} %copy-done, bf16[512,384]{1,0:T(8,128)(2,1)S(1)} %copy-done.2, bf16[512,384]{1,0:T(8,128)(2,1)S(1)} %collective-permute-done.7.refs_0_.refs_3_, ...), custom_call_target="tpu_custom_call" | custom-call | flops 99999997952 | tf_op jit(solution)/shard_map/holes/pallas_call | solution.py:53
  61.2 2.8 %collective-permute-done.14.m1 = s16[528,384]{1,0:T(8,128)(2,1)S(1)} collective-permute-done((s16[528,384]{1,0:T(8,128)(2,1)S(1)}, s16[528,384]{1,0:T(8,128)(2,1)S(1)}, u32[]{:S(2)}, u32[]{:S(2)}) %collective-permute-start.14) | collective-permute-done | bytes 405536 | tf_op jit(solution)/shard_map/ppermute | solution.py:38
  64.0 4.4 %collective-permute-done.15.m2 = s16[528,384]{1,0:T(8,128)(2,1)S(1)} collective-permute-done((s16[528,384]{1,0:T(8,128)(2,1)S(1)}, s16[528,384]{1,0:T(8,128)(2,1)S(1)}, u32[]{:S(2)}, u32[]{:S(2)}) %collective-permute-start.15) | collective-permute-done | bytes 405536 | tf_op jit(solution)/shard_map/ppermute | solution.py:38
  68.4 0.0 collective-permute-done.16.m3
  68.4 0.0 copy-done.5
  68.4 1.4 %finish.1 = f32[512,384]{1,0:T(8,128)} custom-call(f32[512,384]{1,0:T(8,128)S(1)} %get-tuple-element.33.own_ref, s16[528,384]{1,0:T(8,128)(2,1)S(1)} %collective-permute-done.14.m1, s16[528,384]{1,0:T(8,128)(2,1)S(1)} %collective-permute-done.15.m2, s16[528,384]{1,0:T(8,128)(2,1)S(1)} %collective-permute-done.16.m3, f32[512,384]{1,0:T(8,128)S(1)} %holes.1.holes_ref, ...), custom_call_target="tpu_custom_call" | custom-call | bytes 4718 | tf_op jit(solution)/shard_map/finish/pallas_call | solution.py:359
  (5 shorter events, 0.1 us)
Async XLA Ops:
  0.0 4.1 %copy-start = (bf16[512,384]{1,0:T(8,128)(2,1)S(1)}, bf16[512,384]{1,0:T(8,128)(2,1)}, u32[]{:S(2)}) copy-start(bf16[512,384]{1,0:T(8,128)(2,1)} %refs_1_.1) | copy-start | bytes 1179652
  3.5 20.7 %collective-permute-start.1 = (bf16[12,384,384]{2,1,0:T(8,128)(2,1)S(1)}, bf16[12,384,384]{2,1,0:T(8,128)(2,1)S(1)}, u32[]{:S(2)}, u32[]{:S(2)}) collective-permute-start(bf16[12,384,384]{2,1,0:T(8,128)(2,1)S(1)} %get-tuple-element.22), channel_id=1, source_target_pairs={{0,1},{1,0},{2,3},{3,2},{4,5},{5,4},{6,7},{7,6},{8,9},{9,8},{10,11... | collective-permute-start | bytes 10616840 | tf_op jit(solution)/shard_map/ppermute | solution.py:382
  3.6 9.8 %collective-permute-start.4 = (bf16[4,384,384]{2,1,0:T(8,128)(2,1)S(1)}, bf16[4,384,384]{2,1,0:T(8,128)(2,1)S(1)}, u32[]{:S(2)}, u32[]{:S(2)}) collective-permute-start(bf16[4,384,384]{2,1,0:T(8,128)(2,1)S(1)} %get-tuple-element.21.refs_0_), channel_id=1, source_target_pairs={{0,1},{1,0},{2,3},{3,2},{4,5},{5,4},{6,7},{7,6},{8,9},{9,8},{10,11... | collective-permute-start | bytes 3538952 | tf_op jit(solution)/shard_map/ppermute | solution.py:379
  4.1 9.3 %collective-permute-start = (bf16[512,384]{1,0:T(8,128)(2,1)S(1)}, bf16[512,384]{1,0:T(8,128)(2,1)S(1)}, u32[]{:S(2)}, u32[]{:S(2)}) collective-permute-start(bf16[512,384]{1,0:T(8,128)(2,1)S(1)} %copy-done), channel_id=1, source_target_pairs={{0,1},{1,0},{2,3},{3,2},{4,5},{5,4},{6,7},{7,6},{8,9},{9,8},{10,11... | collective-permute-start | bytes 1179656 | tf_op jit(solution)/shard_map/ppermute | solution.py:380
  4.2 15.5 %collective-permute-start.2 = (bf16[512,384]{1,0:T(8,128)(2,1)S(1)}, bf16[512,384]{1,0:T(8,128)(2,1)S(1)}, u32[]{:S(2)}, u32[]{:S(2)}) collective-permute-start(bf16[512,384]{1,0:T(8,128)(2,1)S(1)} %copy-done), channel_id=1, source_target_pairs={{0,32},{32,64},{64,96},{96,128},{128,160},{160,192},{192,224},{224... | collective-permute-start | bytes 1179656 | tf_op jit(solution)/shard_map/ppermute | solution.py:376
  6.1 13.6 %collective-permute-start.3 = (bf16[512,384]{1,0:T(8,128)(2,1)S(1)}, bf16[512,384]{1,0:T(8,128)(2,1)S(1)}, u32[]{:S(2)}, u32[]{:S(2)}) collective-permute-start(bf16[512,384]{1,0:T(8,128)(2,1)S(1)} %copy-done), channel_id=1, source_target_pairs={{0,224},{32,0},{64,32},{96,64},{128,96},{160,128},{192,160},{224,1... | collective-permute-start | bytes 1179656 | tf_op jit(solution)/shard_map/ppermute | solution.py:376
  16.1 13.9 %collective-permute-start.10 = (s16[1040,384]{1,0:T(8,128)(2,1)S(1)}, s16[1040,384]{1,0:T(8,128)(2,1)S(1)}, u32[]{:S(2)}, u32[]{:S(2)}) collective-permute-start(s16[1040,384]{1,0:T(8,128)(2,1)S(1)} %get-tuple-element.23.refs_2_), channel_id=1, source_target_pairs={{0,2},{1,9},{2,4},{3,11},{4,6},{5,13},{6,0},{7,15},{8,10},{9,17},{... | collective-permute-start | bytes 2396168 | tf_op jit(solution)/shard_map/ppermute | solution.py:38
  17.7 14.4 %collective-permute-start.9 = (s16[1040,384]{1,0:T(8,128)(2,1)S(1)}, s16[1040,384]{1,0:T(8,128)(2,1)S(1)}, u32[]{:S(2)}, u32[]{:S(2)}) collective-permute-start(s16[1040,384]{1,0:T(8,128)(2,1)S(1)} %get-tuple-element.28), channel_id=1, source_target_pairs={{0,6},{1,25},{2,0},{3,27},{4,2},{5,29},{6,4},{7,31},{8,14},{9,1},{... | collective-permute-start | bytes 2396168 | tf_op jit(solution)/shard_map/ppermute | solution.py:38
  19.7 4.5 %copy-start.1 = (bf16[512,384]{1,0:T(8,128)(2,1)}, bf16[512,384]{1,0:T(8,128)(2,1)S(1)}, u32[]{:S(2)}) copy-start(bf16[512,384]{1,0:T(8,128)(2,1)S(1)} %collective-permute-done.2.refs_0_.refs_2_) | copy-start | bytes 1179652
  19.7 4.5 %copy-start.3 = (bf16[512,384]{1,0:T(8,128)(2,1)}, bf16[512,384]{1,0:T(8,128)(2,1)S(1)}, u32[]{:S(2)}) copy-start(bf16[512,384]{1,0:T(8,128)(2,1)S(1)} %collective-permute-done.3.refs_1_.refs_6_) | copy-start | bytes 1179652
  19.8 14.8 %collective-permute-start.7 = (bf16[512,384]{1,0:T(8,128)(2,1)S(1)}, bf16[512,384]{1,0:T(8,128)(2,1)S(1)}, u32[]{:S(2)}, u32[]{:S(2)}) collective-permute-start(bf16[512,384]{1,0:T(8,128)(2,1)S(1)} %get-tuple-element.24.refs_4_), channel_id=1, source_target_pairs={{0,32},{32,64},{64,96},{96,128},{128,160},{160,192},{192,224},{224... | collective-permute-start | bytes 1179656 | tf_op jit(solution)/shard_map/ppermute | solution.py:376
  20.2 16.8 %collective-permute-start.8 = (bf16[512,384]{1,0:T(8,128)(2,1)S(1)}, bf16[512,384]{1,0:T(8,128)(2,1)S(1)}, u32[]{:S(2)}, u32[]{:S(2)}) collective-permute-start(bf16[512,384]{1,0:T(8,128)(2,1)S(1)} %get-tuple-element.25.refs_5_), channel_id=1, source_target_pairs={{0,224},{32,0},{64,32},{96,64},{128,96},{160,128},{192,160},{224,1... | collective-permute-start | bytes 1179656 | tf_op jit(solution)/shard_map/ppermute | solution.py:376
  28.3 12.2 %collective-permute-start.5 = (s16[1040,384]{1,0:T(8,128)(2,1)S(1)}, s16[1040,384]{1,0:T(8,128)(2,1)S(1)}, u32[]{:S(2)}, u32[]{:S(2)}) collective-permute-start(s16[1040,384]{1,0:T(8,128)(2,1)S(1)} %get-tuple-element.26), channel_id=1, source_target_pairs={{0,6},{1,25},{2,0},{3,27},{4,2},{5,29},{6,4},{7,31},{8,14},{9,1},{... | collective-permute-start | bytes 2396168 | tf_op jit(solution)/shard_map/ppermute | solution.py:38
  30.0 13.3 %collective-permute-start.6 = (s16[1040,384]{1,0:T(8,128)(2,1)S(1)}, s16[1040,384]{1,0:T(8,128)(2,1)S(1)}, u32[]{:S(2)}, u32[]{:S(2)}) collective-permute-start(s16[1040,384]{1,0:T(8,128)(2,1)S(1)} %get-tuple-element.27), channel_id=1, source_target_pairs={{0,2},{1,9},{2,4},{3,11},{4,6},{5,13},{6,0},{7,15},{8,10},{9,17},{... | collective-permute-start | bytes 2396168 | tf_op jit(solution)/shard_map/ppermute | solution.py:38
  32.1 20.0 %collective-permute-start.11 = (s16[1040,384]{1,0:T(8,128)(2,1)}, s16[1040,384]{1,0:T(8,128)(2,1)}, u32[]{:S(2)}, u32[]{:S(2)}) collective-permute-start(s16[1040,384]{1,0:T(8,128)(2,1)} %relay.2.refs_2_), channel_id=1, source_target_pairs={{0,2},{1,9},{2,4},{3,11},{4,6},{5,13},{6,0},{7,15},{8,10},{9,17},{... | collective-permute-start | bytes 2396168 | tf_op jit(solution)/shard_map/ppermute | solution.py:38
  34.6 14.5 %collective-permute-start.12 = (s16[1040,384]{1,0:T(8,128)(2,1)}, s16[1040,384]{1,0:T(8,128)(2,1)}, u32[]{:S(2)}, u32[]{:S(2)}) collective-permute-start(s16[1040,384]{1,0:T(8,128)(2,1)} %relay.3.refs_2_), channel_id=1, source_target_pairs={{0,6},{1,25},{2,0},{3,27},{4,2},{5,29},{6,4},{7,31},{8,14},{9,1},{... | collective-permute-start | bytes 2396168 | tf_op jit(solution)/shard_map/ppermute | solution.py:38
  37.0 10.6 %collective-permute-start.13 = (bf16[512,384]{1,0:T(8,128)(2,1)S(1)}, bf16[512,384]{1,0:T(8,128)(2,1)S(1)}, u32[]{:S(2)}, u32[]{:S(2)}) collective-permute-start(bf16[512,384]{1,0:T(8,128)(2,1)S(1)} %get-tuple-element.31.refs_6_), channel_id=1, source_target_pairs={{0,32},{32,64},{64,96},{96,128},{128,160},{160,192},{192,224},{224... | collective-permute-start | bytes 1179656 | tf_op jit(solution)/shard_map/ppermute | solution.py:376
  40.5 18.3 %collective-permute-start.18 = (bf16[512,384]{1,0:T(8,128)(2,1)S(1)}, bf16[512,384]{1,0:T(8,128)(2,1)S(1)}, u32[]{:S(2)}, u32[]{:S(2)}) collective-permute-start(bf16[512,384]{1,0:T(8,128)(2,1)S(1)} %get-tuple-element.32.refs_7_), channel_id=1, source_target_pairs={{0,224},{32,0},{64,32},{96,64},{128,96},{160,128},{192,160},{224,1... | collective-permute-start | bytes 1179656 | tf_op jit(solution)/shard_map/ppermute | solution.py:376
  45.8 2.0 %copy-start.7 = (f32[384]{0:T(512)S(1)}, f32[384]{0:T(512)}, u32[]{:S(2)}) copy-start(f32[384]{0:T(512)} %param.11) | copy-start | bytes 4612
  47.7 11.2 %collective-permute-start.17 = (bf16[512,384]{1,0:T(8,128)(2,1)S(1)}, bf16[512,384]{1,0:T(8,128)(2,1)S(1)}, u32[]{:S(2)}, u32[]{:S(2)}) collective-permute-start(bf16[512,384]{1,0:T(8,128)(2,1)S(1)} %hand_on.6.refs_3_), channel_id=1, source_target_pairs={{0,32},{32,64},{64,96},{96,128},{128,160},{160,192},{192,224},{224... | collective-permute-start | bytes 1179656 | tf_op jit(solution)/shard_map/ppermute | solution.py:376
  47.8 11.1 %copy-start.2 = (bf16[512,384]{1,0:T(8,128)(2,1)S(1)}, bf16[512,384]{1,0:T(8,128)(2,1)}, u32[]{:S(2)}) copy-start(bf16[512,384]{1,0:T(8,128)(2,1)} %copy-done.1) | copy-start | bytes 1179652
  47.8 11.1 %copy-start.4 = (bf16[512,384]{1,0:T(8,128)(2,1)S(1)}, bf16[512,384]{1,0:T(8,128)(2,1)}, u32[]{:S(2)}) copy-start(bf16[512,384]{1,0:T(8,128)(2,1)} %copy-done.3) | copy-start | bytes 1179652
  47.8 11.1 %copy-start.6 = (bf16[512,4096]{1,0:T(8,128)(2,1)S(1)}, bf16[512,4096]{1,0:T(8,128)(2,1)}, u32[]{:S(2)}) copy-start(bf16[512,4096]{1,0:T(8,128)(2,1)} %refs_0_.7) | copy-start | bytes 12582916
  54.4 9.6 %collective-permute-start.14 = (s16[528,384]{1,0:T(8,128)(2,1)S(1)}, s16[528,384]{1,0:T(8,128)(2,1)S(1)}, u32[]{:S(2)}, u32[]{:S(2)}) collective-permute-start(s16[528,384]{1,0:T(8,128)(2,1)S(1)} %get-tuple-element.34.refs_2_.refs_10_), channel_id=1, source_target_pairs={{0,16},{1,5},{2,18},{3,7},{4,20},{5,1},{6,22},{7,3},{8,24},{9,13},... | collective-permute-start | bytes 1216520 | tf_op jit(solution)/shard_map/ppermute | solution.py:38
  56.7 11.6 %collective-permute-start.15 = (s16[528,384]{1,0:T(8,128)(2,1)S(1)}, s16[528,384]{1,0:T(8,128)(2,1)S(1)}, u32[]{:S(2)}, u32[]{:S(2)}) collective-permute-start(s16[528,384]{1,0:T(8,128)(2,1)S(1)} %get-tuple-element.35.refs_1_.refs_9_), channel_id=1, source_target_pairs={{0,8},{1,3},{2,10},{3,5},{4,12},{5,7},{6,14},{7,1},{8,16},{9,11},{... | collective-permute-start | bytes 1216520 | tf_op jit(solution)/shard_map/ppermute | solution.py:38
  56.8 11.6 %collective-permute-start.16 = (s16[528,384]{1,0:T(8,128)(2,1)S(1)}, s16[528,384]{1,0:T(8,128)(2,1)S(1)}, u32[]{:S(2)}, u32[]{:S(2)}) collective-permute-start(s16[528,384]{1,0:T(8,128)(2,1)S(1)} %get-tuple-element.36.refs_3_.refs_11_), channel_id=1, source_target_pairs={{0,24},{1,7},{2,26},{3,1},{4,28},{5,3},{6,30},{7,5},{8,0},{9,15},{... | collective-permute-start | bytes 1216520 | tf_op jit(solution)/shard_map/ppermute | solution.py:38
  58.8 9.6 %copy-start.5 = (f32[512]{0:T(512)S(1)}, f32[512]{0:T(512)}, u32[]{:S(2)}) copy-start(f32[512]{0:T(512)} %param.10) | copy-start | bytes 6148

commit v4 on v3

--- a/solution.py
+++ b/solution.py
@@ -20,7 +20,7 @@
 VM = pl.BlockSpec(memory_space=pltpu.VMEM)
 ANY = pl.BlockSpec(memory_space=pl.ANY)
 
-FAR, REST, ALL = (0, 4), (4, 12), (0, 16)
+FAR, REST = (0, 4), (4, 12)
 
 
 def hop(first, d):
@@ -73,7 +73,7 @@
     return pl.CostEstimate(flops=int(flops) // SCALE, bytes_accessed=int(moved) // SCALE, transcendentals=0)
 
 
-LONG = cost(10 ** 14, 0)
+LONG = cost(2 * 10 ** 13, 0)
 
 
 def loop(n, unroll=1):
@@ -218,11 +218,11 @@
 
         @loop(4)
         def _(o):
-            part = product(lhs, own_ref, 4 + o, v2_ref, o)
+            part = product(lhs, own_ref, o, v2_ref, o)
             up_st[rows_at(o, half), :] = part[:half]
             for b in range(n):
                 put(up_ref, o * n + b, part[half + b * TB:half + (b + 1) * TB])
-            part = product(lhs, own_ref, 8 + o, v2_ref, 4 + o)
+            part = product(lhs, own_ref, 4 + o, v2_ref, 4 + o)
             down_st[rows_at(o, half), :] = part[half:]
             for b in range(n):
                 put(down_ref, o * n + b, part[b * TB:(b + 1) * TB])
@@ -250,7 +250,7 @@
 
         @loop(4)
         def _(o):
-            part = product(lhs, own_ref, 12 + o, v2_ref, 8 + o)
+            part = product(lhs, own_ref, 8 + o, v2_ref, 8 + o)
             for b in range(n):
                 here = slice(b * TB, (b + 1) * TB)
                 out_ref[o, here, :] = part[here] + get(up_ref if b < h else down_ref, o * h + b % h)
@@ -316,55 +316,62 @@
     )
 
 
-def hole_part(name, hole_integrals, blocks, away, before=None, after=()):
+def hole_part(hole_integrals, blocks, away, own, occupied, virtual, after=()):
     rows = hole_integrals.shape[0]
     depth, width = blocks[0].shape
     count = hole_integrals.shape[1] // depth
-    more = [] if before is None else [before]
-
-    def body(h_ref, *refs):
-        out_ref = refs[-1]
+
+    def body(h_ref, own_ref, occ_ref, virt_ref, *refs):
+        sum_ref, inverse_ref = refs[-2:]
         here = lax.axis_index("row")
-        total = refs[len(blocks)][...] if more else None
+        virt = virt_ref[...]
+        for b in range(rows // TB):
+            at = slice(b * TB, (b + 1) * TB)
+            occ = jnp.broadcast_to(occ_ref[:, at], (TB, TB)).T
+            inverse_ref[at, :] = 1.0 / (virt - jnp.concatenate([occ] * (width // TB), axis=1))
+        total = own_ref[...]
         for ref, k in zip(refs, away):
             at = lax.rem(here + (k + count), count)
-            part = jnp.dot(h_ref[:, rows_at(at, depth)], ref[...], preferred_element_type=F32)
-            total = part if total is None else total + part
-        out_ref[...] = total
-
-    return run(
-        body,
-        after,
-        [*map(inside, (hole_integrals, *blocks, *more))],
-        [VM] * (1 + len(blocks) + len(more)),
-        out_shape=pltpu.VMEM((rows, width), F32),
-        out_specs=VM,
+            total = total + jnp.dot(h_ref[:, rows_at(at, depth)], ref[...], preferred_element_type=F32)
+        sum_ref[...] = total
+
+    return run(
+        body,
+        after,
+        [*map(inside, (hole_integrals, own)), occupied[None, :], virtual[None, :], *map(inside, blocks)],
+        [VM] * (4 + len(blocks)),
+        out_shape=[pltpu.VMEM((rows, width), F32)] * 2,
+        out_specs=[VM] * 2,
         cost_estimate=LONG,
-        name=name,
-    )
-
-
-def finish(own, got, holes, occupied, virtual):
-    rows, width = own.shape
-
-    def body(own_ref, m1, m2, m3, holes_ref, occ_ref, virt_ref, out_ref):
-        virt = virt_ref[...]
-        for b in range(rows // TB):
+        name="holes",
+    )
+
+
+def finish(total, inverse, got):
+    rows, width = total.shape
+    n = rows // TB
+
+    def body(sum_ref, inverse_ref, m1, m2, m3, out_hbm, out_ref, sem):
+        copies = []
+        for b in range(n):
             here = slice(b * TB, (b + 1) * TB)
-            total = own_ref[here, :] + get(m1, b) + get(m2, b) + get(m3, b)
-            occ = jnp.broadcast_to(occ_ref[:, here], (TB, TB)).T
-            occ = jnp.concatenate([occ] * (width // TB), axis=1)
-            out_ref[here, :] = (total + holes_ref[here, :]) / (virt - occ)
+            part = sum_ref[here, :] + get(m1, b) + get(m2, b) + get(m3, b)
+            out_ref[here, :] = part * inverse_ref[here, :]
+            copies.append(pltpu.make_async_copy(out_ref.at[here, :], out_hbm.at[here, :], sem.at[b]))
+            copies[-1].start()
+        for copy in copies:
+            copy.wait()
 
     return pl.pallas_call(
         body,
         out_shape=jax.ShapeDtypeStruct((rows, width), F32),
-        in_specs=[VM] * 7,
-        out_specs=VM,
+        in_specs=[VM] * 5,
+        out_specs=ANY,
+        scratch_shapes=[pltpu.VMEM((rows, width), F32), pltpu.SemaphoreType.DMA((n,))],
         compiler_params=params(),
         cost_estimate=cost(0, 4 * rows * width * 6),
         name="finish",
-    )(own, *got, holes, occupied[None, :], virtual[None, :])
+    )(*map(inside, (total, inverse, *got)))
 
 
 def shards(amplitudes, integrals, hole_integrals, tile_mask, occupied_energy, virtual_energy):
@@ -375,16 +382,16 @@
     def ring(value, d):
         return lax.ppermute(value, "row", [(i, (i + d) % z) for i in range(z)])
 
-    first, second = pack("pack_theirs", tile_mask, integrals, [(*FAR, False), (*REST, False)])
+    first, own_far, second = pack("pack_first", tile_mask, integrals, [(*FAR, False), (*FAR, True), (*REST, False)])
     v1 = lax.ppermute(first, "layer", swap)
     ap = lax.ppermute(a, "layer", swap)
     high, low = [ring(a, 1)], [ring(a, -1)]
     v2 = lax.ppermute(second, "layer", swap)
-    [own_v] = pack("pack_own", tile_mask, integrals, [(*ALL, True)], [first])
-
-    up, down = far(a, ap, own_v, v1)
+    [own_v] = pack("pack_own", tile_mask, integrals, [(*REST, True)], [own_far])
+
+    up, down = far(a, ap, own_far, v1)
     far_up, far_down = send(up, True, 1), send(down, True, -1)
-    here = hand_on([high[0], low[0]], [up])
+    here = hand_on([high[0], low[0]], [up], LONG)
     high.append(ring(here[0], 1))
     low.append(ring(here[1], -1))
     up, down, up_st, down_st = near(a, ap, own_v, v2, here)
@@ -402,8 +409,9 @@
     own, m1, m2, m3 = turn(st, far_up, far_down, here)
     got = send(m2, False, 2), send(m1, False, 1), send(m3, False, -1)
     low[2:] = hand_on(low[2:], [m1, m2, m3])
-    holes = hole_part("holes", hole_integrals, [a, *high, *low], [0, -1, -2, -3, -4, 1, 2, 3], None, [m1, m2, m3])
-    return finish(own, got, holes, occupied_energy, virtual_energy)
+    blocks, away = [a, *high, *low], [0, -1, -2, -3, -4, 1, 2, 3]
+    total, inverse = hole_part(hole_integrals, blocks, away, own, occupied_energy, virtual_energy, [m1, m2, m3])
+    return finish(total, inverse, got)
 
 
 def solution(mesh):

time: 69.9 us -> 68.7 us (0.983)
  Pallas kernels: 25.6 us -> 22.1 us
  waiting for transfers between devices: 17.4 us -> 19.1 us
    pallas_call x11, Pallas kernels: 17.4 us -> 14.2 us  [run(): pl.pallas_call(whole, in_specs=list(in_specs) + [VM] * c + [ANY] * m, out...]
    ppermute x9, waiting for transfers between devices: 15.2 us -> 17.9 us  [send(): return lax.ppermute(value, ('col', 'layer'), hop(first, d))]
    ppermute x7, waiting for transfers between devices: 2.12 us -> 1.16 us  [ring(): return lax.ppermute(value, 'row', [(i, (i + d) % z) for i in range(z)])]
  transfers between devices with their start and end apart: 19 -> 19, of which waited for: 8 -> 8; matrix products, arithmetic and copies ran while one was open for 0% -> 0% of each run, Pallas kernels for 30% -> 25%
where the time goes in v4:
time: 68.7 us; the launch traced here: 68.6 us
  starting transfers between devices  26.9 us (39%)
  Pallas kernels  22.1 us (32%)
  waiting for transfers between devices  19.1 us (28%)
    ppermute x9, waiting for transfers between devices, send(): return lax.ppermute(value, ('col', 'layer'), hop(first, d))  17.9 us
    pallas_call x11, Pallas kernels, run(): pl.pallas_call(whole, in_specs=list(in_specs) + [VM] * c + [ANY] * m, out...  14.2 us
    ppermute x9, starting transfers between devices, send(): return lax.ppermute(value, ('col', 'layer'), hop(first, d))  13.2 us
    ppermute x7, starting transfers between devices, ring(): return lax.ppermute(value, 'row', [(i, (i + d) % z) for i in range(z)])  13 us
    pallas_call x2, Pallas kernels, pack(): pl.pallas_call(body, out_shape=[pltpu.VMEM((n, width, width), BF16) for _...  6.79 us
  transfers between devices with their start and end apart: 19, of which 8 were waited for; matrix products, arithmetic and copies ran while one was open for 0% of the time, Pallas kernels for 25%

profile of v4, /device:TPU:8, one launch (start us, length us, event | category | flops | bytes accessed | tf_op | source)
XLA Modules:
  0.0 68.6 jit_solution(15226431571588534317)
XLA Ops:
  0.0 0.0 copy-start
  0.0 3.9 %pack_first.1 = (bf16[4,384,384]{2,1,0:T(8,128)(2,1)S(1)}, bf16[4,384,384]{2,1,0:T(8,128)(2,1)S(1)}, bf16[12,384,384]{2,1,0:T(8,128)(2,1)S(1)}) custom-call(s32[96,96]{1,0:T(8,128)} %mask_ref.3, bf16[384,12288]{1,0:T(8,128)(2,1)} %v_ref.3), custom_call_target="tpu_custom_call" | custom-call | bytes 11796 | tf_op jit(solution)/shard_map/pack_first/pallas_call | solution.py:157
  3.9 0.1 collective-permute-start.1
  4.0 0.5 collective-permute-start.4
  4.5 0.0 copy-done
  4.5 0.1 collective-permute-start
  4.6 1.9 %collective-permute-start.2 = (bf16[512,384]{1,0:T(8,128)(2,1)S(1)}, bf16[512,384]{1,0:T(8,128)(2,1)S(1)}, u32[]{:S(2)}, u32[]{:S(2)}) collective-permute-start(bf16[512,384]{1,0:T(8,128)(2,1)S(1)} %copy-done), channel_id=1, source_target_pairs={{0,32},{32,64},{64,96},{96,128},{128,160},{160,192},{192,224},{224... | collective-permute-start | bytes 1179656 | tf_op jit(solution)/shard_map/ppermute | solution.py:383
  6.5 3.9 %collective-permute-start.3 = (bf16[512,384]{1,0:T(8,128)(2,1)S(1)}, bf16[512,384]{1,0:T(8,128)(2,1)S(1)}, u32[]{:S(2)}, u32[]{:S(2)}) collective-permute-start(bf16[512,384]{1,0:T(8,128)(2,1)S(1)} %copy-done), channel_id=1, source_target_pairs={{0,224},{32,0},{64,32},{96,64},{128,96},{160,128},{192,160},{224,1... | collective-permute-start | bytes 1179656 | tf_op jit(solution)/shard_map/ppermute | solution.py:383
  10.5 2.9 %pack_own.1.refs_2_ = bf16[12,384,384]{2,1,0:T(8,128)(2,1)S(1)} custom-call(s32[96,96]{1,0:T(8,128)} %mask_ref.3, bf16[384,12288]{1,0:T(8,128)(2,1)} %v_ref.3, bf16[4,384,384]{2,1,0:T(8,128)(2,1)S(1)} %get-tuple-element.24.refs_0_.refs_2_), custom_call_target="tpu_custom_call" | custom-call | bytes 7077 | tf_op jit(solution)/shard_map/pack_own/pallas_call | solution.py:157
  13.4 0.0 collective-permute-done.refs_1_
  13.4 0.0 collective-permute-done.4.refs_3_
  13.4 2.7 %far.1 = (s16[1040,384]{1,0:T(8,128)(2,1)S(1)}, s16[1040,384]{1,0:T(8,128)(2,1)S(1)}) custom-call(bf16[512,384]{1,0:T(8,128)(2,1)S(1)} %copy-done, bf16[512,384]{1,0:T(8,128)(2,1)S(1)} %collective-permute-done.refs_1_, bf16[4,384,384]{2,1,0:T(8,128)(2,1)S(1)} %get-tuple-element.24.refs_0_.refs_2_, bf16[4,384,384]{2,1,0:T(8,128)(2,1)S(1)} %collective-permute-done.4.refs_3_), custom_call_target="tpu_custom_call" | custom-call | flops 1207959 | bytes 2359 | tf_op jit(solution)/shard_map/far/pallas_call | solution.py:53
  16.1 1.6 %collective-permute-start.10 = (s16[1040,384]{1,0:T(8,128)(2,1)S(1)}, s16[1040,384]{1,0:T(8,128)(2,1)S(1)}, u32[]{:S(2)}, u32[]{:S(2)}) collective-permute-start(s16[1040,384]{1,0:T(8,128)(2,1)S(1)} %get-tuple-element.27.refs_2_), channel_id=1, source_target_pairs={{0,2},{1,9},{2,4},{3,11},{4,6},{5,13},{6,0},{7,15},{8,10},{9,17},{... | collective-permute-start | bytes 2396168 | tf_op jit(solution)/shard_map/ppermute | solution.py:38
  17.7 1.7 %collective-permute-start.9 = (s16[1040,384]{1,0:T(8,128)(2,1)S(1)}, s16[1040,384]{1,0:T(8,128)(2,1)S(1)}, u32[]{:S(2)}, u32[]{:S(2)}) collective-permute-start(s16[1040,384]{1,0:T(8,128)(2,1)S(1)} %get-tuple-element.32), channel_id=1, source_target_pairs={{0,6},{1,25},{2,0},{3,27},{4,2},{5,29},{6,4},{7,31},{8,14},{9,1},{... | collective-permute-start | bytes 2396168 | tf_op jit(solution)/shard_map/ppermute | solution.py:38
  19.4 0.7 %collective-permute-done.2.refs_0_.refs_5_ = bf16[512,384]{1,0:T(8,128)(2,1)S(1)} collective-permute-done((bf16[512,384]{1,0:T(8,128)(2,1)S(1)}, bf16[512,384]{1,0:T(8,128)(2,1)S(1)}, u32[]{:S(2)}, u32[]{:S(2)}) %collective-permute-start.2) | collective-permute-done | bytes 393248 | tf_op jit(solution)/shard_map/ppermute | solution.py:383
  20.2 0.0 collective-permute-done.3.refs_1_.refs_9_
  20.2 0.1 hand_on.4
  20.2 0.4 collective-permute-start.7
  20.6 4.0 %collective-permute-start.8 = (bf16[512,384]{1,0:T(8,128)(2,1)S(1)}, bf16[512,384]{1,0:T(8,128)(2,1)S(1)}, u32[]{:S(2)}, u32[]{:S(2)}) collective-permute-start(bf16[512,384]{1,0:T(8,128)(2,1)S(1)} %get-tuple-element.29.refs_5_), channel_id=1, source_target_pairs={{0,224},{32,0},{64,32},{96,64},{128,96},{160,128},{192,160},{224,1... | collective-permute-start | bytes 1179656 | tf_op jit(solution)/shard_map/ppermute | solution.py:383
  24.6 0.0 collective-permute-done.1.refs_3_
  24.6 4.1 %near.1 = (s16[1040,384]{1,0:T(8,128)(2,1)S(1)}, s16[1040,384]{1,0:T(8,128)(2,1)S(1)}, f32[1024,384]{1,0:T(8,128)S(1)}, f32[1024,384]{1,0:T(8,128)S(1)}) custom-call(bf16[512,384]{1,0:T(8,128)(2,1)S(1)} %copy-done, bf16[512,384]{1,0:T(8,128)(2,1)S(1)} %collective-permute-done.refs_1_, bf16[12,384,384]{2,1,0:T(8,128)(2,1)S(1)} %pack_own.1.refs_2_, ...), custom_call_target="tpu_custom_call" | custom-call | flops 20000000000 | tf_op jit(solution)/shard_map/near/pallas_call | solution.py:53
  28.7 1.8 %collective-permute-start.5 = (s16[1040,384]{1,0:T(8,128)(2,1)S(1)}, s16[1040,384]{1,0:T(8,128)(2,1)S(1)}, u32[]{:S(2)}, u32[]{:S(2)}) collective-permute-start(s16[1040,384]{1,0:T(8,128)(2,1)S(1)} %get-tuple-element.30), channel_id=1, source_target_pairs={{0,6},{1,25},{2,0},{3,27},{4,2},{5,29},{6,4},{7,31},{8,14},{9,1},{... | collective-permute-start | bytes 2396168 | tf_op jit(solution)/shard_map/ppermute | solution.py:38
  30.5 0.0 collective-permute-done.10.refs_0_
  30.5 0.3 collective-permute-start.6
  30.8 0.8 %relay.2.refs_2_ = s16[1040,384]{1,0:T(8,128)(2,1)S(1)} custom-call(s16[1040,384]{1,0:T(8,128)(2,1)S(1)} %collective-permute-done.10.refs_0_, f32[1024,384]{1,0:T(8,128)S(1)} %get-tuple-element.34.refs_1_), custom_call_target="tpu_custom_call" | custom-call | bytes 3145 | tf_op jit(solution)/shard_map/relay/pallas_call | solution.py:53
  31.6 0.0 collective-permute-done.9.refs_0_
  31.6 0.6 collective-permute-start.11
  32.2 0.8 %relay.3.refs_2_ = s16[1040,384]{1,0:T(8,128)(2,1)S(1)} custom-call(s16[1040,384]{1,0:T(8,128)(2,1)S(1)} %collective-permute-done.9.refs_0_, f32[1024,384]{1,0:T(8,128)S(1)} %get-tuple-element.33.refs_1_, s16[1040,384]{1,0:T(8,128)(2,1)S(1)} %relay.2.refs_2_), custom_call_target="tpu_custom_call" | custom-call | bytes 3145 | tf_op jit(solution)/shard_map/relay/pallas_call | solution.py:53
  32.9 0.0 collective-permute-done.7.refs_0_.refs_6_
  32.9 2.8 %collective-permute-start.12 = (s16[1040,384]{1,0:T(8,128)(2,1)S(1)}, s16[1040,384]{1,0:T(8,128)(2,1)S(1)}, u32[]{:S(2)}, u32[]{:S(2)}) collective-permute-start(s16[1040,384]{1,0:T(8,128)(2,1)S(1)} %relay.3.refs_2_), channel_id=1, source_target_pairs={{0,6},{1,25},{2,0},{3,27},{4,2},{5,29},{6,4},{7,31},{8,14},{9,1},{... | collective-permute-start | bytes 2396168 | tf_op jit(solution)/shard_map/ppermute | solution.py:38
  35.8 0.0 collective-permute-done.8.refs_1_.refs_10_
  35.8 0.1 hand_on.5
  35.8 0.3 collective-permute-start.13
  36.1 4.8 %collective-permute-done.5.refs_4_ = s16[1040,384]{1,0:T(8,128)(2,1)S(1)} collective-permute-done((s16[1040,384]{1,0:T(8,128)(2,1)S(1)}, s16[1040,384]{1,0:T(8,128)(2,1)S(1)}, u32[]{:S(2)}, u32[]{:S(2)}) %collective-permute-start.5) | collective-permute-done | bytes 798752 | tf_op jit(solution)/shard_map/ppermute | solution.py:38
  40.9 2.4 %collective-permute-start.15 = (bf16[512,384]{1,0:T(8,128)(2,1)S(1)}, bf16[512,384]{1,0:T(8,128)(2,1)S(1)}, u32[]{:S(2)}, u32[]{:S(2)}) collective-permute-start(bf16[512,384]{1,0:T(8,128)(2,1)S(1)} %get-tuple-element.36.refs_7_), channel_id=1, source_target_pairs={{0,224},{32,0},{64,32},{96,64},{128,96},{160,128},{192,160},{224,1... | collective-permute-start | bytes 1179656 | tf_op jit(solution)/shard_map/ppermute | solution.py:383
  43.3 0.5 collective-permute-done.6.refs_5_
  43.8 2.4 %home.1.refs_1_.refs_0_ = f32[4,512,384]{2,1,0:T(8,128)S(1)} custom-call(bf16[512,384]{1,0:T(8,128)(2,1)S(1)} %copy-done, bf16[512,384]{1,0:T(8,128)(2,1)S(1)} %collective-permute-done.refs_1_, bf16[12,384,384]{2,1,0:T(8,128)(2,1)S(1)} %pack_own.1.refs_2_, bf16[12,384,384]{2,1,0:T(8,128)(2,1)S(1)} %collective-permute-done.1.refs_3_, ...), custom_call_target="tpu_custom_call" | custom-call | flops 20000000000 | tf_op jit(solution)/shard_map/home/pallas_call | solution.py:53
  46.2 0.0 copy-start.3
  46.2 0.4 collective-permute-done.13.refs_0_.refs_7_
  46.7 0.1 collective-permute-start.14
  46.8 0.1 copy-done.3
  46.9 0.0 copy-start.1
  46.9 0.0 copy-start.2
  46.9 2.6 %collective-permute-done.12.refs_2_ = s16[1040,384]{1,0:T(8,128)(2,1)S(1)} collective-permute-done((s16[1040,384]{1,0:T(8,128)(2,1)S(1)}, s16[1040,384]{1,0:T(8,128)(2,1)S(1)}, u32[]{:S(2)}, u32[]{:S(2)}) %collective-permute-start.12) | collective-permute-done | bytes 798752 | tf_op jit(solution)/shard_map/ppermute | solution.py:38
  49.5 2.9 %collective-permute-done.11.refs_1_ = s16[1040,384]{1,0:T(8,128)(2,1)S(1)} collective-permute-done((s16[1040,384]{1,0:T(8,128)(2,1)S(1)}, s16[1040,384]{1,0:T(8,128)(2,1)S(1)}, u32[]{:S(2)}, u32[]{:S(2)}) %collective-permute-start.11) | collective-permute-done | bytes 798752 | tf_op jit(solution)/shard_map/ppermute | solution.py:38
  52.4 0.9 %turn.1 = (f32[512,384]{1,0:T(8,128)S(1)}, s16[528,384]{1,0:T(8,128)(2,1)S(1)}, s16[528,384]{1,0:T(8,128)(2,1)S(1)}, s16[528,384]{1,0:T(8,128)(2,1)S(1)}) custom-call(f32[4,512,384]{2,1,0:T(8,128)S(1)} %home.1.refs_1_.refs_0_, s16[1040,384]{1,0:T(8,128)(2,1)S(1)} %collective-permute-done.11.refs_1_, s16[1040,384]{1,0:T(8,128)(2,1)S(1)} %collective-permute-done.12.refs_2_, ...), custom_call_target="tpu_custom_call" | custom-call | bytes 7864 | tf_op jit(solution)/shard_map/turn/pallas_call | solution.py:53
  53.3 2.4 %collective-permute-start.16 = (s16[528,384]{1,0:T(8,128)(2,1)S(1)}, s16[528,384]{1,0:T(8,128)(2,1)S(1)}, u32[]{:S(2)}, u32[]{:S(2)}) collective-permute-start(s16[528,384]{1,0:T(8,128)(2,1)S(1)} %get-tuple-element.39.refs_2_.refs_13_), channel_id=1, source_target_pairs={{0,16},{1,5},{2,18},{3,7},{4,20},{5,1},{6,22},{7,3},{8,24},{9,13},... | collective-permute-start | bytes 1216520 | tf_op jit(solution)/shard_map/ppermute | solution.py:38
  55.7 0.0 collective-permute-start.17
  55.7 2.0 %collective-permute-start.18 = (s16[528,384]{1,0:T(8,128)(2,1)S(1)}, s16[528,384]{1,0:T(8,128)(2,1)S(1)}, u32[]{:S(2)}, u32[]{:S(2)}) collective-permute-start(s16[528,384]{1,0:T(8,128)(2,1)S(1)} %get-tuple-element.40.refs_3_.refs_14_), channel_id=1, source_target_pairs={{0,24},{1,7},{2,26},{3,1},{4,28},{5,3},{6,30},{7,5},{8,0},{9,15},{... | collective-permute-start | bytes 1216520 | tf_op jit(solution)/shard_map/ppermute | solution.py:38
  57.7 0.0 collective-permute-done.15.refs_0_
  57.7 0.0 collective-permute-done.14.refs_8_
  57.8 0.0 copy-done.1
  57.8 0.0 copy-done.2
  57.8 2.3 %holes.1 = (f32[512,384]{1,0:T(8,128)S(1)}, f32[512,384]{1,0:T(8,128)S(1)}) custom-call(bf16[512,4096]{1,0:T(8,128)(2,1)S(1)} %copy-done.1, f32[512,384]{1,0:T(8,128)S(1)} %get-tuple-element.37.refs_1_, f32[1,512]{1,0:T(1,128)S(1)} %bitcast.1, f32[1,384]{1,0:T(1,128)S(1)} %broadcast_in_dim.7.refs_3_, bf16[512,384]{1,0:T(8,128)(2,1)S(1)} %copy-done, ...), custom_call_target="tpu_custom_call" | custom-call | flops 20000000000 | tf_op jit(solution)/shard_map/holes/pallas_call | solution.py:53
  60.1 2.8 %collective-permute-done.16.m1 = s16[528,384]{1,0:T(8,128)(2,1)S(1)} collective-permute-done((s16[528,384]{1,0:T(8,128)(2,1)S(1)}, s16[528,384]{1,0:T(8,128)(2,1)S(1)}, u32[]{:S(2)}, u32[]{:S(2)}) %collective-permute-start.16) | collective-permute-done | bytes 405536 | tf_op jit(solution)/shard_map/ppermute | solution.py:38
  62.9 4.4 %collective-permute-done.17.m2 = s16[528,384]{1,0:T(8,128)(2,1)S(1)} collective-permute-done((s16[528,384]{1,0:T(8,128)(2,1)S(1)}, s16[528,384]{1,0:T(8,128)(2,1)S(1)}, u32[]{:S(2)}, u32[]{:S(2)}) %collective-permute-start.17) | collective-permute-done | bytes 405536 | tf_op jit(solution)/shard_map/ppermute | solution.py:38
  67.3 0.0 collective-permute-done.18.m3
  67.3 1.1 %finish.1 = f32[512,384]{1,0:T(8,128)} custom-call(f32[512,384]{1,0:T(8,128)S(1)} %get-tuple-element.41.sum_ref, f32[512,384]{1,0:T(8,128)S(1)} %get-tuple-element.42.inverse_ref, s16[528,384]{1,0:T(8,128)(2,1)S(1)} %collective-permute-done.16.m1, s16[528,384]{1,0:T(8,128)(2,1)S(1)} %collective-permute-done.17.m2, s16[528,384]{1,0:T(8,128)(2,1)S(1)} %collective-permute-done.18.m3), custom_call_target="tpu_custom_call" | custom-call | bytes 4718 | tf_op jit(solution)/shard_map/finish/pallas_call | solution.py:365
  (3 shorter events, 0.1 us)
Async XLA Ops:
  0.0 4.5 %copy-start = (bf16[512,384]{1,0:T(8,128)(2,1)S(1)}, bf16[512,384]{1,0:T(8,128)(2,1)}, u32[]{:S(2)}) copy-start(bf16[512,384]{1,0:T(8,128)(2,1)} %refs_4_.1) | copy-start | bytes 1179652
  3.9 20.7 %collective-permute-start.1 = (bf16[12,384,384]{2,1,0:T(8,128)(2,1)S(1)}, bf16[12,384,384]{2,1,0:T(8,128)(2,1)S(1)}, u32[]{:S(2)}, u32[]{:S(2)}) collective-permute-start(bf16[12,384,384]{2,1,0:T(8,128)(2,1)S(1)} %get-tuple-element.25), channel_id=1, source_target_pairs={{0,1},{1,0},{2,3},{3,2},{4,5},{5,4},{6,7},{7,6},{8,9},{9,8},{10,11... | collective-permute-start | bytes 10616840 | tf_op jit(solution)/shard_map/ppermute | solution.py:389
  4.0 9.3 %collective-permute-start.4 = (bf16[4,384,384]{2,1,0:T(8,128)(2,1)S(1)}, bf16[4,384,384]{2,1,0:T(8,128)(2,1)S(1)}, u32[]{:S(2)}, u32[]{:S(2)}) collective-permute-start(bf16[4,384,384]{2,1,0:T(8,128)(2,1)S(1)} %get-tuple-element.26), channel_id=1, source_target_pairs={{0,1},{1,0},{2,3},{3,2},{4,5},{5,4},{6,7},{7,6},{8,9},{9,8},{10,11... | collective-permute-start | bytes 3538952 | tf_op jit(solution)/shard_map/ppermute | solution.py:386
  4.5 8.8 %collective-permute-start = (bf16[512,384]{1,0:T(8,128)(2,1)S(1)}, bf16[512,384]{1,0:T(8,128)(2,1)S(1)}, u32[]{:S(2)}, u32[]{:S(2)}) collective-permute-start(bf16[512,384]{1,0:T(8,128)(2,1)S(1)} %copy-done), channel_id=1, source_target_pairs={{0,1},{1,0},{2,3},{3,2},{4,5},{5,4},{6,7},{7,6},{8,9},{9,8},{10,11... | collective-permute-start | bytes 1179656 | tf_op jit(solution)/shard_map/ppermute | solution.py:387
  4.6 15.5 %collective-permute-start.2 = (bf16[512,384]{1,0:T(8,128)(2,1)S(1)}, bf16[512,384]{1,0:T(8,128)(2,1)S(1)}, u32[]{:S(2)}, u32[]{:S(2)}) collective-permute-start(bf16[512,384]{1,0:T(8,128)(2,1)S(1)} %copy-done), channel_id=1, source_target_pairs={{0,32},{32,64},{64,96},{96,128},{128,160},{160,192},{192,224},{224... | collective-permute-start | bytes 1179656 | tf_op jit(solution)/shard_map/ppermute | solution.py:383
  6.5 13.6 %collective-permute-start.3 = (bf16[512,384]{1,0:T(8,128)(2,1)S(1)}, bf16[512,384]{1,0:T(8,128)(2,1)S(1)}, u32[]{:S(2)}, u32[]{:S(2)}) collective-permute-start(bf16[512,384]{1,0:T(8,128)(2,1)S(1)} %copy-done), channel_id=1, source_target_pairs={{0,224},{32,0},{64,32},{96,64},{128,96},{160,128},{192,160},{224,1... | collective-permute-start | bytes 1179656 | tf_op jit(solution)/shard_map/ppermute | solution.py:383
  16.1 14.4 %collective-permute-start.10 = (s16[1040,384]{1,0:T(8,128)(2,1)S(1)}, s16[1040,384]{1,0:T(8,128)(2,1)S(1)}, u32[]{:S(2)}, u32[]{:S(2)}) collective-permute-start(s16[1040,384]{1,0:T(8,128)(2,1)S(1)} %get-tuple-element.27.refs_2_), channel_id=1, source_target_pairs={{0,2},{1,9},{2,4},{3,11},{4,6},{5,13},{6,0},{7,15},{8,10},{9,17},{... | collective-permute-start | bytes 2396168 | tf_op jit(solution)/shard_map/ppermute | solution.py:38
  17.7 13.9 %collective-permute-start.9 = (s16[1040,384]{1,0:T(8,128)(2,1)S(1)}, s16[1040,384]{1,0:T(8,128)(2,1)S(1)}, u32[]{:S(2)}, u32[]{:S(2)}) collective-permute-start(s16[1040,384]{1,0:T(8,128)(2,1)S(1)} %get-tuple-element.32), channel_id=1, source_target_pairs={{0,6},{1,25},{2,0},{3,27},{4,2},{5,29},{6,4},{7,31},{8,14},{9,1},{... | collective-permute-start | bytes 2396168 | tf_op jit(solution)/shard_map/ppermute | solution.py:38
  20.2 12.7 %collective-permute-start.7 = (bf16[512,384]{1,0:T(8,128)(2,1)S(1)}, bf16[512,384]{1,0:T(8,128)(2,1)S(1)}, u32[]{:S(2)}, u32[]{:S(2)}) collective-permute-start(bf16[512,384]{1,0:T(8,128)(2,1)S(1)} %get-tuple-element.28.refs_4_), channel_id=1, source_target_pairs={{0,32},{32,64},{64,96},{96,128},{128,160},{160,192},{192,224},{224... | collective-permute-start | bytes 1179656 | tf_op jit(solution)/shard_map/ppermute | solution.py:383
  20.6 15.2 %collective-permute-start.8 = (bf16[512,384]{1,0:T(8,128)(2,1)S(1)}, bf16[512,384]{1,0:T(8,128)(2,1)S(1)}, u32[]{:S(2)}, u32[]{:S(2)}) collective-permute-start(bf16[512,384]{1,0:T(8,128)(2,1)S(1)} %get-tuple-element.29.refs_5_), channel_id=1, source_target_pairs={{0,224},{32,0},{64,32},{96,64},{128,96},{160,128},{192,160},{224,1... | collective-permute-start | bytes 1179656 | tf_op jit(solution)/shard_map/ppermute | solution.py:383
  28.7 12.2 %collective-permute-start.5 = (s16[1040,384]{1,0:T(8,128)(2,1)S(1)}, s16[1040,384]{1,0:T(8,128)(2,1)S(1)}, u32[]{:S(2)}, u32[]{:S(2)}) collective-permute-start(s16[1040,384]{1,0:T(8,128)(2,1)S(1)} %get-tuple-element.30), channel_id=1, source_target_pairs={{0,6},{1,25},{2,0},{3,27},{4,2},{5,29},{6,4},{7,31},{8,14},{9,1},{... | collective-permute-start | bytes 2396168 | tf_op jit(solution)/shard_map/ppermute | solution.py:38
  30.5 13.3 %collective-permute-start.6 = (s16[1040,384]{1,0:T(8,128)(2,1)S(1)}, s16[1040,384]{1,0:T(8,128)(2,1)S(1)}, u32[]{:S(2)}, u32[]{:S(2)}) collective-permute-start(s16[1040,384]{1,0:T(8,128)(2,1)S(1)} %get-tuple-element.31), channel_id=1, source_target_pairs={{0,2},{1,9},{2,4},{3,11},{4,6},{5,13},{6,0},{7,15},{8,10},{9,17},{... | collective-permute-start | bytes 2396168 | tf_op jit(solution)/shard_map/ppermute | solution.py:38
  31.6 20.8 %collective-permute-start.11 = (s16[1040,384]{1,0:T(8,128)(2,1)S(1)}, s16[1040,384]{1,0:T(8,128)(2,1)S(1)}, u32[]{:S(2)}, u32[]{:S(2)}) collective-permute-start(s16[1040,384]{1,0:T(8,128)(2,1)S(1)} %relay.2.refs_2_), channel_id=1, source_target_pairs={{0,2},{1,9},{2,4},{3,11},{4,6},{5,13},{6,0},{7,15},{8,10},{9,17},{... | collective-permute-start | bytes 2396168 | tf_op jit(solution)/shard_map/ppermute | solution.py:38
  32.9 16.5 %collective-permute-start.12 = (s16[1040,384]{1,0:T(8,128)(2,1)S(1)}, s16[1040,384]{1,0:T(8,128)(2,1)S(1)}, u32[]{:S(2)}, u32[]{:S(2)}) collective-permute-start(s16[1040,384]{1,0:T(8,128)(2,1)S(1)} %relay.3.refs_2_), channel_id=1, source_target_pairs={{0,6},{1,25},{2,0},{3,27},{4,2},{5,29},{6,4},{7,31},{8,14},{9,1},{... | collective-permute-start | bytes 2396168 | tf_op jit(solution)/shard_map/ppermute | solution.py:38
  35.8 10.8 %collective-permute-start.13 = (bf16[512,384]{1,0:T(8,128)(2,1)S(1)}, bf16[512,384]{1,0:T(8,128)(2,1)S(1)}, u32[]{:S(2)}, u32[]{:S(2)}) collective-permute-start(bf16[512,384]{1,0:T(8,128)(2,1)S(1)} %get-tuple-element.35.refs_6_), channel_id=1, source_target_pairs={{0,32},{32,64},{64,96},{96,128},{128,160},{160,192},{192,224},{224... | collective-permute-start | bytes 1179656 | tf_op jit(solution)/shard_map/ppermute | solution.py:383
  40.9 16.8 %collective-permute-start.15 = (bf16[512,384]{1,0:T(8,128)(2,1)S(1)}, bf16[512,384]{1,0:T(8,128)(2,1)S(1)}, u32[]{:S(2)}, u32[]{:S(2)}) collective-permute-start(bf16[512,384]{1,0:T(8,128)(2,1)S(1)} %get-tuple-element.36.refs_7_), channel_id=1, source_target_pairs={{0,224},{32,0},{64,32},{96,64},{128,96},{160,128},{192,160},{224,1... | collective-permute-start | bytes 1179656 | tf_op jit(solution)/shard_map/ppermute | solution.py:383
  46.2 0.7 copy-start.3
  46.7 11.1 %collective-permute-start.14 = (bf16[512,384]{1,0:T(8,128)(2,1)S(1)}, bf16[512,384]{1,0:T(8,128)(2,1)S(1)}, u32[]{:S(2)}, u32[]{:S(2)}) collective-permute-start(bf16[512,384]{1,0:T(8,128)(2,1)S(1)} %hand_on.6.refs_3_), channel_id=1, source_target_pairs={{0,32},{32,64},{64,96},{96,128},{128,160},{160,192},{192,224},{224... | collective-permute-start | bytes 1179656 | tf_op jit(solution)/shard_map/ppermute | solution.py:383
  46.9 10.8 %copy-start.1 = (bf16[512,4096]{1,0:T(8,128)(2,1)S(1)}, bf16[512,4096]{1,0:T(8,128)(2,1)}, u32[]{:S(2)}) copy-start(bf16[512,4096]{1,0:T(8,128)(2,1)} %refs_0_.7) | copy-start | bytes 12582916
  46.9 10.9 %copy-start.2 = (f32[512]{0:T(512)S(1)}, f32[512]{0:T(512)}, u32[]{:S(2)}) copy-start(f32[512]{0:T(512)} %param.10) | copy-start | bytes 6148
  53.3 9.6 %collective-permute-start.16 = (s16[528,384]{1,0:T(8,128)(2,1)S(1)}, s16[528,384]{1,0:T(8,128)(2,1)S(1)}, u32[]{:S(2)}, u32[]{:S(2)}) collective-permute-start(s16[528,384]{1,0:T(8,128)(2,1)S(1)} %get-tuple-element.39.refs_2_.refs_13_), channel_id=1, source_target_pairs={{0,16},{1,5},{2,18},{3,7},{4,20},{5,1},{6,22},{7,3},{8,24},{9,13},... | collective-permute-start | bytes 1216520 | tf_op jit(solution)/shard_map/ppermute | solution.py:38
  55.7 11.6 %collective-permute-start.17 = (s16[528,384]{1,0:T(8,128)(2,1)S(1)}, s16[528,384]{1,0:T(8,128)(2,1)S(1)}, u32[]{:S(2)}, u32[]{:S(2)}) collective-permute-start(s16[528,384]{1,0:T(8,128)(2,1)S(1)} %get-tuple-element.38.refs_1_.refs_12_), channel_id=1, source_target_pairs={{0,8},{1,3},{2,10},{3,5},{4,12},{5,7},{6,14},{7,1},{8,16},{9,11},{... | collective-permute-start | bytes 1216520 | tf_op jit(solution)/shard_map/ppermute | solution.py:38
  55.7 11.6 %collective-permute-start.18 = (s16[528,384]{1,0:T(8,128)(2,1)S(1)}, s16[528,384]{1,0:T(8,128)(2,1)S(1)}, u32[]{:S(2)}, u32[]{:S(2)}) collective-permute-start(s16[528,384]{1,0:T(8,128)(2,1)S(1)} %get-tuple-element.40.refs_3_.refs_14_), channel_id=1, source_target_pairs={{0,24},{1,7},{2,26},{3,1},{4,28},{5,3},{6,30},{7,5},{8,0},{9,15},{... | collective-permute-start | bytes 1216520 | tf_op jit(solution)/shard_map/ppermute | solution.py:38

commit v5 on v4

--- a/solution.py
+++ b/solution.py
@@ -187,7 +187,7 @@
     def body(a_ref, ap_ref, own_ref, v1_ref, up_ref, down_ref):
         lhs = left(a_ref, ap_ref)
 
-        @loop(4)
+        @loop(4, 2)
         def _(o):
             part = product(lhs, own_ref, o, v1_ref, o)
             for b in range(n):
@@ -216,7 +216,7 @@
     def body(a_ref, ap_ref, own_ref, v2_ref, up_ref, down_ref, up_st, down_st):
         lhs = left(a_ref, ap_ref)
 
-        @loop(4)
+        @loop(4, 2)
         def _(o):
             part = product(lhs, own_ref, o, v2_ref, o)
             up_st[rows_at(o, half), :] = part[:half]
@@ -248,7 +248,7 @@
     def body(a_ref, ap_ref, own_ref, v2_ref, up_ref, down_ref, out_ref):
         lhs = left(a_ref, ap_ref)
 
-        @loop(4)
+        @loop(4, 2)
         def _(o):
             part = product(lhs, own_ref, 8 + o, v2_ref, 8 + o)
             for b in range(n):

time: 68.7 us -> 68.3 us (level)
  Pallas kernels: 22.1 us -> 20.9 us
  waiting for transfers between devices: 19.1 us -> 19.9 us
    pallas_call x11, Pallas kernels: 14.2 us -> 13 us  [run(): pl.pallas_call(whole, in_specs=list(in_specs) + [VM] * c + [ANY] * m, out...]
    ppermute x7, waiting for transfers between devices: 1.16 us -> 1.85 us  [ring(): return lax.ppermute(value, 'row', [(i, (i + d) % z) for i in range(z)])]
  transfers between devices with their start and end apart: 19 -> 19, of which waited for: 8 -> 8; matrix products, arithmetic and copies ran while one was open for 0% -> 0% of each run, Pallas kernels for 25% -> 23%
where the time goes in v5:
time: 68.3 us; the launch traced here: 68.2 us
  starting transfers between devices  27.1 us (40%)
  Pallas kernels  20.9 us (31%)
  waiting for transfers between devices  19.9 us (29%)
    ppermute x9, waiting for transfers between devices, send(): return lax.ppermute(value, ('col', 'layer'), hop(first, d))  18 us
    ppermute x9, starting transfers between devices, send(): return lax.ppermute(value, ('col', 'layer'), hop(first, d))  13.6 us
    pallas_call x11, Pallas kernels, run(): pl.pallas_call(whole, in_specs=list(in_specs) + [VM] * c + [ANY] * m, out...  13 us
    ppermute x7, starting transfers between devices, ring(): return lax.ppermute(value, 'row', [(i, (i + d) % z) for i in range(z)])  12.8 us
    pallas_call x2, Pallas kernels, pack(): pl.pallas_call(body, out_shape=[pltpu.VMEM((n, width, width), BF16) for _...  6.79 us
    ppermute x7, waiting for transfers between devices, ring(): return lax.ppermute(value, 'row', [(i, (i + d) % z) for i in range(z)])  1.85 us
  transfers between devices with their start and end apart: 19, of which 8 were waited for; matrix products, arithmetic and copies ran while one was open for 0% of the time, Pallas kernels for 23%

profile of v5, /device:TPU:8, one launch (start us, length us, event | category | flops | bytes accessed | tf_op | source)
XLA Modules:
  0.0 68.2 jit_solution(12111367867111394257)
XLA Ops:
  0.0 0.0 copy-start
  0.0 3.9 %pack_first.1 = (bf16[4,384,384]{2,1,0:T(8,128)(2,1)S(1)}, bf16[4,384,384]{2,1,0:T(8,128)(2,1)S(1)}, bf16[12,384,384]{2,1,0:T(8,128)(2,1)S(1)}) custom-call(s32[96,96]{1,0:T(8,128)} %mask_ref.3, bf16[384,12288]{1,0:T(8,128)(2,1)} %v_ref.3), custom_call_target="tpu_custom_call" | custom-call | bytes 11796 | tf_op jit(solution)/shard_map/pack_first/pallas_call | solution.py:157
  3.9 0.1 collective-permute-start.1
  4.0 0.5 collective-permute-start.4
  4.5 0.0 copy-done
  4.5 0.1 collective-permute-start
  4.6 1.9 %collective-permute-start.2 = (bf16[512,384]{1,0:T(8,128)(2,1)S(1)}, bf16[512,384]{1,0:T(8,128)(2,1)S(1)}, u32[]{:S(2)}, u32[]{:S(2)}) collective-permute-start(bf16[512,384]{1,0:T(8,128)(2,1)S(1)} %copy-done), channel_id=1, source_target_pairs={{0,32},{32,64},{64,96},{96,128},{128,160},{160,192},{192,224},{224... | collective-permute-start | bytes 1179656 | tf_op jit(solution)/shard_map/ppermute | solution.py:383
  6.5 3.9 %collective-permute-start.3 = (bf16[512,384]{1,0:T(8,128)(2,1)S(1)}, bf16[512,384]{1,0:T(8,128)(2,1)S(1)}, u32[]{:S(2)}, u32[]{:S(2)}) collective-permute-start(bf16[512,384]{1,0:T(8,128)(2,1)S(1)} %copy-done), channel_id=1, source_target_pairs={{0,224},{32,0},{64,32},{96,64},{128,96},{160,128},{192,160},{224,1... | collective-permute-start | bytes 1179656 | tf_op jit(solution)/shard_map/ppermute | solution.py:383
  10.5 2.9 %pack_own.1.refs_2_ = bf16[12,384,384]{2,1,0:T(8,128)(2,1)S(1)} custom-call(s32[96,96]{1,0:T(8,128)} %mask_ref.3, bf16[384,12288]{1,0:T(8,128)(2,1)} %v_ref.3, bf16[4,384,384]{2,1,0:T(8,128)(2,1)S(1)} %get-tuple-element.24.refs_0_.refs_2_), custom_call_target="tpu_custom_call" | custom-call | bytes 7077 | tf_op jit(solution)/shard_map/pack_own/pallas_call | solution.py:157
  13.4 0.0 collective-permute-done.refs_1_
  13.4 0.0 collective-permute-done.4.refs_3_
  13.4 2.2 %far.1 = (s16[1040,384]{1,0:T(8,128)(2,1)S(1)}, s16[1040,384]{1,0:T(8,128)(2,1)S(1)}) custom-call(bf16[512,384]{1,0:T(8,128)(2,1)S(1)} %copy-done, bf16[512,384]{1,0:T(8,128)(2,1)S(1)} %collective-permute-done.refs_1_, bf16[4,384,384]{2,1,0:T(8,128)(2,1)S(1)} %get-tuple-element.24.refs_0_.refs_2_, bf16[4,384,384]{2,1,0:T(8,128)(2,1)S(1)} %collective-permute-done.4.refs_3_), custom_call_target="tpu_custom_call" | custom-call | flops 1207959 | bytes 2359 | tf_op jit(solution)/shard_map/far/pallas_call | solution.py:53
  15.6 1.6 %collective-permute-start.10 = (s16[1040,384]{1,0:T(8,128)(2,1)S(1)}, s16[1040,384]{1,0:T(8,128)(2,1)S(1)}, u32[]{:S(2)}, u32[]{:S(2)}) collective-permute-start(s16[1040,384]{1,0:T(8,128)(2,1)S(1)} %get-tuple-element.27.refs_2_), channel_id=1, source_target_pairs={{0,2},{1,9},{2,4},{3,11},{4,6},{5,13},{6,0},{7,15},{8,10},{9,17},{... | collective-permute-start | bytes 2396168 | tf_op jit(solution)/shard_map/ppermute | solution.py:38
  17.2 1.7 %collective-permute-start.9 = (s16[1040,384]{1,0:T(8,128)(2,1)S(1)}, s16[1040,384]{1,0:T(8,128)(2,1)S(1)}, u32[]{:S(2)}, u32[]{:S(2)}) collective-permute-start(s16[1040,384]{1,0:T(8,128)(2,1)S(1)} %get-tuple-element.32), channel_id=1, source_target_pairs={{0,6},{1,25},{2,0},{3,27},{4,2},{5,29},{6,4},{7,31},{8,14},{9,1},{... | collective-permute-start | bytes 2396168 | tf_op jit(solution)/shard_map/ppermute | solution.py:38
  18.9 1.2 %collective-permute-done.2.refs_0_.refs_5_ = bf16[512,384]{1,0:T(8,128)(2,1)S(1)} collective-permute-done((bf16[512,384]{1,0:T(8,128)(2,1)S(1)}, bf16[512,384]{1,0:T(8,128)(2,1)S(1)}, u32[]{:S(2)}, u32[]{:S(2)}) %collective-permute-start.2) | collective-permute-done | bytes 393248 | tf_op jit(solution)/shard_map/ppermute | solution.py:383
  20.2 0.0 collective-permute-done.3.refs_1_.refs_9_
  20.2 0.1 hand_on.4
  20.2 0.1 collective-permute-start.7
  20.3 3.8 %collective-permute-start.8 = (bf16[512,384]{1,0:T(8,128)(2,1)S(1)}, bf16[512,384]{1,0:T(8,128)(2,1)S(1)}, u32[]{:S(2)}, u32[]{:S(2)}) collective-permute-start(bf16[512,384]{1,0:T(8,128)(2,1)S(1)} %get-tuple-element.29.refs_5_), channel_id=1, source_target_pairs={{0,224},{32,0},{64,32},{96,64},{128,96},{160,128},{192,160},{224,1... | collective-permute-start | bytes 1179656 | tf_op jit(solution)/shard_map/ppermute | solution.py:383
  24.1 0.0 collective-permute-done.1.refs_3_
  24.1 3.7 %near.1 = (s16[1040,384]{1,0:T(8,128)(2,1)S(1)}, s16[1040,384]{1,0:T(8,128)(2,1)S(1)}, f32[1024,384]{1,0:T(8,128)S(1)}, f32[1024,384]{1,0:T(8,128)S(1)}) custom-call(bf16[512,384]{1,0:T(8,128)(2,1)S(1)} %copy-done, bf16[512,384]{1,0:T(8,128)(2,1)S(1)} %collective-permute-done.refs_1_, bf16[12,384,384]{2,1,0:T(8,128)(2,1)S(1)} %pack_own.1.refs_2_, ...), custom_call_target="tpu_custom_call" | custom-call | flops 20000000000 | tf_op jit(solution)/shard_map/near/pallas_call | solution.py:53
  27.9 2.3 %collective-permute-start.5 = (s16[1040,384]{1,0:T(8,128)(2,1)S(1)}, s16[1040,384]{1,0:T(8,128)(2,1)S(1)}, u32[]{:S(2)}, u32[]{:S(2)}) collective-permute-start(s16[1040,384]{1,0:T(8,128)(2,1)S(1)} %get-tuple-element.30), channel_id=1, source_target_pairs={{0,6},{1,25},{2,0},{3,27},{4,2},{5,29},{6,4},{7,31},{8,14},{9,1},{... | collective-permute-start | bytes 2396168 | tf_op jit(solution)/shard_map/ppermute | solution.py:38
  30.1 0.0 collective-permute-done.10.refs_0_
  30.1 0.0 collective-permute-start.6
  30.1 0.8 %relay.2.refs_2_ = s16[1040,384]{1,0:T(8,128)(2,1)S(1)} custom-call(s16[1040,384]{1,0:T(8,128)(2,1)S(1)} %collective-permute-done.10.refs_0_, f32[1024,384]{1,0:T(8,128)S(1)} %get-tuple-element.34.refs_1_), custom_call_target="tpu_custom_call" | custom-call | bytes 3145 | tf_op jit(solution)/shard_map/relay/pallas_call | solution.py:53
  30.9 0.0 collective-permute-done.9.refs_0_
  30.9 0.8 %collective-permute-start.11 = (s16[1040,384]{1,0:T(8,128)(2,1)S(1)}, s16[1040,384]{1,0:T(8,128)(2,1)S(1)}, u32[]{:S(2)}, u32[]{:S(2)}) collective-permute-start(s16[1040,384]{1,0:T(8,128)(2,1)S(1)} %relay.2.refs_2_), channel_id=1, source_target_pairs={{0,2},{1,9},{2,4},{3,11},{4,6},{5,13},{6,0},{7,15},{8,10},{9,17},{... | collective-permute-start | bytes 2396168 | tf_op jit(solution)/shard_map/ppermute | solution.py:38
  31.7 0.8 %relay.3.refs_2_ = s16[1040,384]{1,0:T(8,128)(2,1)S(1)} custom-call(s16[1040,384]{1,0:T(8,128)(2,1)S(1)} %collective-permute-done.9.refs_0_, f32[1024,384]{1,0:T(8,128)S(1)} %get-tuple-element.33.refs_1_, s16[1040,384]{1,0:T(8,128)(2,1)S(1)} %relay.2.refs_2_), custom_call_target="tpu_custom_call" | custom-call | bytes 3145 | tf_op jit(solution)/shard_map/relay/pallas_call | solution.py:53
  32.5 0.0 collective-permute-done.7.refs_0_.refs_6_
  32.5 2.8 %collective-permute-start.12 = (s16[1040,384]{1,0:T(8,128)(2,1)S(1)}, s16[1040,384]{1,0:T(8,128)(2,1)S(1)}, u32[]{:S(2)}, u32[]{:S(2)}) collective-permute-start(s16[1040,384]{1,0:T(8,128)(2,1)S(1)} %relay.3.refs_2_), channel_id=1, source_target_pairs={{0,6},{1,25},{2,0},{3,27},{4,2},{5,29},{6,4},{7,31},{8,14},{9,1},{... | collective-permute-start | bytes 2396168 | tf_op jit(solution)/shard_map/ppermute | solution.py:38
  35.3 0.0 collective-permute-done.8.refs_1_.refs_10_
  35.3 0.1 hand_on.5
  35.4 0.2 collective-permute-start.13
  35.6 4.5 %collective-permute-done.5.refs_4_ = s16[1040,384]{1,0:T(8,128)(2,1)S(1)} collective-permute-done((s16[1040,384]{1,0:T(8,128)(2,1)S(1)}, s16[1040,384]{1,0:T(8,128)(2,1)S(1)}, u32[]{:S(2)}, u32[]{:S(2)}) %collective-permute-start.5) | collective-permute-done | bytes 798752 | tf_op jit(solution)/shard_map/ppermute | solution.py:38
  40.1 2.8 %collective-permute-start.15 = (bf16[512,384]{1,0:T(8,128)(2,1)S(1)}, bf16[512,384]{1,0:T(8,128)(2,1)S(1)}, u32[]{:S(2)}, u32[]{:S(2)}) collective-permute-start(bf16[512,384]{1,0:T(8,128)(2,1)S(1)} %get-tuple-element.36.refs_7_), channel_id=1, source_target_pairs={{0,224},{32,0},{64,32},{96,64},{128,96},{160,128},{192,160},{224,1... | collective-permute-start | bytes 1179656 | tf_op jit(solution)/shard_map/ppermute | solution.py:383
  42.8 0.7 collective-permute-done.6.refs_5_
  43.5 2.1 %home.1.refs_1_.refs_0_ = f32[4,512,384]{2,1,0:T(8,128)S(1)} custom-call(bf16[512,384]{1,0:T(8,128)(2,1)S(1)} %copy-done, bf16[512,384]{1,0:T(8,128)(2,1)S(1)} %collective-permute-done.refs_1_, bf16[12,384,384]{2,1,0:T(8,128)(2,1)S(1)} %pack_own.1.refs_2_, bf16[12,384,384]{2,1,0:T(8,128)(2,1)S(1)} %collective-permute-done.1.refs_3_, ...), custom_call_target="tpu_custom_call" | custom-call | flops 20000000000 | tf_op jit(solution)/shard_map/home/pallas_call | solution.py:53
  45.5 0.0 copy-start.3
  45.5 0.6 collective-permute-done.13.refs_0_.refs_7_
  46.2 0.1 collective-permute-start.14
  46.3 0.0 copy-done.3
  46.3 0.0 copy-start.1
  46.3 0.0 copy-start.2
  46.3 2.3 %collective-permute-done.12.refs_2_ = s16[1040,384]{1,0:T(8,128)(2,1)S(1)} collective-permute-done((s16[1040,384]{1,0:T(8,128)(2,1)S(1)}, s16[1040,384]{1,0:T(8,128)(2,1)S(1)}, u32[]{:S(2)}, u32[]{:S(2)}) %collective-permute-start.12) | collective-permute-done | bytes 798752 | tf_op jit(solution)/shard_map/ppermute | solution.py:38
  48.6 3.4 %collective-permute-done.11.refs_1_ = s16[1040,384]{1,0:T(8,128)(2,1)S(1)} collective-permute-done((s16[1040,384]{1,0:T(8,128)(2,1)S(1)}, s16[1040,384]{1,0:T(8,128)(2,1)S(1)}, u32[]{:S(2)}, u32[]{:S(2)}) %collective-permute-start.11) | collective-permute-done | bytes 798752 | tf_op jit(solution)/shard_map/ppermute | solution.py:38
  52.0 0.9 %turn.1 = (f32[512,384]{1,0:T(8,128)S(1)}, s16[528,384]{1,0:T(8,128)(2,1)S(1)}, s16[528,384]{1,0:T(8,128)(2,1)S(1)}, s16[528,384]{1,0:T(8,128)(2,1)S(1)}) custom-call(f32[4,512,384]{2,1,0:T(8,128)S(1)} %home.1.refs_1_.refs_0_, s16[1040,384]{1,0:T(8,128)(2,1)S(1)} %collective-permute-done.11.refs_1_, s16[1040,384]{1,0:T(8,128)(2,1)S(1)} %collective-permute-done.12.refs_2_, ...), custom_call_target="tpu_custom_call" | custom-call | bytes 7864 | tf_op jit(solution)/shard_map/turn/pallas_call | solution.py:53
  52.9 2.4 %collective-permute-start.16 = (s16[528,384]{1,0:T(8,128)(2,1)S(1)}, s16[528,384]{1,0:T(8,128)(2,1)S(1)}, u32[]{:S(2)}, u32[]{:S(2)}) collective-permute-start(s16[528,384]{1,0:T(8,128)(2,1)S(1)} %get-tuple-element.39.refs_2_.refs_13_), channel_id=1, source_target_pairs={{0,16},{1,5},{2,18},{3,7},{4,20},{5,1},{6,22},{7,3},{8,24},{9,13},... | collective-permute-start | bytes 1216520 | tf_op jit(solution)/shard_map/ppermute | solution.py:38
  55.3 0.0 collective-permute-start.17
  55.3 2.0 %collective-permute-start.18 = (s16[528,384]{1,0:T(8,128)(2,1)S(1)}, s16[528,384]{1,0:T(8,128)(2,1)S(1)}, u32[]{:S(2)}, u32[]{:S(2)}) collective-permute-start(s16[528,384]{1,0:T(8,128)(2,1)S(1)} %get-tuple-element.40.refs_3_.refs_14_), channel_id=1, source_target_pairs={{0,24},{1,7},{2,26},{3,1},{4,28},{5,3},{6,30},{7,5},{8,0},{9,15},{... | collective-permute-start | bytes 1216520 | tf_op jit(solution)/shard_map/ppermute | solution.py:38
  57.4 0.0 collective-permute-done.15.refs_0_
  57.4 0.0 collective-permute-done.14.refs_8_
  57.4 0.0 copy-done.1
  57.4 0.0 copy-done.2
  57.4 2.3 %holes.1 = (f32[512,384]{1,0:T(8,128)S(1)}, f32[512,384]{1,0:T(8,128)S(1)}) custom-call(bf16[512,4096]{1,0:T(8,128)(2,1)S(1)} %copy-done.1, f32[512,384]{1,0:T(8,128)S(1)} %get-tuple-element.37.refs_1_, f32[1,512]{1,0:T(1,128)S(1)} %bitcast.1, f32[1,384]{1,0:T(1,128)S(1)} %broadcast_in_dim.7.refs_3_, bf16[512,384]{1,0:T(8,128)(2,1)S(1)} %copy-done, ...), custom_call_target="tpu_custom_call" | custom-call | flops 20000000000 | tf_op jit(solution)/shard_map/holes/pallas_call | solution.py:53
  59.8 2.8 %collective-permute-done.16.m1 = s16[528,384]{1,0:T(8,128)(2,1)S(1)} collective-permute-done((s16[528,384]{1,0:T(8,128)(2,1)S(1)}, s16[528,384]{1,0:T(8,128)(2,1)S(1)}, u32[]{:S(2)}, u32[]{:S(2)}) %collective-permute-start.16) | collective-permute-done | bytes 405536 | tf_op jit(solution)/shard_map/ppermute | solution.py:38
  62.6 4.4 %collective-permute-done.17.m2 = s16[528,384]{1,0:T(8,128)(2,1)S(1)} collective-permute-done((s16[528,384]{1,0:T(8,128)(2,1)S(1)}, s16[528,384]{1,0:T(8,128)(2,1)S(1)}, u32[]{:S(2)}, u32[]{:S(2)}) %collective-permute-start.17) | collective-permute-done | bytes 405536 | tf_op jit(solution)/shard_map/ppermute | solution.py:38
  66.9 0.0 collective-permute-done.18.m3
  67.0 1.1 %finish.1 = f32[512,384]{1,0:T(8,128)} custom-call(f32[512,384]{1,0:T(8,128)S(1)} %get-tuple-element.41.sum_ref, f32[512,384]{1,0:T(8,128)S(1)} %get-tuple-element.42.inverse_ref, s16[528,384]{1,0:T(8,128)(2,1)S(1)} %collective-permute-done.16.m1, s16[528,384]{1,0:T(8,128)(2,1)S(1)} %collective-permute-done.17.m2, s16[528,384]{1,0:T(8,128)(2,1)S(1)} %collective-permute-done.18.m3), custom_call_target="tpu_custom_call" | custom-call | bytes 4718 | tf_op jit(solution)/shard_map/finish/pallas_call | solution.py:365
  (3 shorter events, 0.1 us)
Async XLA Ops:
  0.0 4.5 %copy-start = (bf16[512,384]{1,0:T(8,128)(2,1)S(1)}, bf16[512,384]{1,0:T(8,128)(2,1)}, u32[]{:S(2)}) copy-start(bf16[512,384]{1,0:T(8,128)(2,1)} %refs_4_.1) | copy-start | bytes 1179652
  3.9 20.2 %collective-permute-start.1 = (bf16[12,384,384]{2,1,0:T(8,128)(2,1)S(1)}, bf16[12,384,384]{2,1,0:T(8,128)(2,1)S(1)}, u32[]{:S(2)}, u32[]{:S(2)}) collective-permute-start(bf16[12,384,384]{2,1,0:T(8,128)(2,1)S(1)} %get-tuple-element.25), channel_id=1, source_target_pairs={{0,1},{1,0},{2,3},{3,2},{4,5},{5,4},{6,7},{7,6},{8,9},{9,8},{10,11... | collective-permute-start | bytes 10616840 | tf_op jit(solution)/shard_map/ppermute | solution.py:389
  4.0 9.4 %collective-permute-start.4 = (bf16[4,384,384]{2,1,0:T(8,128)(2,1)S(1)}, bf16[4,384,384]{2,1,0:T(8,128)(2,1)S(1)}, u32[]{:S(2)}, u32[]{:S(2)}) collective-permute-start(bf16[4,384,384]{2,1,0:T(8,128)(2,1)S(1)} %get-tuple-element.26), channel_id=1, source_target_pairs={{0,1},{1,0},{2,3},{3,2},{4,5},{5,4},{6,7},{7,6},{8,9},{9,8},{10,11... | collective-permute-start | bytes 3538952 | tf_op jit(solution)/shard_map/ppermute | solution.py:386
  4.5 8.8 %collective-permute-start = (bf16[512,384]{1,0:T(8,128)(2,1)S(1)}, bf16[512,384]{1,0:T(8,128)(2,1)S(1)}, u32[]{:S(2)}, u32[]{:S(2)}) collective-permute-start(bf16[512,384]{1,0:T(8,128)(2,1)S(1)} %copy-done), channel_id=1, source_target_pairs={{0,1},{1,0},{2,3},{3,2},{4,5},{5,4},{6,7},{7,6},{8,9},{9,8},{10,11... | collective-permute-start | bytes 1179656 | tf_op jit(solution)/shard_map/ppermute | solution.py:387
  4.6 15.5 %collective-permute-start.2 = (bf16[512,384]{1,0:T(8,128)(2,1)S(1)}, bf16[512,384]{1,0:T(8,128)(2,1)S(1)}, u32[]{:S(2)}, u32[]{:S(2)}) collective-permute-start(bf16[512,384]{1,0:T(8,128)(2,1)S(1)} %copy-done), channel_id=1, source_target_pairs={{0,32},{32,64},{64,96},{96,128},{128,160},{160,192},{192,224},{224... | collective-permute-start | bytes 1179656 | tf_op jit(solution)/shard_map/ppermute | solution.py:383
  6.5 13.6 %collective-permute-start.3 = (bf16[512,384]{1,0:T(8,128)(2,1)S(1)}, bf16[512,384]{1,0:T(8,128)(2,1)S(1)}, u32[]{:S(2)}, u32[]{:S(2)}) collective-permute-start(bf16[512,384]{1,0:T(8,128)(2,1)S(1)} %copy-done), channel_id=1, source_target_pairs={{0,224},{32,0},{64,32},{96,64},{128,96},{160,128},{192,160},{224,1... | collective-permute-start | bytes 1179656 | tf_op jit(solution)/shard_map/ppermute | solution.py:383
  15.6 14.5 %collective-permute-start.10 = (s16[1040,384]{1,0:T(8,128)(2,1)S(1)}, s16[1040,384]{1,0:T(8,128)(2,1)S(1)}, u32[]{:S(2)}, u32[]{:S(2)}) collective-permute-start(s16[1040,384]{1,0:T(8,128)(2,1)S(1)} %get-tuple-element.27.refs_2_), channel_id=1, source_target_pairs={{0,2},{1,9},{2,4},{3,11},{4,6},{5,13},{6,0},{7,15},{8,10},{9,17},{... | collective-permute-start | bytes 2396168 | tf_op jit(solution)/shard_map/ppermute | solution.py:38
  17.2 13.7 %collective-permute-start.9 = (s16[1040,384]{1,0:T(8,128)(2,1)S(1)}, s16[1040,384]{1,0:T(8,128)(2,1)S(1)}, u32[]{:S(2)}, u32[]{:S(2)}) collective-permute-start(s16[1040,384]{1,0:T(8,128)(2,1)S(1)} %get-tuple-element.32), channel_id=1, source_target_pairs={{0,6},{1,25},{2,0},{3,27},{4,2},{5,29},{6,4},{7,31},{8,14},{9,1},{... | collective-permute-start | bytes 2396168 | tf_op jit(solution)/shard_map/ppermute | solution.py:38
  20.2 12.3 %collective-permute-start.7 = (bf16[512,384]{1,0:T(8,128)(2,1)S(1)}, bf16[512,384]{1,0:T(8,128)(2,1)S(1)}, u32[]{:S(2)}, u32[]{:S(2)}) collective-permute-start(bf16[512,384]{1,0:T(8,128)(2,1)S(1)} %get-tuple-element.28.refs_4_), channel_id=1, source_target_pairs={{0,32},{32,64},{64,96},{96,128},{128,160},{160,192},{192,224},{224... | collective-permute-start | bytes 1179656 | tf_op jit(solution)/shard_map/ppermute | solution.py:383
  20.3 14.9 %collective-permute-start.8 = (bf16[512,384]{1,0:T(8,128)(2,1)S(1)}, bf16[512,384]{1,0:T(8,128)(2,1)S(1)}, u32[]{:S(2)}, u32[]{:S(2)}) collective-permute-start(bf16[512,384]{1,0:T(8,128)(2,1)S(1)} %get-tuple-element.29.refs_5_), channel_id=1, source_target_pairs={{0,224},{32,0},{64,32},{96,64},{128,96},{160,128},{192,160},{224,1... | collective-permute-start | bytes 1179656 | tf_op jit(solution)/shard_map/ppermute | solution.py:383
  27.9 12.2 %collective-permute-start.5 = (s16[1040,384]{1,0:T(8,128)(2,1)S(1)}, s16[1040,384]{1,0:T(8,128)(2,1)S(1)}, u32[]{:S(2)}, u32[]{:S(2)}) collective-permute-start(s16[1040,384]{1,0:T(8,128)(2,1)S(1)} %get-tuple-element.30), channel_id=1, source_target_pairs={{0,6},{1,25},{2,0},{3,27},{4,2},{5,29},{6,4},{7,31},{8,14},{9,1},{... | collective-permute-start | bytes 2396168 | tf_op jit(solution)/shard_map/ppermute | solution.py:38
  30.1 13.3 %collective-permute-start.6 = (s16[1040,384]{1,0:T(8,128)(2,1)S(1)}, s16[1040,384]{1,0:T(8,128)(2,1)S(1)}, u32[]{:S(2)}, u32[]{:S(2)}) collective-permute-start(s16[1040,384]{1,0:T(8,128)(2,1)S(1)} %get-tuple-element.31), channel_id=1, source_target_pairs={{0,2},{1,9},{2,4},{3,11},{4,6},{5,13},{6,0},{7,15},{8,10},{9,17},{... | collective-permute-start | bytes 2396168 | tf_op jit(solution)/shard_map/ppermute | solution.py:38
  30.9 21.1 %collective-permute-start.11 = (s16[1040,384]{1,0:T(8,128)(2,1)S(1)}, s16[1040,384]{1,0:T(8,128)(2,1)S(1)}, u32[]{:S(2)}, u32[]{:S(2)}) collective-permute-start(s16[1040,384]{1,0:T(8,128)(2,1)S(1)} %relay.2.refs_2_), channel_id=1, source_target_pairs={{0,2},{1,9},{2,4},{3,11},{4,6},{5,13},{6,0},{7,15},{8,10},{9,17},{... | collective-permute-start | bytes 2396168 | tf_op jit(solution)/shard_map/ppermute | solution.py:38
  32.5 16.1 %collective-permute-start.12 = (s16[1040,384]{1,0:T(8,128)(2,1)S(1)}, s16[1040,384]{1,0:T(8,128)(2,1)S(1)}, u32[]{:S(2)}, u32[]{:S(2)}) collective-permute-start(s16[1040,384]{1,0:T(8,128)(2,1)S(1)} %relay.3.refs_2_), channel_id=1, source_target_pairs={{0,6},{1,25},{2,0},{3,27},{4,2},{5,29},{6,4},{7,31},{8,14},{9,1},{... | collective-permute-start | bytes 2396168 | tf_op jit(solution)/shard_map/ppermute | solution.py:38
  35.4 10.8 %collective-permute-start.13 = (bf16[512,384]{1,0:T(8,128)(2,1)S(1)}, bf16[512,384]{1,0:T(8,128)(2,1)S(1)}, u32[]{:S(2)}, u32[]{:S(2)}) collective-permute-start(bf16[512,384]{1,0:T(8,128)(2,1)S(1)} %get-tuple-element.35.refs_6_), channel_id=1, source_target_pairs={{0,32},{32,64},{64,96},{96,128},{128,160},{160,192},{192,224},{224... | collective-permute-start | bytes 1179656 | tf_op jit(solution)/shard_map/ppermute | solution.py:383
  40.1 17.3 %collective-permute-start.15 = (bf16[512,384]{1,0:T(8,128)(2,1)S(1)}, bf16[512,384]{1,0:T(8,128)(2,1)S(1)}, u32[]{:S(2)}, u32[]{:S(2)}) collective-permute-start(bf16[512,384]{1,0:T(8,128)(2,1)S(1)} %get-tuple-element.36.refs_7_), channel_id=1, source_target_pairs={{0,224},{32,0},{64,32},{96,64},{128,96},{160,128},{192,160},{224,1... | collective-permute-start | bytes 1179656 | tf_op jit(solution)/shard_map/ppermute | solution.py:383
  45.5 0.7 %copy-start.3 = (f32[384]{0:T(512)S(1)}, f32[384]{0:T(512)}, u32[]{:S(2)}) copy-start(f32[384]{0:T(512)} %param.11) | copy-start | bytes 4612
  46.2 11.2 %collective-permute-start.14 = (bf16[512,384]{1,0:T(8,128)(2,1)S(1)}, bf16[512,384]{1,0:T(8,128)(2,1)S(1)}, u32[]{:S(2)}, u32[]{:S(2)}) collective-permute-start(bf16[512,384]{1,0:T(8,128)(2,1)S(1)} %hand_on.6.refs_3_), channel_id=1, source_target_pairs={{0,32},{32,64},{64,96},{96,128},{128,160},{160,192},{192,224},{224... | collective-permute-start | bytes 1179656 | tf_op jit(solution)/shard_map/ppermute | solution.py:383
  46.3 11.1 %copy-start.1 = (bf16[512,4096]{1,0:T(8,128)(2,1)S(1)}, bf16[512,4096]{1,0:T(8,128)(2,1)}, u32[]{:S(2)}) copy-start(bf16[512,4096]{1,0:T(8,128)(2,1)} %refs_0_.7) | copy-start | bytes 12582916
  46.3 11.1 %copy-start.2 = (f32[512]{0:T(512)S(1)}, f32[512]{0:T(512)}, u32[]{:S(2)}) copy-start(f32[512]{0:T(512)} %param.10) | copy-start | bytes 6148
  52.9 9.6 %collective-permute-start.16 = (s16[528,384]{1,0:T(8,128)(2,1)S(1)}, s16[528,384]{1,0:T(8,128)(2,1)S(1)}, u32[]{:S(2)}, u32[]{:S(2)}) collective-permute-start(s16[528,384]{1,0:T(8,128)(2,1)S(1)} %get-tuple-element.39.refs_2_.refs_13_), channel_id=1, source_target_pairs={{0,16},{1,5},{2,18},{3,7},{4,20},{5,1},{6,22},{7,3},{8,24},{9,13},... | collective-permute-start | bytes 1216520 | tf_op jit(solution)/shard_map/ppermute | solution.py:38
  55.3 11.6 %collective-permute-start.17 = (s16[528,384]{1,0:T(8,128)(2,1)S(1)}, s16[528,384]{1,0:T(8,128)(2,1)S(1)}, u32[]{:S(2)}, u32[]{:S(2)}) collective-permute-start(s16[528,384]{1,0:T(8,128)(2,1)S(1)} %get-tuple-element.38.refs_1_.refs_12_), channel_id=1, source_target_pairs={{0,8},{1,3},{2,10},{3,5},{4,12},{5,7},{6,14},{7,1},{8,16},{9,11},{... | collective-permute-start | bytes 1216520 | tf_op jit(solution)/shard_map/ppermute | solution.py:38
  55.3 11.6 %collective-permute-start.18 = (s16[528,384]{1,0:T(8,128)(2,1)S(1)}, s16[528,384]{1,0:T(8,128)(2,1)S(1)}, u32[]{:S(2)}, u32[]{:S(2)}) collective-permute-start(s16[528,384]{1,0:T(8,128)(2,1)S(1)} %get-tuple-element.40.refs_3_.refs_14_), channel_id=1, source_target_pairs={{0,24},{1,7},{2,26},{3,1},{4,28},{5,3},{6,30},{7,5},{8,0},{9,15},{... | collective-permute-start | bytes 1216520 | tf_op jit(solution)/shard_map/ppermute | solution.py:38
